TPU v7x, 32 devices: a whole 2x2x4 slice. The times are simulated.
32 devices in a mesh: rep: 4 (over y, x), exp: 8 (over z, core).
Axes of the slice: x: 2, y: 2, z: 4, core: 2. Of those that a mesh axis runs over, the one named last changes fastest.
Arguments:
- cotangent: bfloat16 [4096, 4096], P(('rep', 'exp')), may hold values from -0.59765625 to 0.59765625
- routes: int32 [4096, 1], P(('rep', 'exp')), may hold values from 0 to 7; in each aligned block of 128 rows (0 to 127, 128 to 255, ...) at most 24 rows name the same one
- gate_weight: float32 [4096, 1], P(('rep', 'exp')), may hold values from 0.1 to 1
- down_weight: bfloat16 [8, 4096, 768], P('exp'), may hold values from -0.21875 to 0.21875
- saved_pre: bfloat16 [4, 8, 192, 1536], P('rep', 'exp'), may hold values from -6 to 6
Outputs:
- weight_grad: float32 [8, 4096, 768], P('exp', 'rep')
- input_grads: bfloat16 [4, 8, 192, 1536], P('rep', 'exp')
- token_grad: float32 [4096, 1], P(('rep', 'exp'))
Inputs may be any that keep to these rules, and one draw needn't show every extreme that they name: `routes`: the rows of one device name each expert at most 24 times; in every draw some device names some expert exactly 24 times.
All inputs are finite; a program needn't handle non-finite values.
Results may differ from a plain program's by a relative error of at most 0.019.
Values may be sent and summed in bfloat16 or wider, within the bound.
No kernel may reach another device: no remote copies, remote signals or barrier semaphores. Data moves between devices by JAX's collectives and lax.ppermute only.
A program may use at most 64 MiB of HBM per device.

v0:
```python
import jax
import jax.numpy as jnp
from jax import lax
from jax.sharding import PartitionSpec as P


def shards(cotangent, routes, gate_weight, down_weight, saved_pre):
    peers = lax.axis_size("exp")
    rows_all = saved_pre.shape[2]
    capacity = rows_all // peers
    width = down_weight.shape[2]
    expert_ids = routes[:, 0]
    experts = lax.broadcasted_iota(jnp.int32, (1, peers), 1)
    one_hot = (expert_ids[:, None] == experts).astype(jnp.int32)
    earlier = jnp.cumsum(one_hot, axis=0) - one_hot
    position = jnp.sum(earlier * one_hot, axis=1)
    slot_ids = expert_ids * capacity + position
    slot_index = lax.broadcasted_iota(jnp.int32, (rows_all, 1), 0)
    placement = slot_index == slot_ids[None, :]
    outgoing = jnp.dot(
        placement.astype(jnp.bfloat16), cotangent, preferred_element_type=jnp.float32
    ).astype(jnp.bfloat16)
    send_weight = jnp.sum(jnp.where(placement, gate_weight[:, 0][None, :], 0.0), axis=1).astype(
        jnp.bfloat16
    )
    arrived, arrived_weight = (
        lax.all_to_all(
            outgoing.reshape(peers, capacity, -1), "exp", split_axis=0, concat_axis=0, tiled=True
        ),
        lax.all_to_all(
            send_weight.reshape(peers, capacity), "exp", split_axis=0, concat_axis=0, tiled=True
        ),
    )
    received = arrived.reshape(rows_all, -1)
    scale_col = arrived_weight.reshape(rows_all, 1).astype(jnp.float32)
    pulled = jnp.dot(received, down_weight[0], preferred_element_type=jnp.float32)
    saved_pair = saved_pre[0, 0].astype(jnp.float32)
    gate_pre = saved_pair[:, :width]
    up_pre = saved_pair[:, width:]
    sigmoid_gate = jax.nn.sigmoid(gate_pre)
    silu_gate = gate_pre * sigmoid_gate
    hidden = silu_gate * up_pre
    router = jnp.sum(pulled * hidden, axis=1)
    returned_grad = lax.all_to_all(
        router.reshape(peers, capacity), "exp", split_axis=0, concat_axis=0, tiled=True
    )
    token_grad = jnp.sum(jnp.where(placement, returned_grad.reshape(rows_all, 1), 0.0), axis=0)[
        :, None
    ]
    hidden_grad = scale_col * pulled
    gate_grad = hidden_grad * up_pre * sigmoid_gate * (1.0 + gate_pre * (1.0 - sigmoid_gate))
    up_grad = hidden_grad * silu_gate
    pair_grads = jnp.concatenate([gate_grad, up_grad], axis=1).astype(jnp.bfloat16)
    scaled = (scale_col * hidden).astype(jnp.bfloat16)
    partial_value = lax.dot_general(
        received, scaled, (((0,), (0,)), ((), ())), preferred_element_type=jnp.float32
    )
    grad_share = lax.psum_scatter(
        partial_value.astype(jnp.bfloat16), "rep", scatter_dimension=0, tiled=True
    ).astype(jnp.float32)
    return (grad_share[None], pair_grads.reshape(1, 1, rows_all, 2 * width), token_grad)


def solution(mesh):
    in_specs = (
        P(("rep", "exp"), None),
        P(("rep", "exp"), None),
        P(("rep", "exp"), None),
        P("exp", None, None),
        P("rep", "exp", None, None),
    )
    out_specs = (P("exp", "rep", None), P("rep", "exp", None, None), P(("rep", "exp"), None))
    return jax.shard_map(shards, mesh=mesh, in_specs=in_specs, out_specs=out_specs, check_vma=False)
```

profile of v0, /device:TPU:0, one launch (start us, length us, event | category | flops | bytes accessed | tf_op | source)
XLA Modules:
  0.0 163.3 jit_solution(14510898774154002390)
XLA Ops:
  7.2 0.0 copy-start
  7.2 0.8 fusion.6
  8.0 0.2 reduce_window_sum.11
  8.2 0.8 select_reduce_fusion.2
  9.0 0.7 multiply_add_fusion
  9.7 0.0 copy-done
  9.7 1.7 %convolution_convert_fusion.1 = bf16[192,4096]{1,0:T(8,128)(2,1)} fusion(bf16[128,4096]{1,0:T(8,128)(2,1)S(1)} %copy-done, s32[128]{0:T(128)S(1)} %multiply_add_fusion), kind=kOutput, calls=%fused_computation.3 | convolution fusion | flops 202137600 | bytes 2621952 | tf_op jit(solution)/shard_map/dot_general | solution.py:20
  11.4 0.0 copy-start.1
  11.4 6.5 %all-to-all-start = ((bf16[8,24,4096]{2,1,0:T(8,128)(2,1)}), bf16[8,24,4096]{2,1,0:T(8,128)(2,1)}, u32[]{:S(2)}, u32[]{:S(2)}) async-start(bf16[8,24,4096]{2,1,0:T(8,128)(2,1)} %bitcast.1), calls=%async_computation | async-start | bytes 3145728 | tf_op jit(solution)/shard_map/all_to_all | solution.py:27
  17.8 0.0 reduce-scatter.2.cloned.1.call-start
  17.9 0.0 copy-done.1
  17.9 0.1 bitcast_convert_fusion.1
  18.0 37.8 %all-to-all-done = bf16[8,24,4096]{2,1,0:T(8,128)(2,1)} async-done(((bf16[8,24,4096]{2,1,0:T(8,128)(2,1)}), bf16[8,24,4096]{2,1,0:T(8,128)(2,1)}, u32[]{:S(2)}, u32[]{:S(2)}) %all-to-all-start) | async-done | bytes 1572896 | tf_op jit(solution)/shard_map/all_to_all | solution.py:27
  55.8 0.0 copy-start.2
  55.8 4.8 %multiply_reduce_fusion = (f32[192]{0:T(256)S(1)}, f32[192,768]{1,0:T(8,128)S(1)}) fusion(f32[192,1536]{1,0:T(8,128)S(1)} %bitcast_convert_fusion.1, bf16[192,4096]{1,0:T(8,128)(2,1)} %bitcast.2, bf16[1,4096,768]{2,1,0:T(8,128)(2,1)} %param.8), kind=kOutput, calls=%fused_computation.7 | convolution fusion | flops 1208991488 | bytes 9634560 | tf_op jit(solution)/shard_map/dot_general | solution.py:36
  60.6 0.1 all_to_all.15
  60.7 7.9 %all_to_all.20 = f32[8,1,24]{2,1,0:T(1,128)S(1)} all-to-all(f32[8,1,24]{2,1,0:T(1,128)S(1)} %all_to_all.15), channel_id=1, replica_groups=mesh['rep'=4,'exp'=8] {'exp'}, dimensions={0} | all-to-all | bytes 1536 | tf_op jit(solution)/shard_map/all_to_all | solution.py:44
  68.6 0.5 broadcast.30
  69.1 0.7 reduce.7
  69.7 0.1 broadcast_in_dim.41
  69.8 0.0 copy-done.2
  69.8 0.6 select_reduce_fusion
  70.5 0.1 convert_element_type.65
  70.5 7.9 %all_to_all.21 = bf16[8,1,24]{2,1,0:T(2,128)(2,1)S(1)} all-to-all(bf16[8,1,24]{2,1,0:T(2,128)(2,1)S(1)} %convert_element_type.65), channel_id=1, replica_groups=mesh['rep'=4,'exp'=8] {'exp'}, dimensions={0} | all-to-all | bytes 768 | tf_op jit(solution)/shard_map/all_to_all | solution.py:30
  78.5 0.1 reshape.90
  78.6 6.0 %convolution_convert_fusion = bf16[4096,768]{1,0:T(8,128)(2,1)} fusion(bf16[192,4096]{1,0:T(8,128)(2,1)} %bitcast.2, f32[192]{0:T(256)S(1)} %reshape.90, f32[192,1536]{1,0:T(8,128)S(1)} %bitcast_convert_fusion.1), kind=kOutput, calls=%fused_computation | convolution fusion | flops 1212137472 | bytes 9044736 | tf_op jit(solution)/shard_map/dot_general | solution.py:55
  84.6 0.0 reduce-scatter.2.cloned.1.call-update
  84.6 0.3 fusion.5
  84.9 0.9 pad_maximum_fusion
  85.8 67.4 %reduce-scatter.2.cloned.1.call-done = bf16[1024,768]{1,0:T(8,128)(2,1)} async-done(((bf16[4096,768]{1,0:T(8,128)(2,1)}), bf16[1024,768]{1,0:T(8,128)(2,1)}) %reduce-scatter.2.cloned.1.call-update) | async-done | bytes 1572880 | tf_op jit(solution)/shard_map/reduce_scatter | solution.py:58
  153.2 3.3 %bitcast_convert_fusion = f32[1,1024,768]{2,1,0:T(8,128)} fusion(bf16[1024,768]{1,0:T(8,128)(2,1)} %reduce-scatter.2.cloned.1.call-done), kind=kLoop, calls=%fused_computation.4 | loop fusion | flops 786432 | bytes 4718592 | tf_op jit(solution)/shard_map/broadcast_in_dim | solution.py:61
  (1 shorter events, 0.0 us)
Async XLA Ops:
  7.2 2.5 %copy-start = (bf16[128,4096]{1,0:T(8,128)(2,1)S(1)}, bf16[128,4096]{1,0:T(8,128)(2,1)}, u32[]{:S(2)}) copy-start(bf16[128,4096]{1,0:T(8,128)(2,1)} %param.5) | copy-start | bytes 3145732
  11.4 6.5 %copy-start.1 = (bf16[1,1,192,1536]{3,2,1,0:T(8,128)(2,1)S(1)}, bf16[1,1,192,1536]{3,2,1,0:T(8,128)(2,1)}, u32[]{:S(2)}) copy-start(bf16[1,1,192,1536]{3,2,1,0:T(8,128)(2,1)} %param.9) | copy-start | bytes 1769476
  11.4 44.4 %all-to-all-start = ((bf16[8,24,4096]{2,1,0:T(8,128)(2,1)}), bf16[8,24,4096]{2,1,0:T(8,128)(2,1)}, u32[]{:S(2)}, u32[]{:S(2)}) async-start(bf16[8,24,4096]{2,1,0:T(8,128)(2,1)} %bitcast.1), calls=%async_computation | async-start | bytes 3145728 | tf_op jit(solution)/shard_map/all_to_all | solution.py:27
  17.8 135.3 %reduce-scatter.2.cloned.1.call-start = ((), (), s32[]{:S(2)}) async-start(), calls=%async_computation.4 | async-start | bytes 7864320 | tf_op jit(solution)/shard_map/reduce_scatter | solution.py:58
  55.8 14.0 %copy-start.2 = (f32[128,1]{0,1:T(1,128)S(1)}, f32[128,1]{0,1:T(1,128)}, u32[]{:S(2)}) copy-start(f32[128,1]{0,1:T(1,128)} %param.7) | copy-start | bytes 1540
Sparse Core Ops, SparseCore 0:
  84.7 68.4 reduce-scatter.1
where the time goes:
time: 164 us; the launch traced here: 163 us
  waiting for transfers between devices  105 us (64%)
  blocking collectives  15.8 us (10%)
  between operations  14.1 us (9%)
  matrix products  12.5 us (8%)
  other arithmetic  8.39 us (5%)
  starting transfers between devices  6.49 us (4%)
    reduce_scatter x1, waiting for transfers between devices, shards(): lax.psum_scatter(partial_value.astype(jnp.bfloat16), 'rep', scatter_dimen...  67.4 us
    all_to_all x1, waiting for transfers between devices, shards(): lax.all_to_all(outgoing.reshape(peers, capacity, -1), 'exp', split_axis=0...  37.8 us
    all_to_all x1, blocking collectives, shards(): lax.all_to_all(router.reshape(peers, capacity), 'exp', split_axis=0, conc...  7.92 us
    all_to_all x1, blocking collectives, shards(): lax.all_to_all(send_weight.reshape(peers, capacity), 'exp', split_axis=0,...  7.91 us
    all_to_all x1, starting transfers between devices, shards(): lax.all_to_all(outgoing.reshape(peers, capacity, -1), 'exp', split_axis=0...  6.46 us
    dot_general x1, matrix products, shards(): lax.dot_general(received, scaled, (((0,), (0,)), ((), ())), preferred_ele...  6 us
    dot_general x1, matrix products, shards(): jnp.dot(received, down_weight[0], preferred_element_type=jnp.float32)  4.77 us
    broadcast_in_dim x1, other arithmetic, shards(): grad_share[None]  3.3 us
  transfers between devices with their start and end apart: 2, of which 2 were waited for; matrix products, arithmetic and copies ran while one was open for 1% of the time, Pallas kernels for 0%

commit v1 on v0

v1 whole, which is shorter than its diff:
```python
import jax
import jax.numpy as jnp
from jax import lax
from jax.experimental import pallas as pl
from jax.experimental.pallas import tpu as pltpu
from jax.sharding import PartitionSpec as P

WHOLE_VMEM = pl.BlockSpec(memory_space=pltpu.VMEM)
SMALL = pl.CostEstimate(flops=1024, bytes_accessed=1024, transcendentals=0)
LARGE = pl.CostEstimate(flops=10**10, bytes_accessed=1024, transcendentals=0)


def swap(value, axis, step):
    n = lax.axis_size(axis)
    return lax.ppermute(value, axis, [(i, i ^ step) for i in range(n)])


def kernel_call(kernel, outs, operands, name, cost=SMALL, vmem=24, **more):
    more.setdefault("in_specs", [WHOLE_VMEM] * len(operands))
    more.setdefault("out_specs", [WHOLE_VMEM] * len(outs))
    return pl.pallas_call(
        kernel,
        out_shape=outs,
        compiler_params=pltpu.CompilerParams(vmem_limit_bytes=vmem * 1024 * 1024),
        cost_estimate=cost,
        name=name,
        **more,
    )(*operands)


def prepare_kernel(saved, hidden):
    width = hidden.shape[2]
    for k in range(saved.shape[0]):
        gate = saved[k, :, :width].astype(jnp.float32)
        up = saved[k, :, width:].astype(jnp.float32)
        hidden[k] = (gate / (1.0 + jnp.exp(-gate)) * up).astype(jnp.bfloat16)


def place_kernel(cap, order, cot, cot_sib, routes, routes_sib, weights, weights_sib, *outs):
    chips = len(order)
    blocks, slots_out, last_out = outs[:chips], outs[chips], outs[chips + 1]
    me, mine = lax.axis_index("exp"), lax.axis_index("rep")
    chip, core = me // 2, lax.rem(me, 2)
    replicas, pair, share = blocks[0].shape
    tokens = cot.shape[0]
    before = (
        lax.broadcasted_iota(jnp.int32, (tokens, tokens), 0)
        < lax.broadcasted_iota(jnp.int32, (tokens, tokens), 1)
    ).astype(jnp.bfloat16)
    placements = []
    for i, (ids, gains) in enumerate(((routes, weights), (routes_sib, weights_sib))):
        expert = ids[...]
        weight = gains[...].astype(jnp.bfloat16).astype(jnp.float32)
        hot = lax.broadcasted_iota(jnp.int32, (2 * chips, tokens), 0) == expert
        earlier = jnp.dot(hot.astype(jnp.bfloat16), before, preferred_element_type=jnp.float32)
        position = jnp.sum(jnp.where(hot, earlier, 0.0), axis=0, keepdims=True).astype(jnp.int32)
        source = core if i == 0 else 1 - core
        step = (expert >> 1) ^ chip
        same = (expert & 1) == core
        rank = sum(jnp.where(step == k, i, 0) for i, k in enumerate(order))
        slot = jnp.where(same, rank * pair + source * cap + position, -1)
        slots_out[i : i + 1, :] = slot
        if i == 0:
            last_out[...] = jnp.where(
                step == order[-1], jnp.where(same, position, cap + position), -1
            )
        here = lax.broadcasted_iota(jnp.int32, (chips * pair, tokens), 0) == slot
        placements.append(jnp.where(here, weight, 0.0).astype(jnp.bfloat16))
    placement = jnp.concatenate(placements, axis=1)
    for j in range(replicas):
        columns = pl.ds(pl.multiple_of((mine ^ j) * share, share), share)
        rows = jnp.concatenate([cot[:, columns], cot_sib[:, columns]], axis=0)
        sent = jnp.dot(placement, rows, preferred_element_type=jnp.float32).astype(jnp.bfloat16)
        for k in range(chips):
            blocks[k][j] = sent[k * pair : (k + 1) * pair]


def products(arrived, down):
    mine = lax.axis_index("rep")
    replicas, _, share = arrived[0].shape
    pulled = 0
    for j in range(replicas):
        rows = jnp.concatenate([ref[j] for ref in arrived], axis=0)
        begin = pl.multiple_of((mine ^ j) * share, share)
        pulled += jnp.dot(rows, down[0, pl.ds(begin, share), :], preferred_element_type=jnp.float32)
    return pulled


def gate_parts(saved):
    width = saved.shape[1] // 2
    gate, up = saved[:, :width].astype(jnp.float32), saved[:, width:].astype(jnp.float32)
    sigmoid = 1.0 / (1.0 + jnp.exp(-gate))
    return gate, up, sigmoid


def router_sums(pulled, saved):
    gate, up, sigmoid = gate_parts(saved)
    return lax.dot_general(
        jnp.ones((8, pulled.shape[1]), jnp.float32),
        pulled * (gate * sigmoid * up),
        (((1,), (1,)), ((), ())),
        precision=lax.Precision.HIGHEST,
        preferred_element_type=jnp.float32,
    )[0:1]


def pair_grads(pulled, saved):
    gate, up, sigmoid = gate_parts(saved)
    both = [pulled * up * sigmoid * (1.0 + gate * (1.0 - sigmoid)), pulled * (gate * sigmoid)]
    return jnp.concatenate(both, axis=1).astype(jnp.bfloat16)


def pull_early_kernel(steps, *refs):
    count = len(steps)
    arrived, (down, saved, grads), routers = refs[:count], refs[count : count + 3], refs[count + 3 :]
    chip = lax.axis_index("exp") // 2
    pulled = products(arrived, down)
    pair = arrived[0].shape[1]
    for i, k in enumerate(steps):
        part = pulled[i * pair : (i + 1) * pair]
        routers[i][...] = router_sums(part, saved[chip ^ k])
        grads[chip ^ k] = pair_grads(part, saved[chip ^ k])


def pull_last_kernel(step, arrived, down, saved, pulled, same, other):
    me = lax.axis_index("exp")
    chip, core = me // 2, lax.rem(me, 2)
    pulled[...] = products([arrived], down)
    router = router_sums(pulled[...], saved[chip ^ step])
    cap = router.shape[1] // 2
    same[...] = jnp.where(core == 0, router[:, :cap], router[:, cap:])
    other[...] = jnp.where(core == 0, router[:, cap:], router[:, :cap])


def grads_last_kernel(step, pulled, saved, early, grads):
    chip = lax.axis_index("exp") // 2
    grads[...] = early[...]
    grads[chip ^ step] = pair_grads(pulled[...], saved[chip ^ step])


def stack_kernel(count, *refs):
    for j, out in enumerate(refs[count:]):
        out[...] = jnp.concatenate([ref[j] for ref in refs[:count]], axis=0)


def stack(rows):
    replicas, pair, share = rows[0].shape
    return kernel_call(
        lambda *refs: stack_kernel(len(rows), *refs),
        [jax.ShapeDtypeStruct((len(rows) * pair, share), jnp.bfloat16)] * replicas,
        rows,
        "stack",
    )


def units_of(hidden, steps):
    chip = lax.axis_index("exp") // 2
    return jnp.concatenate([ref[chip ^ k] for ref in hidden for k in steps], axis=0)


def weight_early_kernel(steps, replicas, *refs):
    rows, hidden, out = refs[:replicas], refs[replicas : 2 * replicas], refs[-1]
    out[...] = lax.dot_general(
        jnp.concatenate([ref[...] for ref in rows], axis=0),
        units_of(hidden, steps),
        (((0,), (0,)), ((), ())),
        preferred_element_type=jnp.float32,
    )


def weight_last_kernel(steps, replicas, parts, *refs):
    rows, hidden = refs[:replicas], refs[replicas : 2 * replicas]
    early, out, held, sems = refs[2 * replicas :]
    units = units_of(hidden, steps)
    size = early.shape[0] // parts
    copies = []
    for i in range(parts):
        span = pl.ds(i * size, size)
        left = jnp.concatenate([ref[:, i * size : (i + 1) * size] for ref in rows], axis=0)
        held[span, :] = early[span, :] + lax.dot_general(
            left, units, (((0,), (0,)), ((), ())), preferred_element_type=jnp.float32
        )
        copy = pltpu.make_async_copy(held.at[span, :], out.at[0, span, :], sems.at[i])
        copy.start()
        copies.append(copy)
    for copy in copies:
        copy.wait()


def shards(cotangent, routes, gate_weight, down_weight, saved_pre):
    peers = lax.axis_size("exp")
    replicas = lax.axis_size("rep")
    rows_all = saved_pre.shape[2]
    cap = rows_all // peers
    chips = peers // 2
    pair = 2 * cap
    if pair % 16:
        return plain_shards(cotangent, routes, gate_weight, down_weight, saved_pre)
    width = down_weight.shape[2]
    tokens, model = cotangent.shape
    share = model // replicas

    last = chips // 2
    early = [k for k in range(chips) if k != last]
    order = early + [last]

    routes = routes.reshape(1, tokens)
    weights = gate_weight.reshape(1, tokens)
    cot_sib = swap(cotangent, "exp", 1)
    routes_sib = swap(routes, "exp", 1)
    weights_sib = swap(weights, "exp", 1)
    saved = saved_pre.reshape(chips, pair, 2 * width)
    hidden = kernel_call(
        prepare_kernel,
        [jax.ShapeDtypeStruct((chips, pair, width), jnp.bfloat16)],
        [saved],
        "prepare",
        LARGE,
    )[0]
    hidden, cot_sib = lax.optimization_barrier((hidden, cot_sib))
    *blocks, slots, last_slots = kernel_call(
        lambda *refs: place_kernel(cap, order, *refs),
        [jax.ShapeDtypeStruct((replicas, pair, share), jnp.bfloat16)] * chips
        + [
            jax.ShapeDtypeStruct((2, tokens), jnp.int32),
            jax.ShapeDtypeStruct((1, tokens), jnp.int32),
        ],
        [cotangent, cot_sib, routes, routes_sib, weights, weights_sib],
        "place",
    )

    blocks = dict(zip(order, blocks))
    arrived = {0: blocks[0]}
    for k in reversed(early[1:]):
        arrived[k] = swap(blocks[k], "exp", 2 * k)
    hidden_of = [hidden] + [swap(hidden, "rep", j) for j in range(1, replicas)]

    rows, last_block, hidden_of = lax.optimization_barrier(
        ([arrived[k] for k in early], blocks[last], hidden_of)
    )
    arrived = dict(zip(early, rows))
    arrived[last] = swap(last_block, "exp", 2 * last)
    early_rows = stack(rows)
    early_rows = [early_rows[0]] + [swap(early_rows[j], "rep", j) for j in range(1, replicas)]
    grads, *routers = kernel_call(
        lambda *refs: pull_early_kernel(early, *refs),
        [jax.ShapeDtypeStruct(saved.shape, jnp.bfloat16)]
        + [jax.ShapeDtypeStruct((1, pair), jnp.float32)] * len(early),
        [*[arrived[k] for k in early], down_weight, saved],
        "pull_early",
    )
    returned = routers[:1] + [swap(router, "exp", 2 * k) for router, k in zip(routers[1:], early[1:])]
    total = kernel_call(
        lambda *refs: weight_early_kernel(early, replicas, *refs),
        [jax.ShapeDtypeStruct((share, width), jnp.float32)],
        [*early_rows, *hidden_of],
        "weight_early",
    )[0]

    arrived[last], grads, total, returned = lax.optimization_barrier(
        (arrived[last], grads, total, returned)
    )
    rows = arrived[last]
    late_rows = [rows[0]] + [swap(rows[j], "rep", j) for j in range(1, replicas)]
    pulled, *routers = kernel_call(
        lambda *refs: pull_last_kernel(last, *refs),
        [jax.ShapeDtypeStruct((pair, width), jnp.float32)]
        + [jax.ShapeDtypeStruct((1, cap), jnp.float32)] * 2,
        [arrived[last], down_weight, saved],
        "pull_last",
    )
    returned = jnp.concatenate(returned, axis=1).reshape(len(early) * pair, 1)
    slot_index = lax.broadcasted_iota(jnp.int32, (len(early) * pair, 1), 0)
    sums = [
        jnp.sum(jnp.where(slot_index == slots[i][None, :], returned, 0.0), axis=0)
        for i in range(2)
    ]
    sum_sib = swap(sums[1], "exp", 1)
    routers, sum_sib = lax.optimization_barrier((routers, sum_sib))
    returned_last = [swap(routers[i], "exp", 2 * last + i) for i in range(2)]
    weight_grad = kernel_call(
        lambda *refs: weight_last_kernel([last], replicas, 4, *refs),
        jax.ShapeDtypeStruct((1, share, width), jnp.float32),
        [*late_rows, *hidden_of, total],
        "weight_last",
        LARGE,
        out_specs=pl.BlockSpec(memory_space=pl.ANY),
        scratch_shapes=[pltpu.VMEM((share, width), jnp.float32), pltpu.SemaphoreType.DMA((4,))],
    )
    weight_grad, pulled = lax.optimization_barrier((weight_grad, pulled))
    grads = kernel_call(
        lambda *refs: grads_last_kernel(last, *refs),
        [jax.ShapeDtypeStruct(saved.shape, jnp.bfloat16)],
        [pulled, saved, grads],
        "grads_last",
    )[0]
    returned_last, grads = lax.optimization_barrier((returned_last, grads))
    returned = jnp.concatenate(returned_last, axis=1).reshape(pair, 1)
    slot_index = lax.broadcasted_iota(jnp.int32, (pair, 1), 0)
    last_sum = jnp.sum(jnp.where(slot_index == last_slots, returned, 0.0), axis=0)
    token_grad = (sums[0] + sum_sib + last_sum) / weights[0].astype(jnp.bfloat16).astype(jnp.float32)
    return (weight_grad, grads.reshape(1, 1, rows_all, 2 * width), token_grad[:, None])


def plain_shards(cotangent, routes, gate_weight, down_weight, saved_pre):
    peers = lax.axis_size("exp")
    replicas = lax.axis_size("rep")
    me = lax.axis_index("exp")
    mine = lax.axis_index("rep")
    rows_all = saved_pre.shape[2]
    capacity = rows_all // peers
    width = down_weight.shape[2]
    model = cotangent.shape[1]
    share = model // replicas

    expert_ids = routes[:, 0]
    experts = lax.broadcasted_iota(jnp.int32, (1, peers), 1)
    one_hot = (expert_ids[:, None] == experts).astype(jnp.int32)
    earlier = jnp.cumsum(one_hot, axis=0) - one_hot
    position = jnp.sum(earlier * one_hot, axis=1)
    slot_ids = (expert_ids ^ me) * capacity + position
    slot_index = lax.broadcasted_iota(jnp.int32, (rows_all, 1), 0)
    placement = slot_index == slot_ids[None, :]
    weight = gate_weight[:, 0].astype(jnp.bfloat16)
    outgoing = jnp.dot(
        jnp.where(placement, weight[None, :], 0), cotangent, preferred_element_type=jnp.float32
    ).astype(jnp.bfloat16)
    outgoing = outgoing.reshape(peers, capacity, model)

    groups = [
        list(range(0, peers // 2)),
        list(range(peers // 2, peers // 4 * 3)),
        list(range(peers // 4 * 3, peers)),
    ]
    arrived = {0: outgoing[0]}
    for k in groups[1] + groups[2] + groups[0][1:]:
        arrived[k] = swap(outgoing[k], "exp", k)

    saved = saved_pre[0, 0].reshape(peers, capacity, 2 * width)
    saved = jnp.take(saved, jnp.arange(peers) ^ me, axis=0).reshape(rows_all, 2 * width)
    saved = saved.astype(jnp.float32)
    gate_pre = saved[:, :width]
    up_pre = saved[:, width:]
    sigmoid_gate = jax.nn.sigmoid(gate_pre)
    silu_gate = gate_pre * sigmoid_gate
    hidden = silu_gate * up_pre
    hidden_sent = hidden.astype(jnp.bfloat16)
    hidden_of = [hidden_sent] + [swap(hidden_sent, "rep", j) for j in range(1, replicas)]
    gate_factor = up_pre * sigmoid_gate * (1.0 + gate_pre * (1.0 - sigmoid_gate))

    total = 0
    pulled_parts = []
    returned = []
    for group in groups:
        begin, end = group[0] * capacity, (group[-1] + 1) * capacity
        rows = jnp.concatenate([arrived[k] for k in group], axis=0)
        columns = [
            lax.dynamic_slice_in_dim(rows, (mine ^ j) * share, share, 1) for j in range(replicas)
        ]
        left = [columns[0]] + [swap(columns[j], "rep", j) for j in range(1, replicas)]
        right = [hidden_of[j][begin:end] for j in range(replicas)]
        total = total + lax.dot_general(
            jnp.concatenate(left, axis=0),
            jnp.concatenate(right, axis=0),
            (((0,), (0,)), ((), ())),
            preferred_element_type=jnp.float32,
        )
        pulled = jnp.dot(rows, down_weight[0], preferred_element_type=jnp.float32)
        pulled_parts.append(pulled)
        router = jnp.sum(pulled * hidden[begin:end], axis=1).reshape(len(group), capacity)
        returned += [router[i] if k == 0 else swap(router[i], "exp", k) for i, k in enumerate(group)]
    pulled = jnp.concatenate(pulled_parts, axis=0)
    pair_grads = jnp.concatenate([pulled * gate_factor, pulled * silu_gate], axis=1).astype(
        jnp.bfloat16
    )
    pair_grads = pair_grads.reshape(peers, capacity, 2 * width)
    pair_grads = jnp.take(pair_grads, jnp.arange(peers) ^ me, axis=0)
    returned_grad = jnp.concatenate(returned, axis=0)
    token_grad = jnp.sum(jnp.where(placement, returned_grad[:, None], 0.0), axis=0)
    token_grad = token_grad / weight.astype(jnp.float32)
    return (
        total[None],
        pair_grads.reshape(1, 1, rows_all, 2 * width),
        token_grad[:, None],
    )


def solution(mesh):
    in_specs = (
        P(("rep", "exp"), None),
        P(("rep", "exp"), None),
        P(("rep", "exp"), None),
        P("exp", None, None),
        P("rep", "exp", None, None),
    )
    out_specs = (P("exp", "rep", None), P("rep", "exp", None, None), P(("rep", "exp"), None))
    return jax.shard_map(shards, mesh=mesh, in_specs=in_specs, out_specs=out_specs, check_vma=False)
```

time: 164 us -> 59.2 us (0.36)
  waiting for transfers between devices: 105 us -> 23.4 us
  starting transfers between devices: 6.49 us -> 22.9 us
  blocking collectives: 15.8 us -> 0 us
  between operations: 14.1 us -> 0.76 us
  matrix products: 12.5 us -> 0 us
  Pallas kernels: 0 us -> 9.17 us
  other arithmetic: 8.39 us -> 0.87 us
    reduce_scatter x1 -> x0, waiting for transfers between devices: 67.4 us -> none  [shards(): lax.psum_scatter(partial_value.astype(jnp.bfloat16), 'rep', scatter_dimen...]
    all_to_all x1 -> x0, waiting for transfers between devices: 37.8 us -> none  [shards(): lax.all_to_all(outgoing.reshape(peers, capacity, -1), 'exp', split_axis=0...]
    ppermute x0 -> x20, waiting for transfers between devices: none -> 23.4 us  [swap(): return lax.ppermute(value, axis, [(i, i ^ step) for i in range(n)])]
    ppermute x0 -> x20, starting transfers between devices: none -> 22.9 us  [swap(): return lax.ppermute(value, axis, [(i, i ^ step) for i in range(n)])]
    all_to_all x2 -> x0, blocking collectives: 15.8 us -> none  [the longest x1 7.92 us: shards(): lax.all_to_all(router.reshape(peers, capacity), 'exp', split_axis=0, conc...]
    dot_general x3 -> x0, matrix products: 12.5 us -> none  [the longest x1 6 us: shards(): lax.dot_general(received, scaled, (((0,), (0,)), ((), ())), preferred_ele...]
    pallas_call x0 -> x8, Pallas kernels: none -> 9.17 us  [kernel_call(): pl.pallas_call(kernel, out_shape=outs, compiler_params=pltpu.CompilerPara...]
    all_to_all x1 -> x0, starting transfers between devices: 6.46 us -> none  [shards(): lax.all_to_all(outgoing.reshape(peers, capacity, -1), 'exp', split_axis=0...]
  transfers between devices with their start and end apart: 2 -> 20, of which waited for: 2 -> 7; matrix products, arithmetic and copies ran while one was open for 1% -> 0% of each run, Pallas kernels for 0% -> 14%
where the time goes in v1:
time: 59.2 us; the launch traced here: 59 us
  waiting for transfers between devices  23.4 us (40%)
  starting transfers between devices  22.9 us (39%)
  Pallas kernels  9.17 us (15%)
  local copies, waits for them, and re-layouts  1.94 us (3%)
  other arithmetic  0.87 us (1%)
  between operations  0.76 us (1%)
    ppermute x20, waiting for transfers between devices, swap(): return lax.ppermute(value, axis, [(i, i ^ step) for i in range(n)])  23.4 us
    ppermute x20, starting transfers between devices, swap(): return lax.ppermute(value, axis, [(i, i ^ step) for i in range(n)])  22.9 us
    pallas_call x8, Pallas kernels, kernel_call(): pl.pallas_call(kernel, out_shape=outs, compiler_params=pltpu.CompilerPara...  9.17 us
    unnamed x14, local copies, waits for them, and re-layouts  1.91 us
  transfers between devices with their start and end apart: 20, of which 7 were waited for; matrix products, arithmetic and copies ran while one was open for 0% of the time, Pallas kernels for 14%

profile of v1, /device:TPU:0, one launch (start us, length us, event | category | flops | bytes accessed | tf_op | source)
XLA Modules:
  0.0 59.0 jit_solution(9989140925124400615)
XLA Ops:
  0.6 0.5 collective-permute-start
  1.1 0.1 collective-permute-start.1
  1.2 0.4 collective-permute-start.2
  1.7 0.0 slice-start
  1.7 0.0 copy-start
  1.7 1.2 %copy-done = bf16[1,1,192,1536]{3,2,1,0:T(8,128)(2,1)S(1)} copy-done((bf16[1,1,192,1536]{3,2,1,0:T(8,128)(2,1)S(1)}, bf16[1,1,192,1536]{3,2,1,0:T(8,128)(2,1)}, u32[]{:S(2)}) %copy-start) | copy-done | bytes 589848
  2.9 0.0 copy-start.2
  2.9 0.2 prepare.1.refs_4_
  3.1 0.0 copy-start.1
  3.1 0.5 collective-permute-done.refs_1_
  3.6 0.0 collective-permute-done.1.refs_3_
  3.6 0.0 collective-permute-done.2.refs_5_
  3.7 0.7 %copy-done.2 = bf16[128,4096]{1,0:T(8,128)(2,1)S(1)} copy-done((bf16[128,4096]{1,0:T(8,128)(2,1)S(1)}, bf16[128,4096]{1,0:T(8,128)(2,1)}, u32[]{:S(2)}) %copy-start.2) | copy-done | bytes 1048600
  4.3 0.0 copy-done.3
  4.3 0.0 copy-done.4
  4.3 0.7 %place.1 = (bf16[4,48,1024]{2,1,0:T(8,128)(2,1)S(1)}, bf16[4,48,1024]{2,1,0:T(8,128)(2,1)S(1)}, bf16[4,48,1024]{2,1,0:T(8,128)(2,1)S(1)}, bf16[4,48,1024]{2,1,0:...) custom-call(bf16[128,4096]{1,0:T(8,128)(2,1)S(1)} %copy-done.2, ...), custom_call_target="tpu_custom_call" | custom-call | flops 1024 | bytes 1024 | tf_op jit(solution)/shard_map/place/pallas_call | solution.py:21
  5.0 2.7 %collective-permute-start.3 = (bf16[4,48,1024]{2,1,0:T(8,128)(2,1)S(1)}, bf16[4,48,1024]{2,1,0:T(8,128)(2,1)S(1)}, u32[]{:S(2)}, u32[]{:S(2)}) collective-permute-start(bf16[4,48,1024]{2,1,0:T(8,128)(2,1)S(1)} %get-tuple-element.46), channel_id=1, source_target_pairs={{0,2},{1,3},{2,0},{3,1},{4,6},{5,7},{6,4},{7,5},{8,10},{9,11},{10,... | collective-permute-start | bytes 1179656 | tf_op jit(solution)/shard_map/ppermute | solution.py:15
  7.7 2.5 %collective-permute-start.4 = (bf16[4,48,1024]{2,1,0:T(8,128)(2,1)S(1)}, bf16[4,48,1024]{2,1,0:T(8,128)(2,1)S(1)}, u32[]{:S(2)}, u32[]{:S(2)}) collective-permute-start(bf16[4,48,1024]{2,1,0:T(8,128)(2,1)S(1)} %get-tuple-element.47), channel_id=1, source_target_pairs={{0,6},{1,7},{2,4},{3,5},{4,2},{5,3},{6,0},{7,1},{8,14},{9,15},{10,... | collective-permute-start | bytes 1179656 | tf_op jit(solution)/shard_map/ppermute | solution.py:15
  10.2 2.4 %collective-permute-start.7 = (bf16[4,48,768]{2,1,0:T(8,128)(2,1)S(1)}, bf16[4,48,768]{2,1,0:T(8,128)(2,1)S(1)}, u32[]{:S(2)}, u32[]{:S(2)}) collective-permute-start(bf16[4,48,768]{2,1,0:T(8,128)(2,1)S(1)} %prepare.1.refs_4_), channel_id=1, source_target_pairs={{0,24},{8,16},{16,8},{24,0},{1,25},{9,17},{17,9},{25,1},{2,26},{10... | collective-permute-start | bytes 884744 | tf_op jit(solution)/shard_map/ppermute | solution.py:15
  12.7 0.5 collective-permute-start.6
  13.2 0.5 collective-permute-start.5
  13.7 7.3 %collective-permute-done.7.refs_7_ = bf16[4,48,768]{2,1,0:T(8,128)(2,1)S(1)} collective-permute-done((bf16[4,48,768]{2,1,0:T(8,128)(2,1)S(1)}, bf16[4,48,768]{2,1,0:T(8,128)(2,1)S(1)}, u32[]{:S(2)}, u32[]{:S(2)}) %collective-permute-start.7) | collective-permute-done | bytes 294944 | tf_op jit(solution)/shard_map/ppermute | solution.py:15
  21.1 5.2 %collective-permute-done.6.refs_6_ = bf16[4,48,768]{2,1,0:T(8,128)(2,1)S(1)} collective-permute-done((bf16[4,48,768]{2,1,0:T(8,128)(2,1)S(1)}, bf16[4,48,768]{2,1,0:T(8,128)(2,1)S(1)}, u32[]{:S(2)}, u32[]{:S(2)}) %collective-permute-start.6) | collective-permute-done | bytes 294944 | tf_op jit(solution)/shard_map/ppermute | solution.py:15
  26.2 0.1 collective-permute-done.5.refs_5_
  26.3 0.0 collective-permute-done.3.refs_1_
  26.3 1.8 %collective-permute-done.4.refs_2_ = bf16[4,48,1024]{2,1,0:T(8,128)(2,1)S(1)} collective-permute-done((bf16[4,48,1024]{2,1,0:T(8,128)(2,1)S(1)}, bf16[4,48,1024]{2,1,0:T(8,128)(2,1)S(1)}, u32[]{:S(2)}, u32[]{:S(2)}) %collective-permute-start.4) | collective-permute-done | bytes 393248 | tf_op jit(solution)/shard_map/ppermute | solution.py:15
  28.2 1.8 %collective-permute-start.8 = (bf16[4,48,1024]{2,1,0:T(8,128)(2,1)S(1)}, bf16[4,48,1024]{2,1,0:T(8,128)(2,1)S(1)}, u32[]{:S(2)}, u32[]{:S(2)}) collective-permute-start(bf16[4,48,1024]{2,1,0:T(8,128)(2,1)S(1)} %get-tuple-element.50), channel_id=1, source_target_pairs={{0,4},{1,5},{2,6},{3,7},{4,0},{5,1},{6,2},{7,3},{8,12},{9,13},{10,... | collective-permute-start | bytes 1179656 | tf_op jit(solution)/shard_map/ppermute | solution.py:15
  29.9 0.1 stack.1
  30.0 1.6 %collective-permute-start.9 = (bf16[144,1024]{1,0:T(8,128)(2,1)S(1)}, bf16[144,1024]{1,0:T(8,128)(2,1)S(1)}, u32[]{:S(2)}, u32[]{:S(2)}) collective-permute-start(bf16[144,1024]{1,0:T(8,128)(2,1)S(1)} %get-tuple-element.56), channel_id=1, source_target_pairs={{0,8},{8,0},{16,24},{24,16},{1,9},{9,1},{17,25},{25,17},{2,10},{10... | collective-permute-start | bytes 884744 | tf_op jit(solution)/shard_map/ppermute | solution.py:15
  31.6 1.5 %collective-permute-start.10 = (bf16[144,1024]{1,0:T(8,128)(2,1)S(1)}, bf16[144,1024]{1,0:T(8,128)(2,1)S(1)}, u32[]{:S(2)}, u32[]{:S(2)}) collective-permute-start(bf16[144,1024]{1,0:T(8,128)(2,1)S(1)} %get-tuple-element.57), channel_id=1, source_target_pairs={{0,16},{8,24},{16,0},{24,8},{1,17},{9,25},{17,1},{25,9},{2,18},{10... | collective-permute-start | bytes 884744 | tf_op jit(solution)/shard_map/ppermute | solution.py:15
  33.1 0.5 collective-permute-start.11
  33.6 0.0 slice-done
  33.6 0.0 slice-done.1
  33.6 0.0 copy-done.1
  33.6 2.1 %pull_early.1 = (bf16[4,48,1536]{2,1,0:T(8,128)(2,1)S(1)}, f32[1,48]{1,0:T(1,128)S(1)}, f32[1,48]{1,0:T(1,128)S(1)}, f32[1,48]{1,0:T(1,128)S(1)}) custom-call(bf16[4,48,1024]{2,1,0:T(8,128)(2,1)S(1)} %get-tuple-element.51.refs_0_, bf16[4,48,1024]{2,1,0:T(8,128)(2,1)S(1)} %collective-permute-done.3.refs_1_, ...), custom_call_target="tpu_custom_call" | custom-call | flops 1024 | bytes 1024 | tf_op jit(solution)/shard_map/pull_early/pallas_call | solution.py:21
  35.8 0.3 collective-permute-start.12
  36.1 4.0 %collective-permute-done.9.refs_1_ = bf16[144,1024]{1,0:T(8,128)(2,1)S(1)} collective-permute-done((bf16[144,1024]{1,0:T(8,128)(2,1)S(1)}, bf16[144,1024]{1,0:T(8,128)(2,1)S(1)}, u32[]{:S(2)}, u32[]{:S(2)}) %collective-permute-start.9) | collective-permute-done | bytes 294944 | tf_op jit(solution)/shard_map/ppermute | solution.py:15
  40.0 1.2 %collective-permute-start.13 = (f32[1,48]{1,0:T(1,128)S(1)}, f32[1,48]{1,0:T(1,128)S(1)}, u32[]{:S(2)}, u32[]{:S(2)}) collective-permute-start(f32[1,48]{1,0:T(1,128)S(1)} %get-tuple-element.65), channel_id=1, source_target_pairs={{0,6},{1,7},{2,4},{3,5},{4,2},{5,3},{6,0},{7,1},{8,14},{9,15},{10,... | collective-permute-start | bytes 584 | tf_op jit(solution)/shard_map/ppermute | solution.py:15
  41.2 4.4 %collective-permute-done.10.refs_2_ = bf16[144,1024]{1,0:T(8,128)(2,1)S(1)} collective-permute-done((bf16[144,1024]{1,0:T(8,128)(2,1)S(1)}, bf16[144,1024]{1,0:T(8,128)(2,1)S(1)}, u32[]{:S(2)}, u32[]{:S(2)}) %collective-permute-start.10) | collective-permute-done | bytes 294944 | tf_op jit(solution)/shard_map/ppermute | solution.py:15
  45.6 0.0 collective-permute-done.11.refs_3_
  45.6 1.5 %weight_early.1.refs_8_ = f32[1024,768]{1,0:T(8,128)S(1)} custom-call(bf16[144,1024]{1,0:T(8,128)(2,1)S(1)} %get-tuple-element.55.refs_0_, bf16[144,1024]{1,0:T(8,128)(2,1)S(1)} %collective-permute-done.9.refs_1_, bf16[144,1024]{1,0:T(8,128)(2,1)S(1)} %collective-permute-done.10.refs_2_, bf16[144,1024]{1,0:T(8,128)(2,1)S(1)} %collective-permute-done.11.refs_3_, ...), custom_call_target="tpu_custom_call" | custom-call | flops 1024 | bytes 1024 | tf_op jit(solution)/shard_map/weight_early/pallas_call | solution.py:21
  47.1 0.0 collective-permute-done.12
  47.1 0.0 collective-permute-done.13
  47.1 0.0 collective-permute-done.8.refs_0_
  47.1 2.4 %collective-permute-start.16 = (bf16[48,1024]{1,0:T(8,128)(2,1)S(1)}, bf16[48,1024]{1,0:T(8,128)(2,1)S(1)}, u32[]{:S(2)}, u32[]{:S(2)}) collective-permute-start(bf16[48,1024]{1,0:T(8,128)(2,1)S(1)} %get-tuple-element.87), channel_id=1, source_target_pairs={{0,24},{8,16},{16,8},{24,0},{1,25},{9,17},{17,9},{25,1},{2,26},{10... | collective-permute-start | bytes 294920 | tf_op jit(solution)/shard_map/ppermute | solution.py:15
  49.6 0.5 collective-permute-start.15
  50.1 0.6 %collective-permute-start.14 = (bf16[48,1024]{1,0:T(8,128)(2,1)S(1)}, bf16[48,1024]{1,0:T(8,128)(2,1)S(1)}, u32[]{:S(2)}, u32[]{:S(2)}) collective-permute-start(bf16[48,1024]{1,0:T(8,128)(2,1)S(1)} %get-tuple-element.89), channel_id=1, source_target_pairs={{0,8},{8,0},{16,24},{24,16},{1,9},{9,1},{17,25},{25,17},{2,10},{10... | collective-permute-start | bytes 294920 | tf_op jit(solution)/shard_map/ppermute | solution.py:15
  50.7 0.1 pad_maximum_fusion
  50.8 0.1 select_reduce_fusion
  50.9 0.1 collective-permute-start.17
  51.0 1.6 %pull_last.1 = (f32[48,768]{1,0:T(8,128)S(1)}, f32[1,24]{1,0:T(1,128)S(1)}, f32[1,24]{1,0:T(1,128)S(1)}) custom-call(bf16[4,48,1024]{2,1,0:T(8,128)(2,1)S(1)} %collective-permute-done.8.refs_0_, bf16[1,4096,768]{2,1,0:T(8,128)(2,1)S(1)} %bitcast.28, bf16[4,48,1536]{2,1,0:T(8,128)(2,1)S(1)} %bitcast.31), custom_call_target="tpu_custom_call" | custom-call | flops 1024 | bytes 1024 | tf_op jit(solution)/shard_map/pull_last/pallas_call | solution.py:21
  52.5 0.0 collective-permute-done.17
  52.5 1.5 %collective-permute-start.18 = (f32[1,24]{1,0:T(1,128)S(1)}, f32[1,24]{1,0:T(1,128)S(1)}, u32[]{:S(2)}, u32[]{:S(2)}) collective-permute-start(f32[1,24]{1,0:T(1,128)S(1)} %get-tuple-element.76), channel_id=1, source_target_pairs={{0,4},{1,5},{2,6},{3,7},{4,0},{5,1},{6,2},{7,3},{8,12},{9,13},{10,... | collective-permute-start | bytes 296 | tf_op jit(solution)/shard_map/ppermute | solution.py:15
  54.0 1.3 %collective-permute-start.19 = (f32[1,24]{1,0:T(1,128)S(1)}, f32[1,24]{1,0:T(1,128)S(1)}, u32[]{:S(2)}, u32[]{:S(2)}) collective-permute-start(f32[1,24]{1,0:T(1,128)S(1)} %get-tuple-element.77), channel_id=1, source_target_pairs={{0,5},{1,4},{2,7},{3,6},{4,1},{5,0},{6,3},{7,2},{8,13},{9,12},{10,... | collective-permute-start | bytes 296 | tf_op jit(solution)/shard_map/ppermute | solution.py:15
  55.3 0.0 collective-permute-done.16.refs_3_
  55.3 0.0 collective-permute-done.15.refs_2_
  55.3 0.0 collective-permute-done.14.refs_1_
  55.3 2.1 %weight_last.1 = f32[1,1024,768]{2,1,0:T(8,128)} custom-call(bf16[48,1024]{1,0:T(8,128)(2,1)S(1)} %get-tuple-element.90.refs_0_, bf16[48,1024]{1,0:T(8,128)(2,1)S(1)} %collective-permute-done.14.refs_1_, bf16[48,1024]{1,0:T(8,128)(2,1)S(1)} %collective-permute-done.15.refs_2_, bf16[48,1024]{1,0:T(8,128)(2,1)S(1)} %collective-permute-done.16.refs_3_, ...), custom_call_target="tpu_custom_call" | custom-call | flops 10000000000 | bytes 1024 | tf_op jit(solution)/shard_map/weight_last/pallas_call | solution.py:21
  57.4 0.9 %grads_last.1 = bf16[4,48,1536]{2,1,0:T(8,128)(2,1)} custom-call(f32[48,768]{1,0:T(8,128)S(1)} %get-tuple-element.78.refs_0_, bf16[4,48,1536]{2,1,0:T(8,128)(2,1)S(1)} %bitcast.32, bf16[4,48,1536]{2,1,0:T(8,128)(2,1)S(1)} %get-tuple-element.79.refs_2_), custom_call_target="tpu_custom_call" | custom-call | flops 1024 | bytes 1024 | tf_op jit(solution)/shard_map/grads_last/pallas_call | solution.py:21
  58.3 0.0 collective-permute-done.18
  58.3 0.0 collective-permute-done.19
  58.3 0.1 maximum_bitcast_fusion
  58.4 0.1 select_reduce_fusion.2
  58.5 0.5 fusion
  (6 shorter events, 0.0 us)
Async XLA Ops:
  0.6 3.0 %collective-permute-start = (bf16[128,4096]{1,0:T(8,128)(2,1)}, bf16[128,4096]{1,0:T(8,128)(2,1)S(1)}, u32[]{:S(2)}, u32[]{:S(2)}) collective-permute-start(bf16[128,4096]{1,0:T(8,128)(2,1)} %refs_0_.1), channel_id=1, source_target_pairs={{0,1},{1,0},{2,3},{3,2},{4,5},{5,4},{6,7},{7,6},{8,9},{9,8},{10,11... | collective-permute-start | bytes 3145736 | tf_op jit(solution)/shard_map/ppermute | solution.py:15
  1.1 2.5 %collective-permute-start.1 = (s32[1,128]{1,0:T(1,128)}, s32[1,128]{1,0:T(1,128)S(1)}, u32[]{:S(2)}, u32[]{:S(2)}) collective-permute-start(s32[1,128]{1,0:T(1,128)} %bitcast.35), channel_id=1, source_target_pairs={{0,1},{1,0},{2,3},{3,2},{4,5},{5,4},{6,7},{7,6},{8,9},{9,8},{10,11... | collective-permute-start | bytes 1544 | tf_op jit(solution)/shard_map/ppermute | solution.py:15
  1.2 2.4 %collective-permute-start.2 = (f32[1,128]{1,0:T(1,128)}, f32[1,128]{1,0:T(1,128)S(1)}, u32[]{:S(2)}, u32[]{:S(2)}) collective-permute-start(f32[1,128]{1,0:T(1,128)} %bitcast.33), channel_id=1, source_target_pairs={{0,1},{1,0},{2,3},{3,2},{4,5},{5,4},{6,7},{7,6},{8,9},{9,8},{10,11... | collective-permute-start | bytes 1544 | tf_op jit(solution)/shard_map/ppermute | solution.py:15
  1.7 31.9 %slice-start = ((s8[6291456]{0:T(1024)(128)(4,1)}), s8[4194304]{0:T(1024)(128)(4,1)S(1)}, s32[]{:S(2)}) async-start(s8[6291456]{0:T(1024)(128)(4,1)} %bitcast.27), calls=%async_computation | async-start | bytes 8388608
  1.7 1.2 %copy-start = (bf16[1,1,192,1536]{3,2,1,0:T(8,128)(2,1)S(1)}, bf16[1,1,192,1536]{3,2,1,0:T(8,128)(2,1)}, u32[]{:S(2)}) copy-start(bf16[1,1,192,1536]{3,2,1,0:T(8,128)(2,1)} %param.9) | copy-start | bytes 1769476
  2.9 1.4 %copy-start.2 = (bf16[128,4096]{1,0:T(8,128)(2,1)S(1)}, bf16[128,4096]{1,0:T(8,128)(2,1)}, u32[]{:S(2)}) copy-start(bf16[128,4096]{1,0:T(8,128)(2,1)} %refs_0_.1) | copy-start | bytes 3145732
  2.9 1.4 %copy-start.3 = (f32[128,1]{0,1:T(1,128)S(1)}, f32[128,1]{0,1:T(1,128)}, u32[]{:S(2)}) copy-start(f32[128,1]{0,1:T(1,128)} %param.7) | copy-start | bytes 1540
  2.9 1.4 %copy-start.4 = (s32[128,1]{0,1:T(1,128)S(1)}, s32[128,1]{0,1:T(1,128)}, u32[]{:S(2)}) copy-start(s32[128,1]{0,1:T(1,128)} %param.6) | copy-start | bytes 1540
  2.9 30.7 %slice-start.1 = ((s8[6291456]{0:T(1024)(128)(4,1)}), s8[2097152]{0:T(1024)(128)(4,1)S(1)}, s32[]{:S(2)}) async-start(s8[6291456]{0:T(1024)(128)(4,1)} %bitcast.27), calls=%async_computation.1 | async-start | bytes 4194304
  3.1 30.5 %copy-start.1 = (bf16[1,1,192,1536]{3,2,1,0:T(8,128)(2,1)S(1)}, bf16[1,1,192,1536]{3,2,1,0:T(8,128)(2,1)}, u32[]{:S(2)}) copy-start(bf16[1,1,192,1536]{3,2,1,0:T(8,128)(2,1)} %param.9) | copy-start | bytes 1769476
  5.0 21.3 %collective-permute-start.3 = (bf16[4,48,1024]{2,1,0:T(8,128)(2,1)S(1)}, bf16[4,48,1024]{2,1,0:T(8,128)(2,1)S(1)}, u32[]{:S(2)}, u32[]{:S(2)}) collective-permute-start(bf16[4,48,1024]{2,1,0:T(8,128)(2,1)S(1)} %get-tuple-element.46), channel_id=1, source_target_pairs={{0,2},{1,3},{2,0},{3,1},{4,6},{5,7},{6,4},{7,5},{8,10},{9,11},{10,... | collective-permute-start | bytes 1179656 | tf_op jit(solution)/shard_map/ppermute | solution.py:15
  7.7 20.4 %collective-permute-start.4 = (bf16[4,48,1024]{2,1,0:T(8,128)(2,1)S(1)}, bf16[4,48,1024]{2,1,0:T(8,128)(2,1)S(1)}, u32[]{:S(2)}, u32[]{:S(2)}) collective-permute-start(bf16[4,48,1024]{2,1,0:T(8,128)(2,1)S(1)} %get-tuple-element.47), channel_id=1, source_target_pairs={{0,6},{1,7},{2,4},{3,5},{4,2},{5,3},{6,0},{7,1},{8,14},{9,15},{10,... | collective-permute-start | bytes 1179656 | tf_op jit(solution)/shard_map/ppermute | solution.py:15
  10.2 10.8 %collective-permute-start.7 = (bf16[4,48,768]{2,1,0:T(8,128)(2,1)S(1)}, bf16[4,48,768]{2,1,0:T(8,128)(2,1)S(1)}, u32[]{:S(2)}, u32[]{:S(2)}) collective-permute-start(bf16[4,48,768]{2,1,0:T(8,128)(2,1)S(1)} %prepare.1.refs_4_), channel_id=1, source_target_pairs={{0,24},{8,16},{16,8},{24,0},{1,25},{9,17},{17,9},{25,1},{2,26},{10... | collective-permute-start | bytes 884744 | tf_op jit(solution)/shard_map/ppermute | solution.py:15
  12.7 13.6 %collective-permute-start.6 = (bf16[4,48,768]{2,1,0:T(8,128)(2,1)S(1)}, bf16[4,48,768]{2,1,0:T(8,128)(2,1)S(1)}, u32[]{:S(2)}, u32[]{:S(2)}) collective-permute-start(bf16[4,48,768]{2,1,0:T(8,128)(2,1)S(1)} %prepare.1.refs_4_), channel_id=1, source_target_pairs={{0,16},{8,24},{16,0},{24,8},{1,17},{9,25},{17,1},{25,9},{2,18},{10... | collective-permute-start | bytes 884744 | tf_op jit(solution)/shard_map/ppermute | solution.py:15
  13.2 13.2 %collective-permute-start.5 = (bf16[4,48,768]{2,1,0:T(8,128)(2,1)S(1)}, bf16[4,48,768]{2,1,0:T(8,128)(2,1)S(1)}, u32[]{:S(2)}, u32[]{:S(2)}) collective-permute-start(bf16[4,48,768]{2,1,0:T(8,128)(2,1)S(1)} %prepare.1.refs_4_), channel_id=1, source_target_pairs={{0,8},{8,0},{16,24},{24,16},{1,9},{9,1},{17,25},{25,17},{2,10},{10... | collective-permute-start | bytes 884744 | tf_op jit(solution)/shard_map/ppermute | solution.py:15
  28.2 18.9 %collective-permute-start.8 = (bf16[4,48,1024]{2,1,0:T(8,128)(2,1)S(1)}, bf16[4,48,1024]{2,1,0:T(8,128)(2,1)S(1)}, u32[]{:S(2)}, u32[]{:S(2)}) collective-permute-start(bf16[4,48,1024]{2,1,0:T(8,128)(2,1)S(1)} %get-tuple-element.50), channel_id=1, source_target_pairs={{0,4},{1,5},{2,6},{3,7},{4,0},{5,1},{6,2},{7,3},{8,12},{9,13},{10,... | collective-permute-start | bytes 1179656 | tf_op jit(solution)/shard_map/ppermute | solution.py:15
  30.0 10.0 %collective-permute-start.9 = (bf16[144,1024]{1,0:T(8,128)(2,1)S(1)}, bf16[144,1024]{1,0:T(8,128)(2,1)S(1)}, u32[]{:S(2)}, u32[]{:S(2)}) collective-permute-start(bf16[144,1024]{1,0:T(8,128)(2,1)S(1)} %get-tuple-element.56), channel_id=1, source_target_pairs={{0,8},{8,0},{16,24},{24,16},{1,9},{9,1},{17,25},{25,17},{2,10},{10... | collective-permute-start | bytes 884744 | tf_op jit(solution)/shard_map/ppermute | solution.py:15
  31.6 14.0 %collective-permute-start.10 = (bf16[144,1024]{1,0:T(8,128)(2,1)S(1)}, bf16[144,1024]{1,0:T(8,128)(2,1)S(1)}, u32[]{:S(2)}, u32[]{:S(2)}) collective-permute-start(bf16[144,1024]{1,0:T(8,128)(2,1)S(1)} %get-tuple-element.57), channel_id=1, source_target_pairs={{0,16},{8,24},{16,0},{24,8},{1,17},{9,25},{17,1},{25,9},{2,18},{10... | collective-permute-start | bytes 884744 | tf_op jit(solution)/shard_map/ppermute | solution.py:15
  33.1 12.5 %collective-permute-start.11 = (bf16[144,1024]{1,0:T(8,128)(2,1)S(1)}, bf16[144,1024]{1,0:T(8,128)(2,1)S(1)}, u32[]{:S(2)}, u32[]{:S(2)}) collective-permute-start(bf16[144,1024]{1,0:T(8,128)(2,1)S(1)} %get-tuple-element.58), channel_id=1, source_target_pairs={{0,24},{8,16},{16,8},{24,0},{1,25},{9,17},{17,9},{25,1},{2,26},{10... | collective-permute-start | bytes 884744 | tf_op jit(solution)/shard_map/ppermute | solution.py:15
  35.8 11.3 %collective-permute-start.12 = (f32[1,48]{1,0:T(1,128)S(1)}, f32[1,48]{1,0:T(1,128)S(1)}, u32[]{:S(2)}, u32[]{:S(2)}) collective-permute-start(f32[1,48]{1,0:T(1,128)S(1)} %get-tuple-element.64), channel_id=1, source_target_pairs={{0,2},{1,3},{2,0},{3,1},{4,6},{5,7},{6,4},{7,5},{8,10},{9,11},{10,... | collective-permute-start | bytes 584 | tf_op jit(solution)/shard_map/ppermute | solution.py:15
  40.0 7.1 %collective-permute-start.13 = (f32[1,48]{1,0:T(1,128)S(1)}, f32[1,48]{1,0:T(1,128)S(1)}, u32[]{:S(2)}, u32[]{:S(2)}) collective-permute-start(f32[1,48]{1,0:T(1,128)S(1)} %get-tuple-element.65), channel_id=1, source_target_pairs={{0,6},{1,7},{2,4},{3,5},{4,2},{5,3},{6,0},{7,1},{8,14},{9,15},{10,... | collective-permute-start | bytes 584 | tf_op jit(solution)/shard_map/ppermute | solution.py:15
  47.1 8.2 %collective-permute-start.16 = (bf16[48,1024]{1,0:T(8,128)(2,1)S(1)}, bf16[48,1024]{1,0:T(8,128)(2,1)S(1)}, u32[]{:S(2)}, u32[]{:S(2)}) collective-permute-start(bf16[48,1024]{1,0:T(8,128)(2,1)S(1)} %get-tuple-element.87), channel_id=1, source_target_pairs={{0,24},{8,16},{16,8},{24,0},{1,25},{9,17},{17,9},{25,1},{2,26},{10... | collective-permute-start | bytes 294920 | tf_op jit(solution)/shard_map/ppermute | solution.py:15
  49.6 5.8 %collective-permute-start.15 = (bf16[48,1024]{1,0:T(8,128)(2,1)S(1)}, bf16[48,1024]{1,0:T(8,128)(2,1)S(1)}, u32[]{:S(2)}, u32[]{:S(2)}) collective-permute-start(bf16[48,1024]{1,0:T(8,128)(2,1)S(1)} %get-tuple-element.88), channel_id=1, source_target_pairs={{0,16},{8,24},{16,0},{24,8},{1,17},{9,25},{17,1},{25,9},{2,18},{10... | collective-permute-start | bytes 294920 | tf_op jit(solution)/shard_map/ppermute | solution.py:15
  50.1 5.2 %collective-permute-start.14 = (bf16[48,1024]{1,0:T(8,128)(2,1)S(1)}, bf16[48,1024]{1,0:T(8,128)(2,1)S(1)}, u32[]{:S(2)}, u32[]{:S(2)}) collective-permute-start(bf16[48,1024]{1,0:T(8,128)(2,1)S(1)} %get-tuple-element.89), channel_id=1, source_target_pairs={{0,8},{8,0},{16,24},{24,16},{1,9},{9,1},{17,25},{25,17},{2,10},{10... | collective-permute-start | bytes 294920 | tf_op jit(solution)/shard_map/ppermute | solution.py:15
  50.9 1.7 %collective-permute-start.17 = (f32[128]{0:T(128)S(1)}, f32[128]{0:T(128)S(1)}, u32[]{:S(2)}, u32[]{:S(2)}) collective-permute-start(f32[128]{0:T(128)S(1)} %get-tuple-element.86), channel_id=1, source_target_pairs={{0,1},{1,0},{2,3},{3,2},{4,5},{5,4},{6,7},{7,6},{8,9},{9,8},{10,11... | collective-permute-start | bytes 1544 | tf_op jit(solution)/shard_map/ppermute | solution.py:15
  52.5 5.8 %collective-permute-start.18 = (f32[1,24]{1,0:T(1,128)S(1)}, f32[1,24]{1,0:T(1,128)S(1)}, u32[]{:S(2)}, u32[]{:S(2)}) collective-permute-start(f32[1,24]{1,0:T(1,128)S(1)} %get-tuple-element.76), channel_id=1, source_target_pairs={{0,4},{1,5},{2,6},{3,7},{4,0},{5,1},{6,2},{7,3},{8,12},{9,13},{10,... | collective-permute-start | bytes 296 | tf_op jit(solution)/shard_map/ppermute | solution.py:15
  54.0 4.3 %collective-permute-start.19 = (f32[1,24]{1,0:T(1,128)S(1)}, f32[1,24]{1,0:T(1,128)S(1)}, u32[]{:S(2)}, u32[]{:S(2)}) collective-permute-start(f32[1,24]{1,0:T(1,128)S(1)} %get-tuple-element.77), channel_id=1, source_target_pairs={{0,5},{1,4},{2,7},{3,6},{4,1},{5,0},{6,3},{7,2},{8,13},{9,12},{10,... | collective-permute-start | bytes 296 | tf_op jit(solution)/shard_map/ppermute | solution.py:15

commit v2 on v1

--- a/solution.py
+++ b/solution.py
@@ -6,6 +6,7 @@
 from jax.sharding import PartitionSpec as P
 
 WHOLE_VMEM = pl.BlockSpec(memory_space=pltpu.VMEM)
+IN_PLACE = pl.BlockSpec(memory_space=pl.ANY)
 SMALL = pl.CostEstimate(flops=1024, bytes_accessed=1024, transcendentals=0)
 LARGE = pl.CostEstimate(flops=10**10, bytes_accessed=1024, transcendentals=0)
 
@@ -28,12 +29,14 @@
     )(*operands)
 
 
-def prepare_kernel(saved, hidden):
-    width = hidden.shape[2]
+def copy_kernel(rows, out):
+    out[...] = rows[...]
+
+
+def hidden_kernel(saved, hidden):
     for k in range(saved.shape[0]):
-        gate = saved[k, :, :width].astype(jnp.float32)
-        up = saved[k, :, width:].astype(jnp.float32)
-        hidden[k] = (gate / (1.0 + jnp.exp(-gate)) * up).astype(jnp.bfloat16)
+        gate, up, sigmoid = gate_parts(saved[k])
+        hidden[k] = (gate * sigmoid * up).astype(jnp.bfloat16)
 
 
 def place_kernel(cap, order, cot, cot_sib, routes, routes_sib, weights, weights_sib, *outs):
@@ -132,12 +135,6 @@
     other[...] = jnp.where(core == 0, router[:, cap:], router[:, :cap])
 
 
-def grads_last_kernel(step, pulled, saved, early, grads):
-    chip = lax.axis_index("exp") // 2
-    grads[...] = early[...]
-    grads[chip ^ step] = pair_grads(pulled[...], saved[chip ^ step])
-
-
 def stack_kernel(count, *refs):
     for j, out in enumerate(refs[count:]):
         out[...] = jnp.concatenate([ref[j] for ref in refs[:count]], axis=0)
@@ -153,38 +150,57 @@
     )
 
 
-def units_of(hidden, steps):
+def units_kernel(order, *refs):
+    hidden, early, late = refs[:-2], refs[-2], refs[-1]
     chip = lax.axis_index("exp") // 2
-    return jnp.concatenate([ref[chip ^ k] for ref in hidden for k in steps], axis=0)
-
-
-def weight_early_kernel(steps, replicas, *refs):
-    rows, hidden, out = refs[:replicas], refs[replicas : 2 * replicas], refs[-1]
+    early[...] = jnp.concatenate([ref[chip ^ k] for ref in hidden for k in order[:-1]], axis=0)
+    late[...] = jnp.concatenate([ref[chip ^ order[-1]] for ref in hidden], axis=0)
+
+
+def weight_early_kernel(*refs):
+    rows, units, out = refs[:-2], refs[-2], refs[-1]
     out[...] = lax.dot_general(
         jnp.concatenate([ref[...] for ref in rows], axis=0),
-        units_of(hidden, steps),
+        units[...],
         (((0,), (0,)), ((), ())),
         preferred_element_type=jnp.float32,
     )
 
 
-def weight_last_kernel(steps, replicas, parts, *refs):
-    rows, hidden = refs[:replicas], refs[replicas : 2 * replicas]
-    early, out, held, sems = refs[2 * replicas :]
-    units = units_of(hidden, steps)
+def finish_kernel(step, replicas, parts, *refs):
+    rows = refs[:replicas]
+    units, early, pulled, saved, _, out, grads, held, held_grads, sems = refs[replicas:]
     size = early.shape[0] // parts
     copies = []
     for i in range(parts):
         span = pl.ds(i * size, size)
         left = jnp.concatenate([ref[:, i * size : (i + 1) * size] for ref in rows], axis=0)
         held[span, :] = early[span, :] + lax.dot_general(
-            left, units, (((0,), (0,)), ((), ())), preferred_element_type=jnp.float32
+            left, units[...], (((0,), (0,)), ((), ())), preferred_element_type=jnp.float32
         )
-        copy = pltpu.make_async_copy(held.at[span, :], out.at[0, span, :], sems.at[i])
-        copy.start()
-        copies.append(copy)
+        copies.append(pltpu.make_async_copy(held.at[span, :], out.at[0, span, :], sems.at[i]))
+        copies[-1].start()
+        if i == 0:
+            place = (lax.axis_index("exp") // 2) ^ step
+            held_grads[...] = pair_grads(pulled[...], saved[place])
+            copies.append(pltpu.make_async_copy(held_grads, grads.at[place], sems.at[parts]))
+            copies[-1].start()
     for copy in copies:
         copy.wait()
+
+
+def token_kernel(same, other, last_slots, own, sib, weights, out):
+    values = jnp.concatenate([same[...], other[...]], axis=1)
+    hot = lax.broadcasted_iota(jnp.int32, (values.shape[1], out.shape[1]), 0) == last_slots[...]
+    found = lax.dot_general(
+        jnp.broadcast_to(values, (8, values.shape[1])),
+        hot.astype(jnp.float32),
+        (((1,), (0,)), ((), ())),
+        precision=lax.Precision.HIGHEST,
+        preferred_element_type=jnp.float32,
+    )[0:1]
+    weight = weights[...].astype(jnp.bfloat16).astype(jnp.float32)
+    out[...] = (own[...] + sib[...] + found) / weight
 
 
 def shards(cotangent, routes, gate_weight, down_weight, saved_pre):
@@ -209,15 +225,13 @@
     cot_sib = swap(cotangent, "exp", 1)
     routes_sib = swap(routes, "exp", 1)
     weights_sib = swap(weights, "exp", 1)
-    saved = saved_pre.reshape(chips, pair, 2 * width)
-    hidden = kernel_call(
-        prepare_kernel,
-        [jax.ShapeDtypeStruct((chips, pair, width), jnp.bfloat16)],
-        [saved],
-        "prepare",
+    own_rows = kernel_call(
+        copy_kernel,
+        [jax.ShapeDtypeStruct((tokens, model), jnp.bfloat16)],
+        [cotangent],
+        "own_rows",
         LARGE,
     )[0]
-    hidden, cot_sib = lax.optimization_barrier((hidden, cot_sib))
     *blocks, slots, last_slots = kernel_call(
         lambda *refs: place_kernel(cap, order, *refs),
         [jax.ShapeDtypeStruct((replicas, pair, share), jnp.bfloat16)] * chips
@@ -225,7 +239,7 @@
             jax.ShapeDtypeStruct((2, tokens), jnp.int32),
             jax.ShapeDtypeStruct((1, tokens), jnp.int32),
         ],
-        [cotangent, cot_sib, routes, routes_sib, weights, weights_sib],
+        [own_rows, cot_sib, routes, routes_sib, weights, weights_sib],
         "place",
     )
 
@@ -233,13 +247,30 @@
     arrived = {0: blocks[0]}
     for k in reversed(early[1:]):
         arrived[k] = swap(blocks[k], "exp", 2 * k)
+    saved = saved_pre.reshape(chips, pair, 2 * width)
+    saved, slots = lax.optimization_barrier((saved, slots))
+    hidden = kernel_call(
+        hidden_kernel,
+        [jax.ShapeDtypeStruct((chips, pair, width), jnp.bfloat16)],
+        [saved],
+        "hidden",
+    )[0]
     hidden_of = [hidden] + [swap(hidden, "rep", j) for j in range(1, replicas)]
-
-    rows, last_block, hidden_of = lax.optimization_barrier(
-        ([arrived[k] for k in early], blocks[last], hidden_of)
+    units, units_last = kernel_call(
+        lambda *refs: units_kernel(order, *refs),
+        [
+            jax.ShapeDtypeStruct((replicas * len(early) * pair, width), jnp.bfloat16),
+            jax.ShapeDtypeStruct((replicas * pair, width), jnp.bfloat16),
+        ],
+        hidden_of,
+        "units",
+    )
+
+    rows, last_block, units = lax.optimization_barrier(
+        ([arrived[k] for k in early], blocks[last], units)
     )
     arrived = dict(zip(early, rows))
-    arrived[last] = swap(last_block, "exp", 2 * last)
+    last_rows = swap(last_block, "exp", 2 * last)
     early_rows = stack(rows)
     early_rows = [early_rows[0]] + [swap(early_rows[j], "rep", j) for j in range(1, replicas)]
     grads, *routers = kernel_call(
@@ -251,55 +282,57 @@
     )
     returned = routers[:1] + [swap(router, "exp", 2 * k) for router, k in zip(routers[1:], early[1:])]
     total = kernel_call(
-        lambda *refs: weight_early_kernel(early, replicas, *refs),
+        weight_early_kernel,
         [jax.ShapeDtypeStruct((share, width), jnp.float32)],
-        [*early_rows, *hidden_of],
+        [*early_rows, units],
         "weight_early",
     )[0]
 
-    arrived[last], grads, total, returned = lax.optimization_barrier(
-        (arrived[last], grads, total, returned)
-    )
-    rows = arrived[last]
+    rows, grads, total, returned = lax.optimization_barrier((last_rows, grads, total, returned))
     late_rows = [rows[0]] + [swap(rows[j], "rep", j) for j in range(1, replicas)]
     pulled, *routers = kernel_call(
         lambda *refs: pull_last_kernel(last, *refs),
         [jax.ShapeDtypeStruct((pair, width), jnp.float32)]
         + [jax.ShapeDtypeStruct((1, cap), jnp.float32)] * 2,
-        [arrived[last], down_weight, saved],
+        [rows, down_weight, saved],
         "pull_last",
     )
     returned = jnp.concatenate(returned, axis=1).reshape(len(early) * pair, 1)
     slot_index = lax.broadcasted_iota(jnp.int32, (len(early) * pair, 1), 0)
     sums = [
-        jnp.sum(jnp.where(slot_index == slots[i][None, :], returned, 0.0), axis=0)
-        for i in range(2)
+        jnp.sum(jnp.where(slot_index == ids, returned, 0.0), axis=0, keepdims=True)
+        for ids in (slots[0:1], slots[1:2])
     ]
     sum_sib = swap(sums[1], "exp", 1)
     routers, sum_sib = lax.optimization_barrier((routers, sum_sib))
     returned_last = [swap(routers[i], "exp", 2 * last + i) for i in range(2)]
-    weight_grad = kernel_call(
-        lambda *refs: weight_last_kernel([last], replicas, 4, *refs),
-        jax.ShapeDtypeStruct((1, share, width), jnp.float32),
-        [*late_rows, *hidden_of, total],
-        "weight_last",
+    parts = 4
+    weight_grad, grads = kernel_call(
+        lambda *refs: finish_kernel(last, replicas, parts, *refs),
+        [
+            jax.ShapeDtypeStruct((1, share, width), jnp.float32),
+            jax.ShapeDtypeStruct(saved.shape, jnp.bfloat16),
+        ],
+        [*late_rows, units_last, total, pulled, saved, grads],
+        "finish",
         LARGE,
-        out_specs=pl.BlockSpec(memory_space=pl.ANY),
-        scratch_shapes=[pltpu.VMEM((share, width), jnp.float32), pltpu.SemaphoreType.DMA((4,))],
-    )
-    weight_grad, pulled = lax.optimization_barrier((weight_grad, pulled))
-    grads = kernel_call(
-        lambda *refs: grads_last_kernel(last, *refs),
-        [jax.ShapeDtypeStruct(saved.shape, jnp.bfloat16)],
-        [pulled, saved, grads],
-        "grads_last",
+        in_specs=[WHOLE_VMEM] * (replicas + 4) + [IN_PLACE],
+        out_specs=[IN_PLACE] * 2,
+        input_output_aliases={replicas + 4: 1},
+        scratch_shapes=[
+            pltpu.VMEM((share, width), jnp.float32),
+            pltpu.VMEM((pair, 2 * width), jnp.bfloat16),
+            pltpu.SemaphoreType.DMA((parts + 1,)),
+        ],
+    )
+    returned_last, weight_grad = lax.optimization_barrier((returned_last, weight_grad))
+    token_grad = kernel_call(
+        token_kernel,
+        [jax.ShapeDtypeStruct((1, tokens), jnp.float32)],
+        [*returned_last, last_slots, sums[0], sum_sib, weights],
+        "token",
     )[0]
-    returned_last, grads = lax.optimization_barrier((returned_last, grads))
-    returned = jnp.concatenate(returned_last, axis=1).reshape(pair, 1)
-    slot_index = lax.broadcasted_iota(jnp.int32, (pair, 1), 0)
-    last_sum = jnp.sum(jnp.where(slot_index == last_slots, returned, 0.0), axis=0)
-    token_grad = (sums[0] + sum_sib + last_sum) / weights[0].astype(jnp.bfloat16).astype(jnp.float32)
-    return (weight_grad, grads.reshape(1, 1, rows_all, 2 * width), token_grad[:, None])
+    return (weight_grad, grads.reshape(1, 1, rows_all, 2 * width), token_grad.reshape(tokens, 1))
 
 
 def plain_shards(cotangent, routes, gate_weight, down_weight, saved_pre):

time: 59.2 us -> 57.7 us (0.975)
  waiting for transfers between devices: 23.4 us -> 22 us
  other arithmetic: 0.87 us -> 0.18 us
    ppermute x20, waiting for transfers between devices: 23.4 us -> 22 us  [swap(): return lax.ppermute(value, axis, [(i, i ^ step) for i in range(n)])]
    pallas_call x8 -> x10, Pallas kernels: 9.17 us -> 9.76 us  [kernel_call(): pl.pallas_call(kernel, out_shape=outs, compiler_params=pltpu.CompilerPara...]
    broadcast_in_dim x2 -> x0, other arithmetic: 0.59 us -> none  [the longest x1 0.52 us: shards(): token_grad[:, None]]
    unnamed x14 -> x12, local copies, waits for them, and re-layouts: 1.91 us -> 1.53 us
  transfers between devices with their start and end apart: 20 -> 20, of which waited for: 7 -> 8; matrix products, arithmetic and copies ran while one was open for 0% -> 0% of each run, Pallas kernels for 14% -> 15%
where the time goes in v2:
time: 57.7 us; the launch traced here: 57.6 us
  starting transfers between devices  23.3 us (40%)
  waiting for transfers between devices  22 us (38%)
  Pallas kernels  9.76 us (17%)
  local copies, waits for them, and re-layouts  1.56 us (3%)
  between operations  0.76 us (1%)
    ppermute x20, starting transfers between devices, swap(): return lax.ppermute(value, axis, [(i, i ^ step) for i in range(n)])  23.3 us
    ppermute x20, waiting for transfers between devices, swap(): return lax.ppermute(value, axis, [(i, i ^ step) for i in range(n)])  22 us
    pallas_call x10, Pallas kernels, kernel_call(): pl.pallas_call(kernel, out_shape=outs, compiler_params=pltpu.CompilerPara...  9.76 us
    unnamed x12, local copies, waits for them, and re-layouts  1.53 us
  transfers between devices with their start and end apart: 20, of which 8 were waited for; matrix products, arithmetic and copies ran while one was open for 0% of the time, Pallas kernels for 15%

profile of v2, /device:TPU:0, one launch (start us, length us, event | category | flops | bytes accessed | tf_op | source)
XLA Modules:
  0.0 57.6 jit_solution(15208562519843940607)
XLA Ops:
  0.6 0.5 collective-permute-start
  1.1 0.1 collective-permute-start.1
  1.2 0.0 slice-start
  1.2 0.0 copy-start.1
  1.2 0.0 copy-start.2
  1.2 0.0 copy-start
  1.2 0.0 slice-start.1
  1.2 0.5 collective-permute-start.2
  1.7 0.0 copy-start.3
  1.7 1.5 %copy-done.3 = bf16[128,4096]{1,0:T(8,128)(2,1)S(1)} copy-done((bf16[128,4096]{1,0:T(8,128)(2,1)S(1)}, bf16[128,4096]{1,0:T(8,128)(2,1)}, u32[]{:S(2)}) %copy-start.3) | copy-done | bytes 1048600
  3.3 0.1 own_rows.1.refs_0_
  3.3 0.3 collective-permute-done.1.refs_3_
  3.6 0.0 collective-permute-done.2.refs_5_
  3.7 0.0 collective-permute-done.refs_1_
  3.7 0.0 copy-done.1
  3.7 0.0 copy-done.2
  3.7 0.7 %place.1 = (bf16[4,48,1024]{2,1,0:T(8,128)(2,1)S(1)}, bf16[4,48,1024]{2,1,0:T(8,128)(2,1)S(1)}, bf16[4,48,1024]{2,1,0:T(8,128)(2,1)S(1)}, bf16[4,48,1024]{2,1,0:...) custom-call(bf16[128,4096]{1,0:T(8,128)(2,1)S(1)} %own_rows.1.refs_0_, ...), custom_call_target="tpu_custom_call" | custom-call | flops 1024 | bytes 1024 | tf_op jit(solution)/shard_map/place/pallas_call | solution.py:22
  4.4 3.0 %collective-permute-start.3 = (bf16[4,48,1024]{2,1,0:T(8,128)(2,1)S(1)}, bf16[4,48,1024]{2,1,0:T(8,128)(2,1)S(1)}, u32[]{:S(2)}, u32[]{:S(2)}) collective-permute-start(bf16[4,48,1024]{2,1,0:T(8,128)(2,1)S(1)} %get-tuple-element.44), channel_id=1, source_target_pairs={{0,2},{1,3},{2,0},{3,1},{4,6},{5,7},{6,4},{7,5},{8,10},{9,11},{10,... | collective-permute-start | bytes 1179656 | tf_op jit(solution)/shard_map/ppermute | solution.py:16
  7.4 2.5 %collective-permute-start.4 = (bf16[4,48,1024]{2,1,0:T(8,128)(2,1)S(1)}, bf16[4,48,1024]{2,1,0:T(8,128)(2,1)S(1)}, u32[]{:S(2)}, u32[]{:S(2)}) collective-permute-start(bf16[4,48,1024]{2,1,0:T(8,128)(2,1)S(1)} %get-tuple-element.45), channel_id=1, source_target_pairs={{0,6},{1,7},{2,4},{3,5},{4,2},{5,3},{6,0},{7,1},{8,14},{9,15},{10,... | collective-permute-start | bytes 1179656 | tf_op jit(solution)/shard_map/ppermute | solution.py:16
  9.9 0.0 copy-done
  9.9 0.2 hidden.1.refs_0_
  10.0 2.5 %collective-permute-start.7 = (bf16[4,48,768]{2,1,0:T(8,128)(2,1)S(1)}, bf16[4,48,768]{2,1,0:T(8,128)(2,1)S(1)}, u32[]{:S(2)}, u32[]{:S(2)}) collective-permute-start(bf16[4,48,768]{2,1,0:T(8,128)(2,1)S(1)} %hidden.1.refs_0_), channel_id=1, source_target_pairs={{0,24},{8,16},{16,8},{24,0},{1,25},{9,17},{17,9},{25,1},{2,26},{10... | collective-permute-start | bytes 884744 | tf_op jit(solution)/shard_map/ppermute | solution.py:16
  12.6 0.5 collective-permute-start.6
  13.1 0.5 collective-permute-start.5
  13.6 7.4 %collective-permute-done.7.refs_3_ = bf16[4,48,768]{2,1,0:T(8,128)(2,1)S(1)} collective-permute-done((bf16[4,48,768]{2,1,0:T(8,128)(2,1)S(1)}, bf16[4,48,768]{2,1,0:T(8,128)(2,1)S(1)}, u32[]{:S(2)}, u32[]{:S(2)}) %collective-permute-start.7) | collective-permute-done | bytes 294944 | tf_op jit(solution)/shard_map/ppermute | solution.py:16
  21.0 4.8 %collective-permute-done.6.refs_2_ = bf16[4,48,768]{2,1,0:T(8,128)(2,1)S(1)} collective-permute-done((bf16[4,48,768]{2,1,0:T(8,128)(2,1)S(1)}, bf16[4,48,768]{2,1,0:T(8,128)(2,1)S(1)}, u32[]{:S(2)}, u32[]{:S(2)}) %collective-permute-start.6) | collective-permute-done | bytes 294944 | tf_op jit(solution)/shard_map/ppermute | solution.py:16
  25.8 0.1 collective-permute-done.5.refs_1_
  25.9 0.1 units.1
  26.0 0.0 collective-permute-done.3.refs_1_
  26.0 1.5 %collective-permute-done.4.refs_2_ = bf16[4,48,1024]{2,1,0:T(8,128)(2,1)S(1)} collective-permute-done((bf16[4,48,1024]{2,1,0:T(8,128)(2,1)S(1)}, bf16[4,48,1024]{2,1,0:T(8,128)(2,1)S(1)}, u32[]{:S(2)}, u32[]{:S(2)}) %collective-permute-start.4) | collective-permute-done | bytes 393248 | tf_op jit(solution)/shard_map/ppermute | solution.py:16
  27.5 1.7 %collective-permute-start.8 = (bf16[4,48,1024]{2,1,0:T(8,128)(2,1)S(1)}, bf16[4,48,1024]{2,1,0:T(8,128)(2,1)S(1)}, u32[]{:S(2)}, u32[]{:S(2)}) collective-permute-start(bf16[4,48,1024]{2,1,0:T(8,128)(2,1)S(1)} %get-tuple-element.50), channel_id=1, source_target_pairs={{0,4},{1,5},{2,6},{3,7},{4,0},{5,1},{6,2},{7,3},{8,12},{9,13},{10,... | collective-permute-start | bytes 1179656 | tf_op jit(solution)/shard_map/ppermute | solution.py:16
  29.3 0.1 stack.1
  29.3 1.6 %collective-permute-start.9 = (bf16[144,1024]{1,0:T(8,128)(2,1)S(1)}, bf16[144,1024]{1,0:T(8,128)(2,1)S(1)}, u32[]{:S(2)}, u32[]{:S(2)}) collective-permute-start(bf16[144,1024]{1,0:T(8,128)(2,1)S(1)} %get-tuple-element.56), channel_id=1, source_target_pairs={{0,8},{8,0},{16,24},{24,16},{1,9},{9,1},{17,25},{25,17},{2,10},{10... | collective-permute-start | bytes 884744 | tf_op jit(solution)/shard_map/ppermute | solution.py:16
  30.9 1.5 %collective-permute-start.10 = (bf16[144,1024]{1,0:T(8,128)(2,1)S(1)}, bf16[144,1024]{1,0:T(8,128)(2,1)S(1)}, u32[]{:S(2)}, u32[]{:S(2)}) collective-permute-start(bf16[144,1024]{1,0:T(8,128)(2,1)S(1)} %get-tuple-element.57), channel_id=1, source_target_pairs={{0,16},{8,24},{16,0},{24,8},{1,17},{9,25},{17,1},{25,9},{2,18},{10... | collective-permute-start | bytes 884744 | tf_op jit(solution)/shard_map/ppermute | solution.py:16
  32.4 0.5 collective-permute-start.11
  32.9 0.0 slice-done
  32.9 0.0 slice-done.1
  32.9 2.8 %pull_early.1 = (bf16[4,48,1536]{2,1,0:T(8,128)(2,1)}, f32[1,48]{1,0:T(1,128)S(1)}, f32[1,48]{1,0:T(1,128)S(1)}, f32[1,48]{1,0:T(1,128)S(1)}) custom-call(bf16[4,48,1024]{2,1,0:T(8,128)(2,1)S(1)} %get-tuple-element.51.refs_0_, bf16[4,48,1024]{2,1,0:T(8,128)(2,1)S(1)} %collective-permute-done.3.refs_1_, ...), custom_call_target="tpu_custom_call" | custom-call | flops 1024 | bytes 1024 | tf_op jit(solution)/shard_map/pull_early/pallas_call | solution.py:22
  35.7 0.3 collective-permute-start.12
  36.0 3.4 %collective-permute-done.9.refs_1_ = bf16[144,1024]{1,0:T(8,128)(2,1)S(1)} collective-permute-done((bf16[144,1024]{1,0:T(8,128)(2,1)S(1)}, bf16[144,1024]{1,0:T(8,128)(2,1)S(1)}, u32[]{:S(2)}, u32[]{:S(2)}) %collective-permute-start.9) | collective-permute-done | bytes 294944 | tf_op jit(solution)/shard_map/ppermute | solution.py:16
  39.4 1.2 %collective-permute-start.13 = (f32[1,48]{1,0:T(1,128)S(1)}, f32[1,48]{1,0:T(1,128)S(1)}, u32[]{:S(2)}, u32[]{:S(2)}) collective-permute-start(f32[1,48]{1,0:T(1,128)S(1)} %get-tuple-element.62), channel_id=1, source_target_pairs={{0,6},{1,7},{2,4},{3,5},{4,2},{5,3},{6,0},{7,1},{8,14},{9,15},{10,... | collective-permute-start | bytes 584 | tf_op jit(solution)/shard_map/ppermute | solution.py:16
  40.5 4.0 %collective-permute-done.10.refs_2_ = bf16[144,1024]{1,0:T(8,128)(2,1)S(1)} collective-permute-done((bf16[144,1024]{1,0:T(8,128)(2,1)S(1)}, bf16[144,1024]{1,0:T(8,128)(2,1)S(1)}, u32[]{:S(2)}, u32[]{:S(2)}) %collective-permute-start.10) | collective-permute-done | bytes 294944 | tf_op jit(solution)/shard_map/ppermute | solution.py:16
  44.6 0.0 collective-permute-done.11.refs_3_
  44.6 1.5 %weight_early.1.refs_5_ = f32[1024,768]{1,0:T(8,128)S(1)} custom-call(bf16[144,1024]{1,0:T(8,128)(2,1)S(1)} %get-tuple-element.55.refs_0_, bf16[144,1024]{1,0:T(8,128)(2,1)S(1)} %collective-permute-done.9.refs_1_, bf16[144,1024]{1,0:T(8,128)(2,1)S(1)} %collective-permute-done.10.refs_2_, bf16[144,1024]{1,0:T(8,128)(2,1)S(1)} %collective-permute-done.11.refs_3_, ...), custom_call_target="tpu_custom_call" | custom-call | flops 1024 | bytes 1024 | tf_op jit(solution)/shard_map/weight_early/pallas_call | solution.py:22
  46.0 0.0 collective-permute-done.12
  46.1 0.0 collective-permute-done.13
  46.1 0.4 collective-permute-done.8.refs_0_
  46.5 1.9 %collective-permute-start.19 = (bf16[48,1024]{1,0:T(8,128)(2,1)S(1)}, bf16[48,1024]{1,0:T(8,128)(2,1)S(1)}, u32[]{:S(2)}, u32[]{:S(2)}) collective-permute-start(bf16[48,1024]{1,0:T(8,128)(2,1)S(1)} %get-tuple-element.85), channel_id=1, source_target_pairs={{0,24},{8,16},{16,8},{24,0},{1,25},{9,17},{17,9},{25,1},{2,26},{10... | collective-permute-start | bytes 294920 | tf_op jit(solution)/shard_map/ppermute | solution.py:16
  48.4 1.2 %collective-permute-start.18 = (bf16[48,1024]{1,0:T(8,128)(2,1)S(1)}, bf16[48,1024]{1,0:T(8,128)(2,1)S(1)}, u32[]{:S(2)}, u32[]{:S(2)}) collective-permute-start(bf16[48,1024]{1,0:T(8,128)(2,1)S(1)} %get-tuple-element.86), channel_id=1, source_target_pairs={{0,16},{8,24},{16,0},{24,8},{1,17},{9,25},{17,1},{25,9},{2,18},{10... | collective-permute-start | bytes 294920 | tf_op jit(solution)/shard_map/ppermute | solution.py:16
  49.5 0.5 collective-permute-start.17
  50.1 0.1 pad_maximum_fusion
  50.2 0.1 select_reduce_fusion
  50.3 0.1 collective-permute-start.14
  50.3 1.6 %pull_last.1 = (f32[48,768]{1,0:T(8,128)S(1)}, f32[1,24]{1,0:T(1,128)S(1)}, f32[1,24]{1,0:T(1,128)S(1)}) custom-call(bf16[4,48,1024]{2,1,0:T(8,128)(2,1)S(1)} %collective-permute-done.8.refs_0_, bf16[1,4096,768]{2,1,0:T(8,128)(2,1)S(1)} %bitcast.21, bf16[4,48,1536]{2,1,0:T(8,128)(2,1)S(1)} %bitcast.24), custom_call_target="tpu_custom_call" | custom-call | flops 1024 | bytes 1024 | tf_op jit(solution)/shard_map/pull_last/pallas_call | solution.py:22
  51.9 0.0 collective-permute-done.14.sib
  51.9 1.1 %collective-permute-start.15 = (f32[1,24]{1,0:T(1,128)S(1)}, f32[1,24]{1,0:T(1,128)S(1)}, u32[]{:S(2)}, u32[]{:S(2)}) collective-permute-start(f32[1,24]{1,0:T(1,128)S(1)} %get-tuple-element.70), channel_id=1, source_target_pairs={{0,4},{1,5},{2,6},{3,7},{4,0},{5,1},{6,2},{7,3},{8,12},{9,13},{10,... | collective-permute-start | bytes 296 | tf_op jit(solution)/shard_map/ppermute | solution.py:16
  53.0 1.7 %collective-permute-start.16 = (f32[1,24]{1,0:T(1,128)S(1)}, f32[1,24]{1,0:T(1,128)S(1)}, u32[]{:S(2)}, u32[]{:S(2)}) collective-permute-start(f32[1,24]{1,0:T(1,128)S(1)} %get-tuple-element.71), channel_id=1, source_target_pairs={{0,5},{1,4},{2,7},{3,6},{4,1},{5,0},{6,3},{7,2},{8,13},{9,12},{10,... | collective-permute-start | bytes 296 | tf_op jit(solution)/shard_map/ppermute | solution.py:16
  54.7 0.0 collective-permute-done.19.refs_3_
  54.7 0.0 collective-permute-done.18.refs_2_
  54.7 0.0 collective-permute-done.17.refs_1_
  54.7 2.1 %finish.1 = (f32[1,1024,768]{2,1,0:T(8,128)}, bf16[4,48,1536]{2,1,0:T(8,128)(2,1)}) custom-call(bf16[48,1024]{1,0:T(8,128)(2,1)S(1)} %get-tuple-element.88.refs_0_, bf16[48,1024]{1,0:T(8,128)(2,1)S(1)} %collective-permute-done.17.refs_1_, bf16[48,1024]{1,0:T(8,128)(2,1)S(1)} %collective-permute-done.18.refs_2_, ...), custom_call_target="tpu_custom_call", output_to_operand_aliasing={{1}: (8, {})} | custom-call | flops 10000000000 | bytes 1024 | tf_op jit(solution)/shard_map/finish/pallas_call | solution.py:22
  56.8 0.0 collective-permute-done.15.same
  56.8 0.0 collective-permute-done.16.other
  56.9 0.7 %token_.1 = f32[1,128]{1,0:T(1,128)} custom-call(f32[1,24]{1,0:T(1,128)S(1)} %collective-permute-done.15.same, f32[1,24]{1,0:T(1,128)S(1)} %collective-permute-done.16.other, s32[1,128]{1,0:T(1,128)S(1)} %get-tuple-element.81.last_slots, f32[1,128]{1,0:T(1,128)S(1)} %bitcast.29, f32[1,128]{1,0:T(1,128)S(1)} %collective-permute-done.14.sib, f32[1,128]{1,0:T(1,128)S(1)} %bitcast.28), custom_call_target="tpu_custom_call" | custom-call | flops 1024 | bytes 1024 | tf_op jit(solution)/shard_map/token/pallas_call | solution.py:22
  (3 shorter events, 0.0 us)
Async XLA Ops:
  0.6 3.0 %collective-permute-start = (bf16[128,4096]{1,0:T(8,128)(2,1)}, bf16[128,4096]{1,0:T(8,128)(2,1)S(1)}, u32[]{:S(2)}, u32[]{:S(2)}) collective-permute-start(bf16[128,4096]{1,0:T(8,128)(2,1)} %rows.1), channel_id=1, source_target_pairs={{0,1},{1,0},{2,3},{3,2},{4,5},{5,4},{6,7},{7,6},{8,9},{9,8},{10,11... | collective-permute-start | bytes 3145736 | tf_op jit(solution)/shard_map/ppermute | solution.py:16
  1.1 2.5 %collective-permute-start.1 = (s32[1,128]{1,0:T(1,128)}, s32[1,128]{1,0:T(1,128)S(1)}, u32[]{:S(2)}, u32[]{:S(2)}) collective-permute-start(s32[1,128]{1,0:T(1,128)} %bitcast.30), channel_id=1, source_target_pairs={{0,1},{1,0},{2,3},{3,2},{4,5},{5,4},{6,7},{7,6},{8,9},{9,8},{10,11... | collective-permute-start | bytes 1544 | tf_op jit(solution)/shard_map/ppermute | solution.py:16
  1.2 31.7 %slice-start = ((s8[6291456]{0:T(1024)(128)(4,1)}), s8[4194304]{0:T(1024)(128)(4,1)S(1)}, s32[]{:S(2)}) async-start(s8[6291456]{0:T(1024)(128)(4,1)} %bitcast.20), calls=%async_computation | async-start | bytes 8388608
  1.2 2.4 %copy-start.1 = (f32[128,1]{0,1:T(1,128)S(1)}, f32[128,1]{0,1:T(1,128)}, u32[]{:S(2)}) copy-start(f32[128,1]{0,1:T(1,128)} %param.7) | copy-start | bytes 1540
  1.2 2.4 %copy-start.2 = (s32[128,1]{0,1:T(1,128)S(1)}, s32[128,1]{0,1:T(1,128)}, u32[]{:S(2)}) copy-start(s32[128,1]{0,1:T(1,128)} %param.6) | copy-start | bytes 1540
  1.2 8.6 %copy-start = (bf16[1,1,192,1536]{3,2,1,0:T(8,128)(2,1)S(1)}, bf16[1,1,192,1536]{3,2,1,0:T(8,128)(2,1)}, u32[]{:S(2)}) copy-start(bf16[1,1,192,1536]{3,2,1,0:T(8,128)(2,1)} %param.9) | copy-start | bytes 1769476
  1.2 31.7 %slice-start.1 = ((s8[6291456]{0:T(1024)(128)(4,1)}), s8[2097152]{0:T(1024)(128)(4,1)S(1)}, s32[]{:S(2)}) async-start(s8[6291456]{0:T(1024)(128)(4,1)} %bitcast.20), calls=%async_computation.1 | async-start | bytes 4194304
  1.2 2.4 %collective-permute-start.2 = (f32[1,128]{1,0:T(1,128)}, f32[1,128]{1,0:T(1,128)S(1)}, u32[]{:S(2)}, u32[]{:S(2)}) collective-permute-start(f32[1,128]{1,0:T(1,128)} %bitcast.26), channel_id=1, source_target_pairs={{0,1},{1,0},{2,3},{3,2},{4,5},{5,4},{6,7},{7,6},{8,9},{9,8},{10,11... | collective-permute-start | bytes 1544 | tf_op jit(solution)/shard_map/ppermute | solution.py:16
  1.7 1.5 %copy-start.3 = (bf16[128,4096]{1,0:T(8,128)(2,1)S(1)}, bf16[128,4096]{1,0:T(8,128)(2,1)}, u32[]{:S(2)}) copy-start(bf16[128,4096]{1,0:T(8,128)(2,1)} %rows.1) | copy-start | bytes 3145732
  4.4 21.6 %collective-permute-start.3 = (bf16[4,48,1024]{2,1,0:T(8,128)(2,1)S(1)}, bf16[4,48,1024]{2,1,0:T(8,128)(2,1)S(1)}, u32[]{:S(2)}, u32[]{:S(2)}) collective-permute-start(bf16[4,48,1024]{2,1,0:T(8,128)(2,1)S(1)} %get-tuple-element.44), channel_id=1, source_target_pairs={{0,2},{1,3},{2,0},{3,1},{4,6},{5,7},{6,4},{7,5},{8,10},{9,11},{10,... | collective-permute-start | bytes 1179656 | tf_op jit(solution)/shard_map/ppermute | solution.py:16
  7.4 20.1 %collective-permute-start.4 = (bf16[4,48,1024]{2,1,0:T(8,128)(2,1)S(1)}, bf16[4,48,1024]{2,1,0:T(8,128)(2,1)S(1)}, u32[]{:S(2)}, u32[]{:S(2)}) collective-permute-start(bf16[4,48,1024]{2,1,0:T(8,128)(2,1)S(1)} %get-tuple-element.45), channel_id=1, source_target_pairs={{0,6},{1,7},{2,4},{3,5},{4,2},{5,3},{6,0},{7,1},{8,14},{9,15},{10,... | collective-permute-start | bytes 1179656 | tf_op jit(solution)/shard_map/ppermute | solution.py:16
  10.0 10.9 %collective-permute-start.7 = (bf16[4,48,768]{2,1,0:T(8,128)(2,1)S(1)}, bf16[4,48,768]{2,1,0:T(8,128)(2,1)S(1)}, u32[]{:S(2)}, u32[]{:S(2)}) collective-permute-start(bf16[4,48,768]{2,1,0:T(8,128)(2,1)S(1)} %hidden.1.refs_0_), channel_id=1, source_target_pairs={{0,24},{8,16},{16,8},{24,0},{1,25},{9,17},{17,9},{25,1},{2,26},{10... | collective-permute-start | bytes 884744 | tf_op jit(solution)/shard_map/ppermute | solution.py:16
  12.6 13.3 %collective-permute-start.6 = (bf16[4,48,768]{2,1,0:T(8,128)(2,1)S(1)}, bf16[4,48,768]{2,1,0:T(8,128)(2,1)S(1)}, u32[]{:S(2)}, u32[]{:S(2)}) collective-permute-start(bf16[4,48,768]{2,1,0:T(8,128)(2,1)S(1)} %hidden.1.refs_0_), channel_id=1, source_target_pairs={{0,16},{8,24},{16,0},{24,8},{1,17},{9,25},{17,1},{25,9},{2,18},{10... | collective-permute-start | bytes 884744 | tf_op jit(solution)/shard_map/ppermute | solution.py:16
  13.1 12.9 %collective-permute-start.5 = (bf16[4,48,768]{2,1,0:T(8,128)(2,1)S(1)}, bf16[4,48,768]{2,1,0:T(8,128)(2,1)S(1)}, u32[]{:S(2)}, u32[]{:S(2)}) collective-permute-start(bf16[4,48,768]{2,1,0:T(8,128)(2,1)S(1)} %hidden.1.refs_0_), channel_id=1, source_target_pairs={{0,8},{8,0},{16,24},{24,16},{1,9},{9,1},{17,25},{25,17},{2,10},{10... | collective-permute-start | bytes 884744 | tf_op jit(solution)/shard_map/ppermute | solution.py:16
  27.5 19.0 %collective-permute-start.8 = (bf16[4,48,1024]{2,1,0:T(8,128)(2,1)S(1)}, bf16[4,48,1024]{2,1,0:T(8,128)(2,1)S(1)}, u32[]{:S(2)}, u32[]{:S(2)}) collective-permute-start(bf16[4,48,1024]{2,1,0:T(8,128)(2,1)S(1)} %get-tuple-element.50), channel_id=1, source_target_pairs={{0,4},{1,5},{2,6},{3,7},{4,0},{5,1},{6,2},{7,3},{8,12},{9,13},{10,... | collective-permute-start | bytes 1179656 | tf_op jit(solution)/shard_map/ppermute | solution.py:16
  29.3 10.0 %collective-permute-start.9 = (bf16[144,1024]{1,0:T(8,128)(2,1)S(1)}, bf16[144,1024]{1,0:T(8,128)(2,1)S(1)}, u32[]{:S(2)}, u32[]{:S(2)}) collective-permute-start(bf16[144,1024]{1,0:T(8,128)(2,1)S(1)} %get-tuple-element.56), channel_id=1, source_target_pairs={{0,8},{8,0},{16,24},{24,16},{1,9},{9,1},{17,25},{25,17},{2,10},{10... | collective-permute-start | bytes 884744 | tf_op jit(solution)/shard_map/ppermute | solution.py:16
  30.9 13.6 %collective-permute-start.10 = (bf16[144,1024]{1,0:T(8,128)(2,1)S(1)}, bf16[144,1024]{1,0:T(8,128)(2,1)S(1)}, u32[]{:S(2)}, u32[]{:S(2)}) collective-permute-start(bf16[144,1024]{1,0:T(8,128)(2,1)S(1)} %get-tuple-element.57), channel_id=1, source_target_pairs={{0,16},{8,24},{16,0},{24,8},{1,17},{9,25},{17,1},{25,9},{2,18},{10... | collective-permute-start | bytes 884744 | tf_op jit(solution)/shard_map/ppermute | solution.py:16
  32.4 12.1 %collective-permute-start.11 = (bf16[144,1024]{1,0:T(8,128)(2,1)S(1)}, bf16[144,1024]{1,0:T(8,128)(2,1)S(1)}, u32[]{:S(2)}, u32[]{:S(2)}) collective-permute-start(bf16[144,1024]{1,0:T(8,128)(2,1)S(1)} %get-tuple-element.58), channel_id=1, source_target_pairs={{0,24},{8,16},{16,8},{24,0},{1,25},{9,17},{17,9},{25,1},{2,26},{10... | collective-permute-start | bytes 884744 | tf_op jit(solution)/shard_map/ppermute | solution.py:16
  35.7 10.4 %collective-permute-start.12 = (f32[1,48]{1,0:T(1,128)S(1)}, f32[1,48]{1,0:T(1,128)S(1)}, u32[]{:S(2)}, u32[]{:S(2)}) collective-permute-start(f32[1,48]{1,0:T(1,128)S(1)} %get-tuple-element.61), channel_id=1, source_target_pairs={{0,2},{1,3},{2,0},{3,1},{4,6},{5,7},{6,4},{7,5},{8,10},{9,11},{10,... | collective-permute-start | bytes 584 | tf_op jit(solution)/shard_map/ppermute | solution.py:16
  39.4 6.7 %collective-permute-start.13 = (f32[1,48]{1,0:T(1,128)S(1)}, f32[1,48]{1,0:T(1,128)S(1)}, u32[]{:S(2)}, u32[]{:S(2)}) collective-permute-start(f32[1,48]{1,0:T(1,128)S(1)} %get-tuple-element.62), channel_id=1, source_target_pairs={{0,6},{1,7},{2,4},{3,5},{4,2},{5,3},{6,0},{7,1},{8,14},{9,15},{10,... | collective-permute-start | bytes 584 | tf_op jit(solution)/shard_map/ppermute | solution.py:16
  46.5 8.2 %collective-permute-start.19 = (bf16[48,1024]{1,0:T(8,128)(2,1)S(1)}, bf16[48,1024]{1,0:T(8,128)(2,1)S(1)}, u32[]{:S(2)}, u32[]{:S(2)}) collective-permute-start(bf16[48,1024]{1,0:T(8,128)(2,1)S(1)} %get-tuple-element.85), channel_id=1, source_target_pairs={{0,24},{8,16},{16,8},{24,0},{1,25},{9,17},{17,9},{25,1},{2,26},{10... | collective-permute-start | bytes 294920 | tf_op jit(solution)/shard_map/ppermute | solution.py:16
  48.4 6.3 %collective-permute-start.18 = (bf16[48,1024]{1,0:T(8,128)(2,1)S(1)}, bf16[48,1024]{1,0:T(8,128)(2,1)S(1)}, u32[]{:S(2)}, u32[]{:S(2)}) collective-permute-start(bf16[48,1024]{1,0:T(8,128)(2,1)S(1)} %get-tuple-element.86), channel_id=1, source_target_pairs={{0,16},{8,24},{16,0},{24,8},{1,17},{9,25},{17,1},{25,9},{2,18},{10... | collective-permute-start | bytes 294920 | tf_op jit(solution)/shard_map/ppermute | solution.py:16
  49.5 5.2 %collective-permute-start.17 = (bf16[48,1024]{1,0:T(8,128)(2,1)S(1)}, bf16[48,1024]{1,0:T(8,128)(2,1)S(1)}, u32[]{:S(2)}, u32[]{:S(2)}) collective-permute-start(bf16[48,1024]{1,0:T(8,128)(2,1)S(1)} %get-tuple-element.87), channel_id=1, source_target_pairs={{0,8},{8,0},{16,24},{24,16},{1,9},{9,1},{17,25},{25,17},{2,10},{10... | collective-permute-start | bytes 294920 | tf_op jit(solution)/shard_map/ppermute | solution.py:16
  50.3 1.7 %collective-permute-start.14 = (f32[1,128]{1,0:T(1,128)S(1)}, f32[1,128]{1,0:T(1,128)S(1)}, u32[]{:S(2)}, u32[]{:S(2)}) collective-permute-start(f32[1,128]{1,0:T(1,128)S(1)} %bitcast.34), channel_id=1, source_target_pairs={{0,1},{1,0},{2,3},{3,2},{4,5},{5,4},{6,7},{7,6},{8,9},{9,8},{10,11... | collective-permute-start | bytes 1544 | tf_op jit(solution)/shard_map/ppermute | solution.py:16
  51.9 4.9 %collective-permute-start.15 = (f32[1,24]{1,0:T(1,128)S(1)}, f32[1,24]{1,0:T(1,128)S(1)}, u32[]{:S(2)}, u32[]{:S(2)}) collective-permute-start(f32[1,24]{1,0:T(1,128)S(1)} %get-tuple-element.70), channel_id=1, source_target_pairs={{0,4},{1,5},{2,6},{3,7},{4,0},{5,1},{6,2},{7,3},{8,12},{9,13},{10,... | collective-permute-start | bytes 296 | tf_op jit(solution)/shard_map/ppermute | solution.py:16
  53.0 3.9 %collective-permute-start.16 = (f32[1,24]{1,0:T(1,128)S(1)}, f32[1,24]{1,0:T(1,128)S(1)}, u32[]{:S(2)}, u32[]{:S(2)}) collective-permute-start(f32[1,24]{1,0:T(1,128)S(1)} %get-tuple-element.71), channel_id=1, source_target_pairs={{0,5},{1,4},{2,7},{3,6},{4,1},{5,0},{6,3},{7,2},{8,13},{9,12},{10,... | collective-permute-start | bytes 296 | tf_op jit(solution)/shard_map/ppermute | solution.py:16

commit v3 on v2

--- a/solution.py
+++ b/solution.py
@@ -245,7 +245,7 @@
 
     blocks = dict(zip(order, blocks))
     arrived = {0: blocks[0]}
-    for k in reversed(early[1:]):
+    for k in early[1:]:
         arrived[k] = swap(blocks[k], "exp", 2 * k)
     saved = saved_pre.reshape(chips, pair, 2 * width)
     saved, slots = lax.optimization_barrier((saved, slots))
@@ -267,11 +267,11 @@
     )
 
     rows, last_block, units = lax.optimization_barrier(
-        ([arrived[k] for k in early], blocks[last], units)
-    )
-    arrived = dict(zip(early, rows))
+        ([arrived[k] for k in reversed(early)], blocks[last], units)
+    )
+    arrived = dict(zip(reversed(early), rows))
     last_rows = swap(last_block, "exp", 2 * last)
-    early_rows = stack(rows)
+    early_rows = stack([arrived[k] for k in early])
     early_rows = [early_rows[0]] + [swap(early_rows[j], "rep", j) for j in range(1, replicas)]
     grads, *routers = kernel_call(
         lambda *refs: pull_early_kernel(early, *refs),
@@ -306,7 +306,7 @@
     sum_sib = swap(sums[1], "exp", 1)
     routers, sum_sib = lax.optimization_barrier((routers, sum_sib))
     returned_last = [swap(routers[i], "exp", 2 * last + i) for i in range(2)]
-    parts = 4
+    parts = 8
     weight_grad, grads = kernel_call(
         lambda *refs: finish_kernel(last, replicas, parts, *refs),
         [

time: 57.7 us -> 58.9 us (1.021)
  starting transfers between devices: 23.3 us -> 25.3 us
  waiting for transfers between devices: 22 us -> 21.2 us
    ppermute x20, starting transfers between devices: 23.3 us -> 25.3 us  [swap(): return lax.ppermute(value, axis, [(i, i ^ step) for i in range(n)])]
    ppermute x20, waiting for transfers between devices: 22 us -> 21.2 us  [swap(): return lax.ppermute(value, axis, [(i, i ^ step) for i in range(n)])]
  transfers between devices with their start and end apart: 20 -> 20, of which waited for: 8 -> 8; matrix products, arithmetic and copies ran while one was open for 0% -> 0% of each run, Pallas kernels for 15% -> 14%
where the time goes in v3:
time: 58.9 us; the launch traced here: 58.8 us
  starting transfers between devices  25.3 us (43%)
  waiting for transfers between devices  21.2 us (36%)
  Pallas kernels  9.73 us (17%)
  local copies, waits for them, and re-layouts  1.56 us (3%)
  between operations  0.77 us (1%)
    ppermute x20, starting transfers between devices, swap(): return lax.ppermute(value, axis, [(i, i ^ step) for i in range(n)])  25.3 us
    ppermute x20, waiting for transfers between devices, swap(): return lax.ppermute(value, axis, [(i, i ^ step) for i in range(n)])  21.2 us
    pallas_call x10, Pallas kernels, kernel_call(): pl.pallas_call(kernel, out_shape=outs, compiler_params=pltpu.CompilerPara...  9.73 us
    unnamed x12, local copies, waits for them, and re-layouts  1.53 us
  transfers between devices with their start and end apart: 20, of which 8 were waited for; matrix products, arithmetic and copies ran while one was open for 0% of the time, Pallas kernels for 14%

profile of v3, /device:TPU:0, one launch (start us, length us, event | category | flops | bytes accessed | tf_op | source)
XLA Modules:
  0.0 58.8 jit_solution(14627195093883029934)
XLA Ops:
  0.6 0.5 collective-permute-start
  1.1 0.1 collective-permute-start.1
  1.2 0.0 slice-start
  1.2 0.0 copy-start.1
  1.2 0.0 copy-start.2
  1.2 0.0 copy-start
  1.2 0.0 slice-start.1
  1.2 0.5 collective-permute-start.2
  1.7 0.0 copy-start.3
  1.7 1.5 %copy-done.3 = bf16[128,4096]{1,0:T(8,128)(2,1)S(1)} copy-done((bf16[128,4096]{1,0:T(8,128)(2,1)S(1)}, bf16[128,4096]{1,0:T(8,128)(2,1)}, u32[]{:S(2)}) %copy-start.3) | copy-done | bytes 1048600
  3.3 0.1 own_rows.1.refs_0_
  3.3 0.3 collective-permute-done.1.refs_3_
  3.6 0.0 collective-permute-done.2.refs_5_
  3.7 0.0 collective-permute-done.refs_1_
  3.7 0.0 copy-done.1
  3.7 0.0 copy-done.2
  3.7 0.7 %place.1 = (bf16[4,48,1024]{2,1,0:T(8,128)(2,1)S(1)}, bf16[4,48,1024]{2,1,0:T(8,128)(2,1)S(1)}, bf16[4,48,1024]{2,1,0:T(8,128)(2,1)S(1)}, bf16[4,48,1024]{2,1,0:...) custom-call(bf16[128,4096]{1,0:T(8,128)(2,1)S(1)} %own_rows.1.refs_0_, ...), custom_call_target="tpu_custom_call" | custom-call | flops 1024 | bytes 1024 | tf_op jit(solution)/shard_map/place/pallas_call | solution.py:22
  4.4 5.0 %collective-permute-start.3 = (bf16[4,48,1024]{2,1,0:T(8,128)(2,1)S(1)}, bf16[4,48,1024]{2,1,0:T(8,128)(2,1)S(1)}, u32[]{:S(2)}, u32[]{:S(2)}) collective-permute-start(bf16[4,48,1024]{2,1,0:T(8,128)(2,1)S(1)} %get-tuple-element.43), channel_id=1, source_target_pairs={{0,6},{1,7},{2,4},{3,5},{4,2},{5,3},{6,0},{7,1},{8,14},{9,15},{10,... | collective-permute-start | bytes 1179656 | tf_op jit(solution)/shard_map/ppermute | solution.py:16
  9.4 0.0 collective-permute-start.4
  9.4 0.0 copy-done
  9.4 0.2 hidden.1.refs_0_
  9.6 2.5 %collective-permute-start.7 = (bf16[4,48,768]{2,1,0:T(8,128)(2,1)S(1)}, bf16[4,48,768]{2,1,0:T(8,128)(2,1)S(1)}, u32[]{:S(2)}, u32[]{:S(2)}) collective-permute-start(bf16[4,48,768]{2,1,0:T(8,128)(2,1)S(1)} %hidden.1.refs_0_), channel_id=1, source_target_pairs={{0,24},{8,16},{16,8},{24,0},{1,25},{9,17},{17,9},{25,1},{2,26},{10... | collective-permute-start | bytes 884744 | tf_op jit(solution)/shard_map/ppermute | solution.py:16
  12.1 0.5 collective-permute-start.6
  12.6 0.5 collective-permute-start.5
  13.2 7.3 %collective-permute-done.7.refs_3_ = bf16[4,48,768]{2,1,0:T(8,128)(2,1)S(1)} collective-permute-done((bf16[4,48,768]{2,1,0:T(8,128)(2,1)S(1)}, bf16[4,48,768]{2,1,0:T(8,128)(2,1)S(1)}, u32[]{:S(2)}, u32[]{:S(2)}) %collective-permute-start.7) | collective-permute-done | bytes 294944 | tf_op jit(solution)/shard_map/ppermute | solution.py:16
  20.5 5.2 %collective-permute-done.6.refs_2_ = bf16[4,48,768]{2,1,0:T(8,128)(2,1)S(1)} collective-permute-done((bf16[4,48,768]{2,1,0:T(8,128)(2,1)S(1)}, bf16[4,48,768]{2,1,0:T(8,128)(2,1)S(1)}, u32[]{:S(2)}, u32[]{:S(2)}) %collective-permute-start.6) | collective-permute-done | bytes 294944 | tf_op jit(solution)/shard_map/ppermute | solution.py:16
  25.7 0.1 collective-permute-done.5.refs_1_
  25.8 0.1 units.1
  25.9 0.0 collective-permute-done.3.refs_2_
  25.9 1.5 %collective-permute-done.4.refs_1_ = bf16[4,48,1024]{2,1,0:T(8,128)(2,1)S(1)} collective-permute-done((bf16[4,48,1024]{2,1,0:T(8,128)(2,1)S(1)}, bf16[4,48,1024]{2,1,0:T(8,128)(2,1)S(1)}, u32[]{:S(2)}, u32[]{:S(2)}) %collective-permute-start.4) | collective-permute-done | bytes 393248 | tf_op jit(solution)/shard_map/ppermute | solution.py:16
  27.3 0.6 %collective-permute-start.8 = (bf16[4,48,1024]{2,1,0:T(8,128)(2,1)S(1)}, bf16[4,48,1024]{2,1,0:T(8,128)(2,1)S(1)}, u32[]{:S(2)}, u32[]{:S(2)}) collective-permute-start(bf16[4,48,1024]{2,1,0:T(8,128)(2,1)S(1)} %get-tuple-element.50), channel_id=1, source_target_pairs={{0,4},{1,5},{2,6},{3,7},{4,0},{5,1},{6,2},{7,3},{8,12},{9,13},{10,... | collective-permute-start | bytes 1179656 | tf_op jit(solution)/shard_map/ppermute | solution.py:16
  28.0 0.1 stack.1
  28.1 1.5 %collective-permute-start.9 = (bf16[144,1024]{1,0:T(8,128)(2,1)S(1)}, bf16[144,1024]{1,0:T(8,128)(2,1)S(1)}, u32[]{:S(2)}, u32[]{:S(2)}) collective-permute-start(bf16[144,1024]{1,0:T(8,128)(2,1)S(1)} %get-tuple-element.56), channel_id=1, source_target_pairs={{0,8},{8,0},{16,24},{24,16},{1,9},{9,1},{17,25},{25,17},{2,10},{10... | collective-permute-start | bytes 884744 | tf_op jit(solution)/shard_map/ppermute | solution.py:16
  29.6 1.5 %collective-permute-start.10 = (bf16[144,1024]{1,0:T(8,128)(2,1)S(1)}, bf16[144,1024]{1,0:T(8,128)(2,1)S(1)}, u32[]{:S(2)}, u32[]{:S(2)}) collective-permute-start(bf16[144,1024]{1,0:T(8,128)(2,1)S(1)} %get-tuple-element.57), channel_id=1, source_target_pairs={{0,16},{8,24},{16,0},{24,8},{1,17},{9,25},{17,1},{25,9},{2,18},{10... | collective-permute-start | bytes 884744 | tf_op jit(solution)/shard_map/ppermute | solution.py:16
  31.1 0.5 collective-permute-start.11
  31.6 0.0 slice-done
  31.6 0.0 slice-done.1
  31.6 2.8 %pull_early.1 = (bf16[4,48,1536]{2,1,0:T(8,128)(2,1)}, f32[1,48]{1,0:T(1,128)S(1)}, f32[1,48]{1,0:T(1,128)S(1)}, f32[1,48]{1,0:T(1,128)S(1)}) custom-call(bf16[4,48,1024]{2,1,0:T(8,128)(2,1)S(1)} %get-tuple-element.51.refs_0_, bf16[4,48,1024]{2,1,0:T(8,128)(2,1)S(1)} %collective-permute-done.4.refs_1_, ...), custom_call_target="tpu_custom_call" | custom-call | flops 1024 | bytes 1024 | tf_op jit(solution)/shard_map/pull_early/pallas_call | solution.py:22
  34.4 1.6 %collective-permute-start.12 = (f32[1,48]{1,0:T(1,128)S(1)}, f32[1,48]{1,0:T(1,128)S(1)}, u32[]{:S(2)}, u32[]{:S(2)}) collective-permute-start(f32[1,48]{1,0:T(1,128)S(1)} %get-tuple-element.61), channel_id=1, source_target_pairs={{0,2},{1,3},{2,0},{3,1},{4,6},{5,7},{6,4},{7,5},{8,10},{9,11},{10,... | collective-permute-start | bytes 584 | tf_op jit(solution)/shard_map/ppermute | solution.py:16
  36.0 2.0 %collective-permute-done.9.refs_1_ = bf16[144,1024]{1,0:T(8,128)(2,1)S(1)} collective-permute-done((bf16[144,1024]{1,0:T(8,128)(2,1)S(1)}, bf16[144,1024]{1,0:T(8,128)(2,1)S(1)}, u32[]{:S(2)}, u32[]{:S(2)}) %collective-permute-start.9) | collective-permute-done | bytes 294944 | tf_op jit(solution)/shard_map/ppermute | solution.py:16
  38.1 3.4 %collective-permute-start.13 = (f32[1,48]{1,0:T(1,128)S(1)}, f32[1,48]{1,0:T(1,128)S(1)}, u32[]{:S(2)}, u32[]{:S(2)}) collective-permute-start(f32[1,48]{1,0:T(1,128)S(1)} %get-tuple-element.62), channel_id=1, source_target_pairs={{0,6},{1,7},{2,4},{3,5},{4,2},{5,3},{6,0},{7,1},{8,14},{9,15},{10,... | collective-permute-start | bytes 584 | tf_op jit(solution)/shard_map/ppermute | solution.py:16
  41.5 2.5 %collective-permute-done.10.refs_2_ = bf16[144,1024]{1,0:T(8,128)(2,1)S(1)} collective-permute-done((bf16[144,1024]{1,0:T(8,128)(2,1)S(1)}, bf16[144,1024]{1,0:T(8,128)(2,1)S(1)}, u32[]{:S(2)}, u32[]{:S(2)}) %collective-permute-start.10) | collective-permute-done | bytes 294944 | tf_op jit(solution)/shard_map/ppermute | solution.py:16
  44.0 0.0 collective-permute-done.11.refs_3_
  44.0 1.5 %weight_early.1.refs_5_ = f32[1024,768]{1,0:T(8,128)S(1)} custom-call(bf16[144,1024]{1,0:T(8,128)(2,1)S(1)} %get-tuple-element.55.refs_0_, bf16[144,1024]{1,0:T(8,128)(2,1)S(1)} %collective-permute-done.9.refs_1_, bf16[144,1024]{1,0:T(8,128)(2,1)S(1)} %collective-permute-done.10.refs_2_, bf16[144,1024]{1,0:T(8,128)(2,1)S(1)} %collective-permute-done.11.refs_3_, ...), custom_call_target="tpu_custom_call" | custom-call | flops 1024 | bytes 1024 | tf_op jit(solution)/shard_map/weight_early/pallas_call | solution.py:22
  45.4 0.0 collective-permute-done.12
  45.5 0.0 collective-permute-done.13
  45.5 2.3 %collective-permute-done.8.refs_0_ = bf16[4,48,1024]{2,1,0:T(8,128)(2,1)S(1)} collective-permute-done((bf16[4,48,1024]{2,1,0:T(8,128)(2,1)S(1)}, bf16[4,48,1024]{2,1,0:T(8,128)(2,1)S(1)}, u32[]{:S(2)}, u32[]{:S(2)}) %collective-permute-start.8) | collective-permute-done | bytes 393248 | tf_op jit(solution)/shard_map/ppermute | solution.py:16
  47.8 2.5 %collective-permute-start.19 = (bf16[48,1024]{1,0:T(8,128)(2,1)S(1)}, bf16[48,1024]{1,0:T(8,128)(2,1)S(1)}, u32[]{:S(2)}, u32[]{:S(2)}) collective-permute-start(bf16[48,1024]{1,0:T(8,128)(2,1)S(1)} %get-tuple-element.85), channel_id=1, source_target_pairs={{0,24},{8,16},{16,8},{24,0},{1,25},{9,17},{17,9},{25,1},{2,26},{10... | collective-permute-start | bytes 294920 | tf_op jit(solution)/shard_map/ppermute | solution.py:16
  50.3 0.5 collective-permute-start.18
  50.8 0.5 collective-permute-start.17
  51.3 0.1 pad_maximum_fusion
  51.4 0.1 select_reduce_fusion
  51.5 0.1 collective-permute-start.14
  51.6 1.6 %pull_last.1 = (f32[48,768]{1,0:T(8,128)S(1)}, f32[1,24]{1,0:T(1,128)S(1)}, f32[1,24]{1,0:T(1,128)S(1)}) custom-call(bf16[4,48,1024]{2,1,0:T(8,128)(2,1)S(1)} %collective-permute-done.8.refs_0_, bf16[1,4096,768]{2,1,0:T(8,128)(2,1)S(1)} %bitcast.21, bf16[4,48,1536]{2,1,0:T(8,128)(2,1)S(1)} %bitcast.24), custom_call_target="tpu_custom_call" | custom-call | flops 1024 | bytes 1024 | tf_op jit(solution)/shard_map/pull_last/pallas_call | solution.py:22
  53.1 0.0 collective-permute-done.14.sib
  53.1 0.4 collective-permute-start.15
  53.6 2.3 %collective-permute-start.16 = (f32[1,24]{1,0:T(1,128)S(1)}, f32[1,24]{1,0:T(1,128)S(1)}, u32[]{:S(2)}, u32[]{:S(2)}) collective-permute-start(f32[1,24]{1,0:T(1,128)S(1)} %get-tuple-element.71), channel_id=1, source_target_pairs={{0,5},{1,4},{2,7},{3,6},{4,1},{5,0},{6,3},{7,2},{8,13},{9,12},{10,... | collective-permute-start | bytes 296 | tf_op jit(solution)/shard_map/ppermute | solution.py:16
  55.9 0.0 collective-permute-done.19.refs_3_
  55.9 0.0 collective-permute-done.18.refs_2_
  55.9 0.0 collective-permute-done.17.refs_1_
  55.9 2.1 %finish.1 = (f32[1,1024,768]{2,1,0:T(8,128)}, bf16[4,48,1536]{2,1,0:T(8,128)(2,1)}) custom-call(bf16[48,1024]{1,0:T(8,128)(2,1)S(1)} %get-tuple-element.88.refs_0_, bf16[48,1024]{1,0:T(8,128)(2,1)S(1)} %collective-permute-done.17.refs_1_, bf16[48,1024]{1,0:T(8,128)(2,1)S(1)} %collective-permute-done.18.refs_2_, ...), custom_call_target="tpu_custom_call", output_to_operand_aliasing={{1}: (8, {})} | custom-call | flops 10000000000 | bytes 1024 | tf_op jit(solution)/shard_map/finish/pallas_call | solution.py:22
  58.0 0.0 collective-permute-done.15.same
  58.0 0.0 collective-permute-done.16.other
  58.0 0.7 %token_.1 = f32[1,128]{1,0:T(1,128)} custom-call(f32[1,24]{1,0:T(1,128)S(1)} %collective-permute-done.15.same, f32[1,24]{1,0:T(1,128)S(1)} %collective-permute-done.16.other, s32[1,128]{1,0:T(1,128)S(1)} %get-tuple-element.81.last_slots, f32[1,128]{1,0:T(1,128)S(1)} %bitcast.29, f32[1,128]{1,0:T(1,128)S(1)} %collective-permute-done.14.sib, f32[1,128]{1,0:T(1,128)S(1)} %bitcast.28), custom_call_target="tpu_custom_call" | custom-call | flops 1024 | bytes 1024 | tf_op jit(solution)/shard_map/token/pallas_call | solution.py:22
  (3 shorter events, 0.0 us)
Async XLA Ops:
  0.6 3.0 %collective-permute-start = (bf16[128,4096]{1,0:T(8,128)(2,1)}, bf16[128,4096]{1,0:T(8,128)(2,1)S(1)}, u32[]{:S(2)}, u32[]{:S(2)}) collective-permute-start(bf16[128,4096]{1,0:T(8,128)(2,1)} %rows.1), channel_id=1, source_target_pairs={{0,1},{1,0},{2,3},{3,2},{4,5},{5,4},{6,7},{7,6},{8,9},{9,8},{10,11... | collective-permute-start | bytes 3145736 | tf_op jit(solution)/shard_map/ppermute | solution.py:16
  1.1 2.5 %collective-permute-start.1 = (s32[1,128]{1,0:T(1,128)}, s32[1,128]{1,0:T(1,128)S(1)}, u32[]{:S(2)}, u32[]{:S(2)}) collective-permute-start(s32[1,128]{1,0:T(1,128)} %bitcast.30), channel_id=1, source_target_pairs={{0,1},{1,0},{2,3},{3,2},{4,5},{5,4},{6,7},{7,6},{8,9},{9,8},{10,11... | collective-permute-start | bytes 1544 | tf_op jit(solution)/shard_map/ppermute | solution.py:16
  1.2 30.4 %slice-start = ((s8[6291456]{0:T(1024)(128)(4,1)}), s8[4194304]{0:T(1024)(128)(4,1)S(1)}, s32[]{:S(2)}) async-start(s8[6291456]{0:T(1024)(128)(4,1)} %bitcast.20), calls=%async_computation | async-start | bytes 8388608
  1.2 2.4 %copy-start.1 = (f32[128,1]{0,1:T(1,128)S(1)}, f32[128,1]{0,1:T(1,128)}, u32[]{:S(2)}) copy-start(f32[128,1]{0,1:T(1,128)} %param.7) | copy-start | bytes 1540
  1.2 2.4 %copy-start.2 = (s32[128,1]{0,1:T(1,128)S(1)}, s32[128,1]{0,1:T(1,128)}, u32[]{:S(2)}) copy-start(s32[128,1]{0,1:T(1,128)} %param.6) | copy-start | bytes 1540
  1.2 8.2 %copy-start = (bf16[1,1,192,1536]{3,2,1,0:T(8,128)(2,1)S(1)}, bf16[1,1,192,1536]{3,2,1,0:T(8,128)(2,1)}, u32[]{:S(2)}) copy-start(bf16[1,1,192,1536]{3,2,1,0:T(8,128)(2,1)} %param.9) | copy-start | bytes 1769476
  1.2 30.4 %slice-start.1 = ((s8[6291456]{0:T(1024)(128)(4,1)}), s8[2097152]{0:T(1024)(128)(4,1)S(1)}, s32[]{:S(2)}) async-start(s8[6291456]{0:T(1024)(128)(4,1)} %bitcast.20), calls=%async_computation.1 | async-start | bytes 4194304
  1.2 2.4 %collective-permute-start.2 = (f32[1,128]{1,0:T(1,128)}, f32[1,128]{1,0:T(1,128)S(1)}, u32[]{:S(2)}, u32[]{:S(2)}) collective-permute-start(f32[1,128]{1,0:T(1,128)} %bitcast.26), channel_id=1, source_target_pairs={{0,1},{1,0},{2,3},{3,2},{4,5},{5,4},{6,7},{7,6},{8,9},{9,8},{10,11... | collective-permute-start | bytes 1544 | tf_op jit(solution)/shard_map/ppermute | solution.py:16
  1.7 1.5 %copy-start.3 = (bf16[128,4096]{1,0:T(8,128)(2,1)S(1)}, bf16[128,4096]{1,0:T(8,128)(2,1)}, u32[]{:S(2)}) copy-start(bf16[128,4096]{1,0:T(8,128)(2,1)} %rows.1) | copy-start | bytes 3145732
  4.4 21.5 %collective-permute-start.3 = (bf16[4,48,1024]{2,1,0:T(8,128)(2,1)S(1)}, bf16[4,48,1024]{2,1,0:T(8,128)(2,1)S(1)}, u32[]{:S(2)}, u32[]{:S(2)}) collective-permute-start(bf16[4,48,1024]{2,1,0:T(8,128)(2,1)S(1)} %get-tuple-element.43), channel_id=1, source_target_pairs={{0,6},{1,7},{2,4},{3,5},{4,2},{5,3},{6,0},{7,1},{8,14},{9,15},{10,... | collective-permute-start | bytes 1179656 | tf_op jit(solution)/shard_map/ppermute | solution.py:16
  9.4 17.9 %collective-permute-start.4 = (bf16[4,48,1024]{2,1,0:T(8,128)(2,1)S(1)}, bf16[4,48,1024]{2,1,0:T(8,128)(2,1)S(1)}, u32[]{:S(2)}, u32[]{:S(2)}) collective-permute-start(bf16[4,48,1024]{2,1,0:T(8,128)(2,1)S(1)} %get-tuple-element.44), channel_id=1, source_target_pairs={{0,2},{1,3},{2,0},{3,1},{4,6},{5,7},{6,4},{7,5},{8,10},{9,11},{10,... | collective-permute-start | bytes 1179656 | tf_op jit(solution)/shard_map/ppermute | solution.py:16
  9.6 10.9 %collective-permute-start.7 = (bf16[4,48,768]{2,1,0:T(8,128)(2,1)S(1)}, bf16[4,48,768]{2,1,0:T(8,128)(2,1)S(1)}, u32[]{:S(2)}, u32[]{:S(2)}) collective-permute-start(bf16[4,48,768]{2,1,0:T(8,128)(2,1)S(1)} %hidden.1.refs_0_), channel_id=1, source_target_pairs={{0,24},{8,16},{16,8},{24,0},{1,25},{9,17},{17,9},{25,1},{2,26},{10... | collective-permute-start | bytes 884744 | tf_op jit(solution)/shard_map/ppermute | solution.py:16
  12.1 13.5 %collective-permute-start.6 = (bf16[4,48,768]{2,1,0:T(8,128)(2,1)S(1)}, bf16[4,48,768]{2,1,0:T(8,128)(2,1)S(1)}, u32[]{:S(2)}, u32[]{:S(2)}) collective-permute-start(bf16[4,48,768]{2,1,0:T(8,128)(2,1)S(1)} %hidden.1.refs_0_), channel_id=1, source_target_pairs={{0,16},{8,24},{16,0},{24,8},{1,17},{9,25},{17,1},{25,9},{2,18},{10... | collective-permute-start | bytes 884744 | tf_op jit(solution)/shard_map/ppermute | solution.py:16
  12.6 13.1 %collective-permute-start.5 = (bf16[4,48,768]{2,1,0:T(8,128)(2,1)S(1)}, bf16[4,48,768]{2,1,0:T(8,128)(2,1)S(1)}, u32[]{:S(2)}, u32[]{:S(2)}) collective-permute-start(bf16[4,48,768]{2,1,0:T(8,128)(2,1)S(1)} %hidden.1.refs_0_), channel_id=1, source_target_pairs={{0,8},{8,0},{16,24},{24,16},{1,9},{9,1},{17,25},{25,17},{2,10},{10... | collective-permute-start | bytes 884744 | tf_op jit(solution)/shard_map/ppermute | solution.py:16
  27.3 20.4 %collective-permute-start.8 = (bf16[4,48,1024]{2,1,0:T(8,128)(2,1)S(1)}, bf16[4,48,1024]{2,1,0:T(8,128)(2,1)S(1)}, u32[]{:S(2)}, u32[]{:S(2)}) collective-permute-start(bf16[4,48,1024]{2,1,0:T(8,128)(2,1)S(1)} %get-tuple-element.50), channel_id=1, source_target_pairs={{0,4},{1,5},{2,6},{3,7},{4,0},{5,1},{6,2},{7,3},{8,12},{9,13},{10,... | collective-permute-start | bytes 1179656 | tf_op jit(solution)/shard_map/ppermute | solution.py:16
  28.1 10.0 %collective-permute-start.9 = (bf16[144,1024]{1,0:T(8,128)(2,1)S(1)}, bf16[144,1024]{1,0:T(8,128)(2,1)S(1)}, u32[]{:S(2)}, u32[]{:S(2)}) collective-permute-start(bf16[144,1024]{1,0:T(8,128)(2,1)S(1)} %get-tuple-element.56), channel_id=1, source_target_pairs={{0,8},{8,0},{16,24},{24,16},{1,9},{9,1},{17,25},{25,17},{2,10},{10... | collective-permute-start | bytes 884744 | tf_op jit(solution)/shard_map/ppermute | solution.py:16
  29.6 14.3 %collective-permute-start.10 = (bf16[144,1024]{1,0:T(8,128)(2,1)S(1)}, bf16[144,1024]{1,0:T(8,128)(2,1)S(1)}, u32[]{:S(2)}, u32[]{:S(2)}) collective-permute-start(bf16[144,1024]{1,0:T(8,128)(2,1)S(1)} %get-tuple-element.57), channel_id=1, source_target_pairs={{0,16},{8,24},{16,0},{24,8},{1,17},{9,25},{17,1},{25,9},{2,18},{10... | collective-permute-start | bytes 884744 | tf_op jit(solution)/shard_map/ppermute | solution.py:16
  31.1 12.8 %collective-permute-start.11 = (bf16[144,1024]{1,0:T(8,128)(2,1)S(1)}, bf16[144,1024]{1,0:T(8,128)(2,1)S(1)}, u32[]{:S(2)}, u32[]{:S(2)}) collective-permute-start(bf16[144,1024]{1,0:T(8,128)(2,1)S(1)} %get-tuple-element.58), channel_id=1, source_target_pairs={{0,24},{8,16},{16,8},{24,0},{1,25},{9,17},{17,9},{25,1},{2,26},{10... | collective-permute-start | bytes 884744 | tf_op jit(solution)/shard_map/ppermute | solution.py:16
  34.4 11.0 %collective-permute-start.12 = (f32[1,48]{1,0:T(1,128)S(1)}, f32[1,48]{1,0:T(1,128)S(1)}, u32[]{:S(2)}, u32[]{:S(2)}) collective-permute-start(f32[1,48]{1,0:T(1,128)S(1)} %get-tuple-element.61), channel_id=1, source_target_pairs={{0,2},{1,3},{2,0},{3,1},{4,6},{5,7},{6,4},{7,5},{8,10},{9,11},{10,... | collective-permute-start | bytes 584 | tf_op jit(solution)/shard_map/ppermute | solution.py:16
  38.1 7.4 %collective-permute-start.13 = (f32[1,48]{1,0:T(1,128)S(1)}, f32[1,48]{1,0:T(1,128)S(1)}, u32[]{:S(2)}, u32[]{:S(2)}) collective-permute-start(f32[1,48]{1,0:T(1,128)S(1)} %get-tuple-element.62), channel_id=1, source_target_pairs={{0,6},{1,7},{2,4},{3,5},{4,2},{5,3},{6,0},{7,1},{8,14},{9,15},{10,... | collective-permute-start | bytes 584 | tf_op jit(solution)/shard_map/ppermute | solution.py:16
  47.8 8.2 %collective-permute-start.19 = (bf16[48,1024]{1,0:T(8,128)(2,1)S(1)}, bf16[48,1024]{1,0:T(8,128)(2,1)S(1)}, u32[]{:S(2)}, u32[]{:S(2)}) collective-permute-start(bf16[48,1024]{1,0:T(8,128)(2,1)S(1)} %get-tuple-element.85), channel_id=1, source_target_pairs={{0,24},{8,16},{16,8},{24,0},{1,25},{9,17},{17,9},{25,1},{2,26},{10... | collective-permute-start | bytes 294920 | tf_op jit(solution)/shard_map/ppermute | solution.py:16
  50.3 5.7 %collective-permute-start.18 = (bf16[48,1024]{1,0:T(8,128)(2,1)S(1)}, bf16[48,1024]{1,0:T(8,128)(2,1)S(1)}, u32[]{:S(2)}, u32[]{:S(2)}) collective-permute-start(bf16[48,1024]{1,0:T(8,128)(2,1)S(1)} %get-tuple-element.86), channel_id=1, source_target_pairs={{0,16},{8,24},{16,0},{24,8},{1,17},{9,25},{17,1},{25,9},{2,18},{10... | collective-permute-start | bytes 294920 | tf_op jit(solution)/shard_map/ppermute | solution.py:16
  50.8 5.2 %collective-permute-start.17 = (bf16[48,1024]{1,0:T(8,128)(2,1)S(1)}, bf16[48,1024]{1,0:T(8,128)(2,1)S(1)}, u32[]{:S(2)}, u32[]{:S(2)}) collective-permute-start(bf16[48,1024]{1,0:T(8,128)(2,1)S(1)} %get-tuple-element.87), channel_id=1, source_target_pairs={{0,8},{8,0},{16,24},{24,16},{1,9},{9,1},{17,25},{25,17},{2,10},{10... | collective-permute-start | bytes 294920 | tf_op jit(solution)/shard_map/ppermute | solution.py:16
  51.5 1.7 %collective-permute-start.14 = (f32[1,128]{1,0:T(1,128)S(1)}, f32[1,128]{1,0:T(1,128)S(1)}, u32[]{:S(2)}, u32[]{:S(2)}) collective-permute-start(f32[1,128]{1,0:T(1,128)S(1)} %bitcast.34), channel_id=1, source_target_pairs={{0,1},{1,0},{2,3},{3,2},{4,5},{5,4},{6,7},{7,6},{8,9},{9,8},{10,11... | collective-permute-start | bytes 1544 | tf_op jit(solution)/shard_map/ppermute | solution.py:16
  53.1 4.9 %collective-permute-start.15 = (f32[1,24]{1,0:T(1,128)S(1)}, f32[1,24]{1,0:T(1,128)S(1)}, u32[]{:S(2)}, u32[]{:S(2)}) collective-permute-start(f32[1,24]{1,0:T(1,128)S(1)} %get-tuple-element.70), channel_id=1, source_target_pairs={{0,4},{1,5},{2,6},{3,7},{4,0},{5,1},{6,2},{7,3},{8,12},{9,13},{10,... | collective-permute-start | bytes 296 | tf_op jit(solution)/shard_map/ppermute | solution.py:16
  53.6 4.5 %collective-permute-start.16 = (f32[1,24]{1,0:T(1,128)S(1)}, f32[1,24]{1,0:T(1,128)S(1)}, u32[]{:S(2)}, u32[]{:S(2)}) collective-permute-start(f32[1,24]{1,0:T(1,128)S(1)} %get-tuple-element.71), channel_id=1, source_target_pairs={{0,5},{1,4},{2,7},{3,6},{4,1},{5,0},{6,3},{7,2},{8,13},{9,12},{10,... | collective-permute-start | bytes 296 | tf_op jit(solution)/shard_map/ppermute | solution.py:16

commit v4 on v2

--- a/solution.py
+++ b/solution.py
@@ -288,7 +288,10 @@
         "weight_early",
     )[0]
 
-    rows, grads, total, returned = lax.optimization_barrier((last_rows, grads, total, returned))
+    rows, grads, total, near_returned = lax.optimization_barrier(
+        (last_rows, grads, total, returned[:2])
+    )
+    returned = [*near_returned, *returned[2:]]
     late_rows = [rows[0]] + [swap(rows[j], "rep", j) for j in range(1, replicas)]
     pulled, *routers = kernel_call(
         lambda *refs: pull_last_kernel(last, *refs),

time: 57.7 us -> 57.7 us (level)
  no operation moved by 1% of the time
where the time goes in v4:
time: 57.7 us; the launch traced here: 57.6 us
  starting transfers between devices  23.3 us (40%)
  waiting for transfers between devices  22 us (38%)
  Pallas kernels  9.77 us (17%)
  local copies, waits for them, and re-layouts  1.56 us (3%)
  between operations  0.76 us (1%)
    ppermute x20, starting transfers between devices, swap(): return lax.ppermute(value, axis, [(i, i ^ step) for i in range(n)])  23.3 us
    ppermute x20, waiting for transfers between devices, swap(): return lax.ppermute(value, axis, [(i, i ^ step) for i in range(n)])  22 us
    pallas_call x10, Pallas kernels, kernel_call(): pl.pallas_call(kernel, out_shape=outs, compiler_params=pltpu.CompilerPara...  9.77 us
    unnamed x12, local copies, waits for them, and re-layouts  1.53 us
  transfers between devices with their start and end apart: 20, of which 8 were waited for; matrix products, arithmetic and copies ran while one was open for 0% of the time, Pallas kernels for 15%

profile of v4, /device:TPU:0, one launch (start us, length us, event | category | flops | bytes accessed | tf_op | source)
XLA Modules:
  0.0 57.6 jit_solution(6097003209828117545)
XLA Ops:
  0.6 0.5 collective-permute-start
  1.1 0.1 collective-permute-start.1
  1.2 0.0 slice-start
  1.2 0.0 copy-start.1
  1.2 0.0 copy-start.2
  1.2 0.0 copy-start
  1.2 0.0 slice-start.1
  1.2 0.5 collective-permute-start.2
  1.7 0.0 copy-start.3
  1.7 1.5 %copy-done.3 = bf16[128,4096]{1,0:T(8,128)(2,1)S(1)} copy-done((bf16[128,4096]{1,0:T(8,128)(2,1)S(1)}, bf16[128,4096]{1,0:T(8,128)(2,1)}, u32[]{:S(2)}) %copy-start.3) | copy-done | bytes 1048600
  3.3 0.1 own_rows.1.refs_0_
  3.3 0.3 collective-permute-done.1.refs_3_
  3.6 0.0 collective-permute-done.2.refs_5_
  3.7 0.0 collective-permute-done.refs_1_
  3.7 0.0 copy-done.1
  3.7 0.0 copy-done.2
  3.7 0.7 %place.1 = (bf16[4,48,1024]{2,1,0:T(8,128)(2,1)S(1)}, bf16[4,48,1024]{2,1,0:T(8,128)(2,1)S(1)}, bf16[4,48,1024]{2,1,0:T(8,128)(2,1)S(1)}, bf16[4,48,1024]{2,1,0:...) custom-call(bf16[128,4096]{1,0:T(8,128)(2,1)S(1)} %own_rows.1.refs_0_, ...), custom_call_target="tpu_custom_call" | custom-call | flops 1024 | bytes 1024 | tf_op jit(solution)/shard_map/place/pallas_call | solution.py:22
  4.4 3.0 %collective-permute-start.3 = (bf16[4,48,1024]{2,1,0:T(8,128)(2,1)S(1)}, bf16[4,48,1024]{2,1,0:T(8,128)(2,1)S(1)}, u32[]{:S(2)}, u32[]{:S(2)}) collective-permute-start(bf16[4,48,1024]{2,1,0:T(8,128)(2,1)S(1)} %get-tuple-element.43), channel_id=1, source_target_pairs={{0,2},{1,3},{2,0},{3,1},{4,6},{5,7},{6,4},{7,5},{8,10},{9,11},{10,... | collective-permute-start | bytes 1179656 | tf_op jit(solution)/shard_map/ppermute | solution.py:16
  7.4 2.5 %collective-permute-start.4 = (bf16[4,48,1024]{2,1,0:T(8,128)(2,1)S(1)}, bf16[4,48,1024]{2,1,0:T(8,128)(2,1)S(1)}, u32[]{:S(2)}, u32[]{:S(2)}) collective-permute-start(bf16[4,48,1024]{2,1,0:T(8,128)(2,1)S(1)} %get-tuple-element.44), channel_id=1, source_target_pairs={{0,6},{1,7},{2,4},{3,5},{4,2},{5,3},{6,0},{7,1},{8,14},{9,15},{10,... | collective-permute-start | bytes 1179656 | tf_op jit(solution)/shard_map/ppermute | solution.py:16
  9.9 0.0 copy-done
  9.9 0.2 hidden.1.refs_0_
  10.0 2.5 %collective-permute-start.7 = (bf16[4,48,768]{2,1,0:T(8,128)(2,1)S(1)}, bf16[4,48,768]{2,1,0:T(8,128)(2,1)S(1)}, u32[]{:S(2)}, u32[]{:S(2)}) collective-permute-start(bf16[4,48,768]{2,1,0:T(8,128)(2,1)S(1)} %hidden.1.refs_0_), channel_id=1, source_target_pairs={{0,24},{8,16},{16,8},{24,0},{1,25},{9,17},{17,9},{25,1},{2,26},{10... | collective-permute-start | bytes 884744 | tf_op jit(solution)/shard_map/ppermute | solution.py:16
  12.6 0.5 collective-permute-start.6
  13.1 0.5 collective-permute-start.5
  13.6 7.4 %collective-permute-done.7.refs_3_ = bf16[4,48,768]{2,1,0:T(8,128)(2,1)S(1)} collective-permute-done((bf16[4,48,768]{2,1,0:T(8,128)(2,1)S(1)}, bf16[4,48,768]{2,1,0:T(8,128)(2,1)S(1)}, u32[]{:S(2)}, u32[]{:S(2)}) %collective-permute-start.7) | collective-permute-done | bytes 294944 | tf_op jit(solution)/shard_map/ppermute | solution.py:16
  21.0 4.8 %collective-permute-done.6.refs_2_ = bf16[4,48,768]{2,1,0:T(8,128)(2,1)S(1)} collective-permute-done((bf16[4,48,768]{2,1,0:T(8,128)(2,1)S(1)}, bf16[4,48,768]{2,1,0:T(8,128)(2,1)S(1)}, u32[]{:S(2)}, u32[]{:S(2)}) %collective-permute-start.6) | collective-permute-done | bytes 294944 | tf_op jit(solution)/shard_map/ppermute | solution.py:16
  25.8 0.1 collective-permute-done.5.refs_1_
  25.9 0.1 units.1
  26.0 0.0 collective-permute-done.3.refs_1_
  26.0 1.5 %collective-permute-done.4.refs_2_ = bf16[4,48,1024]{2,1,0:T(8,128)(2,1)S(1)} collective-permute-done((bf16[4,48,1024]{2,1,0:T(8,128)(2,1)S(1)}, bf16[4,48,1024]{2,1,0:T(8,128)(2,1)S(1)}, u32[]{:S(2)}, u32[]{:S(2)}) %collective-permute-start.4) | collective-permute-done | bytes 393248 | tf_op jit(solution)/shard_map/ppermute | solution.py:16
  27.5 1.7 %collective-permute-start.8 = (bf16[4,48,1024]{2,1,0:T(8,128)(2,1)S(1)}, bf16[4,48,1024]{2,1,0:T(8,128)(2,1)S(1)}, u32[]{:S(2)}, u32[]{:S(2)}) collective-permute-start(bf16[4,48,1024]{2,1,0:T(8,128)(2,1)S(1)} %get-tuple-element.49), channel_id=1, source_target_pairs={{0,4},{1,5},{2,6},{3,7},{4,0},{5,1},{6,2},{7,3},{8,12},{9,13},{10,... | collective-permute-start | bytes 1179656 | tf_op jit(solution)/shard_map/ppermute | solution.py:16
  29.3 0.1 stack.1
  29.3 1.6 %collective-permute-start.9 = (bf16[144,1024]{1,0:T(8,128)(2,1)S(1)}, bf16[144,1024]{1,0:T(8,128)(2,1)S(1)}, u32[]{:S(2)}, u32[]{:S(2)}) collective-permute-start(bf16[144,1024]{1,0:T(8,128)(2,1)S(1)} %get-tuple-element.55), channel_id=1, source_target_pairs={{0,8},{8,0},{16,24},{24,16},{1,9},{9,1},{17,25},{25,17},{2,10},{10... | collective-permute-start | bytes 884744 | tf_op jit(solution)/shard_map/ppermute | solution.py:16
  30.9 1.5 %collective-permute-start.10 = (bf16[144,1024]{1,0:T(8,128)(2,1)S(1)}, bf16[144,1024]{1,0:T(8,128)(2,1)S(1)}, u32[]{:S(2)}, u32[]{:S(2)}) collective-permute-start(bf16[144,1024]{1,0:T(8,128)(2,1)S(1)} %get-tuple-element.56), channel_id=1, source_target_pairs={{0,16},{8,24},{16,0},{24,8},{1,17},{9,25},{17,1},{25,9},{2,18},{10... | collective-permute-start | bytes 884744 | tf_op jit(solution)/shard_map/ppermute | solution.py:16
  32.4 0.5 collective-permute-start.11
  32.9 0.0 slice-done
  32.9 0.0 slice-done.1
  32.9 2.8 %pull_early.1 = (bf16[4,48,1536]{2,1,0:T(8,128)(2,1)}, f32[1,48]{1,0:T(1,128)S(1)}, f32[1,48]{1,0:T(1,128)S(1)}, f32[1,48]{1,0:T(1,128)S(1)}) custom-call(bf16[4,48,1024]{2,1,0:T(8,128)(2,1)S(1)} %get-tuple-element.50.refs_0_, bf16[4,48,1024]{2,1,0:T(8,128)(2,1)S(1)} %collective-permute-done.3.refs_1_, ...), custom_call_target="tpu_custom_call" | custom-call | flops 1024 | bytes 1024 | tf_op jit(solution)/shard_map/pull_early/pallas_call | solution.py:22
  35.7 0.3 collective-permute-start.12
  36.0 3.4 %collective-permute-done.9.refs_1_ = bf16[144,1024]{1,0:T(8,128)(2,1)S(1)} collective-permute-done((bf16[144,1024]{1,0:T(8,128)(2,1)S(1)}, bf16[144,1024]{1,0:T(8,128)(2,1)S(1)}, u32[]{:S(2)}, u32[]{:S(2)}) %collective-permute-start.9) | collective-permute-done | bytes 294944 | tf_op jit(solution)/shard_map/ppermute | solution.py:16
  39.4 1.2 %collective-permute-start.13 = (f32[1,48]{1,0:T(1,128)S(1)}, f32[1,48]{1,0:T(1,128)S(1)}, u32[]{:S(2)}, u32[]{:S(2)}) collective-permute-start(f32[1,48]{1,0:T(1,128)S(1)} %get-tuple-element.67), channel_id=1, source_target_pairs={{0,6},{1,7},{2,4},{3,5},{4,2},{5,3},{6,0},{7,1},{8,14},{9,15},{10,... | collective-permute-start | bytes 584 | tf_op jit(solution)/shard_map/ppermute | solution.py:16
  40.5 4.0 %collective-permute-done.10.refs_2_ = bf16[144,1024]{1,0:T(8,128)(2,1)S(1)} collective-permute-done((bf16[144,1024]{1,0:T(8,128)(2,1)S(1)}, bf16[144,1024]{1,0:T(8,128)(2,1)S(1)}, u32[]{:S(2)}, u32[]{:S(2)}) %collective-permute-start.10) | collective-permute-done | bytes 294944 | tf_op jit(solution)/shard_map/ppermute | solution.py:16
  44.6 0.0 collective-permute-done.11.refs_3_
  44.6 1.5 %weight_early.1.refs_5_ = f32[1024,768]{1,0:T(8,128)S(1)} custom-call(bf16[144,1024]{1,0:T(8,128)(2,1)S(1)} %get-tuple-element.54.refs_0_, bf16[144,1024]{1,0:T(8,128)(2,1)S(1)} %collective-permute-done.9.refs_1_, bf16[144,1024]{1,0:T(8,128)(2,1)S(1)} %collective-permute-done.10.refs_2_, bf16[144,1024]{1,0:T(8,128)(2,1)S(1)} %collective-permute-done.11.refs_3_, ...), custom_call_target="tpu_custom_call" | custom-call | flops 1024 | bytes 1024 | tf_op jit(solution)/shard_map/weight_early/pallas_call | solution.py:22
  46.0 0.0 collective-permute-done.12
  46.1 0.4 collective-permute-done.8.refs_0_
  46.5 1.9 %collective-permute-start.19 = (bf16[48,1024]{1,0:T(8,128)(2,1)S(1)}, bf16[48,1024]{1,0:T(8,128)(2,1)S(1)}, u32[]{:S(2)}, u32[]{:S(2)}) collective-permute-start(bf16[48,1024]{1,0:T(8,128)(2,1)S(1)} %get-tuple-element.83), channel_id=1, source_target_pairs={{0,24},{8,16},{16,8},{24,0},{1,25},{9,17},{17,9},{25,1},{2,26},{10... | collective-permute-start | bytes 294920 | tf_op jit(solution)/shard_map/ppermute | solution.py:16
  48.4 1.2 %collective-permute-start.18 = (bf16[48,1024]{1,0:T(8,128)(2,1)S(1)}, bf16[48,1024]{1,0:T(8,128)(2,1)S(1)}, u32[]{:S(2)}, u32[]{:S(2)}) collective-permute-start(bf16[48,1024]{1,0:T(8,128)(2,1)S(1)} %get-tuple-element.84), channel_id=1, source_target_pairs={{0,16},{8,24},{16,0},{24,8},{1,17},{9,25},{17,1},{25,9},{2,18},{10... | collective-permute-start | bytes 294920 | tf_op jit(solution)/shard_map/ppermute | solution.py:16
  49.5 0.5 collective-permute-start.17
  50.1 0.0 collective-permute-done.13
  50.1 0.1 pad_maximum_fusion
  50.2 0.1 select_reduce_fusion
  50.3 0.1 collective-permute-start.14
  50.3 1.6 %pull_last.1 = (f32[48,768]{1,0:T(8,128)S(1)}, f32[1,24]{1,0:T(1,128)S(1)}, f32[1,24]{1,0:T(1,128)S(1)}) custom-call(bf16[4,48,1024]{2,1,0:T(8,128)(2,1)S(1)} %collective-permute-done.8.refs_0_, bf16[1,4096,768]{2,1,0:T(8,128)(2,1)S(1)} %bitcast.21, bf16[4,48,1536]{2,1,0:T(8,128)(2,1)S(1)} %bitcast.24), custom_call_target="tpu_custom_call" | custom-call | flops 1024 | bytes 1024 | tf_op jit(solution)/shard_map/pull_last/pallas_call | solution.py:22
  51.9 0.0 collective-permute-done.14.sib
  51.9 1.1 %collective-permute-start.15 = (f32[1,24]{1,0:T(1,128)S(1)}, f32[1,24]{1,0:T(1,128)S(1)}, u32[]{:S(2)}, u32[]{:S(2)}) collective-permute-start(f32[1,24]{1,0:T(1,128)S(1)} %get-tuple-element.68), channel_id=1, source_target_pairs={{0,4},{1,5},{2,6},{3,7},{4,0},{5,1},{6,2},{7,3},{8,12},{9,13},{10,... | collective-permute-start | bytes 296 | tf_op jit(solution)/shard_map/ppermute | solution.py:16
  53.0 1.7 %collective-permute-start.16 = (f32[1,24]{1,0:T(1,128)S(1)}, f32[1,24]{1,0:T(1,128)S(1)}, u32[]{:S(2)}, u32[]{:S(2)}) collective-permute-start(f32[1,24]{1,0:T(1,128)S(1)} %get-tuple-element.69), channel_id=1, source_target_pairs={{0,5},{1,4},{2,7},{3,6},{4,1},{5,0},{6,3},{7,2},{8,13},{9,12},{10,... | collective-permute-start | bytes 296 | tf_op jit(solution)/shard_map/ppermute | solution.py:16
  54.7 0.0 collective-permute-done.19.refs_3_
  54.7 0.0 collective-permute-done.18.refs_2_
  54.7 0.0 collective-permute-done.17.refs_1_
  54.7 2.1 %finish.1 = (f32[1,1024,768]{2,1,0:T(8,128)}, bf16[4,48,1536]{2,1,0:T(8,128)(2,1)}) custom-call(bf16[48,1024]{1,0:T(8,128)(2,1)S(1)} %get-tuple-element.86.refs_0_, bf16[48,1024]{1,0:T(8,128)(2,1)S(1)} %collective-permute-done.17.refs_1_, bf16[48,1024]{1,0:T(8,128)(2,1)S(1)} %collective-permute-done.18.refs_2_, ...), custom_call_target="tpu_custom_call", output_to_operand_aliasing={{1}: (8, {})} | custom-call | flops 10000000000 | bytes 1024 | tf_op jit(solution)/shard_map/finish/pallas_call | solution.py:22
  56.8 0.0 collective-permute-done.15.same
  56.8 0.0 collective-permute-done.16.other
  56.8 0.7 %token_.1 = f32[1,128]{1,0:T(1,128)} custom-call(f32[1,24]{1,0:T(1,128)S(1)} %collective-permute-done.15.same, f32[1,24]{1,0:T(1,128)S(1)} %collective-permute-done.16.other, s32[1,128]{1,0:T(1,128)S(1)} %get-tuple-element.79.last_slots, f32[1,128]{1,0:T(1,128)S(1)} %bitcast.29, f32[1,128]{1,0:T(1,128)S(1)} %collective-permute-done.14.sib, f32[1,128]{1,0:T(1,128)S(1)} %bitcast.28), custom_call_target="tpu_custom_call" | custom-call | flops 1024 | bytes 1024 | tf_op jit(solution)/shard_map/token/pallas_call | solution.py:22
  (3 shorter events, 0.0 us)
Async XLA Ops:
  0.6 3.0 %collective-permute-start = (bf16[128,4096]{1,0:T(8,128)(2,1)}, bf16[128,4096]{1,0:T(8,128)(2,1)S(1)}, u32[]{:S(2)}, u32[]{:S(2)}) collective-permute-start(bf16[128,4096]{1,0:T(8,128)(2,1)} %rows.1), channel_id=1, source_target_pairs={{0,1},{1,0},{2,3},{3,2},{4,5},{5,4},{6,7},{7,6},{8,9},{9,8},{10,11... | collective-permute-start | bytes 3145736 | tf_op jit(solution)/shard_map/ppermute | solution.py:16
  1.1 2.5 %collective-permute-start.1 = (s32[1,128]{1,0:T(1,128)}, s32[1,128]{1,0:T(1,128)S(1)}, u32[]{:S(2)}, u32[]{:S(2)}) collective-permute-start(s32[1,128]{1,0:T(1,128)} %bitcast.30), channel_id=1, source_target_pairs={{0,1},{1,0},{2,3},{3,2},{4,5},{5,4},{6,7},{7,6},{8,9},{9,8},{10,11... | collective-permute-start | bytes 1544 | tf_op jit(solution)/shard_map/ppermute | solution.py:16
  1.2 31.7 %slice-start = ((s8[6291456]{0:T(1024)(128)(4,1)}), s8[4194304]{0:T(1024)(128)(4,1)S(1)}, s32[]{:S(2)}) async-start(s8[6291456]{0:T(1024)(128)(4,1)} %bitcast.20), calls=%async_computation | async-start | bytes 8388608
  1.2 2.4 %copy-start.1 = (f32[128,1]{0,1:T(1,128)S(1)}, f32[128,1]{0,1:T(1,128)}, u32[]{:S(2)}) copy-start(f32[128,1]{0,1:T(1,128)} %param.7) | copy-start | bytes 1540
  1.2 2.4 %copy-start.2 = (s32[128,1]{0,1:T(1,128)S(1)}, s32[128,1]{0,1:T(1,128)}, u32[]{:S(2)}) copy-start(s32[128,1]{0,1:T(1,128)} %param.6) | copy-start | bytes 1540
  1.2 8.6 %copy-start = (bf16[1,1,192,1536]{3,2,1,0:T(8,128)(2,1)S(1)}, bf16[1,1,192,1536]{3,2,1,0:T(8,128)(2,1)}, u32[]{:S(2)}) copy-start(bf16[1,1,192,1536]{3,2,1,0:T(8,128)(2,1)} %param.9) | copy-start | bytes 1769476
  1.2 31.7 %slice-start.1 = ((s8[6291456]{0:T(1024)(128)(4,1)}), s8[2097152]{0:T(1024)(128)(4,1)S(1)}, s32[]{:S(2)}) async-start(s8[6291456]{0:T(1024)(128)(4,1)} %bitcast.20), calls=%async_computation.1 | async-start | bytes 4194304
  1.2 2.4 %collective-permute-start.2 = (f32[1,128]{1,0:T(1,128)}, f32[1,128]{1,0:T(1,128)S(1)}, u32[]{:S(2)}, u32[]{:S(2)}) collective-permute-start(f32[1,128]{1,0:T(1,128)} %bitcast.26), channel_id=1, source_target_pairs={{0,1},{1,0},{2,3},{3,2},{4,5},{5,4},{6,7},{7,6},{8,9},{9,8},{10,11... | collective-permute-start | bytes 1544 | tf_op jit(solution)/shard_map/ppermute | solution.py:16
  1.7 1.5 %copy-start.3 = (bf16[128,4096]{1,0:T(8,128)(2,1)S(1)}, bf16[128,4096]{1,0:T(8,128)(2,1)}, u32[]{:S(2)}) copy-start(bf16[128,4096]{1,0:T(8,128)(2,1)} %rows.1) | copy-start | bytes 3145732
  4.4 21.6 %collective-permute-start.3 = (bf16[4,48,1024]{2,1,0:T(8,128)(2,1)S(1)}, bf16[4,48,1024]{2,1,0:T(8,128)(2,1)S(1)}, u32[]{:S(2)}, u32[]{:S(2)}) collective-permute-start(bf16[4,48,1024]{2,1,0:T(8,128)(2,1)S(1)} %get-tuple-element.43), channel_id=1, source_target_pairs={{0,2},{1,3},{2,0},{3,1},{4,6},{5,7},{6,4},{7,5},{8,10},{9,11},{10,... | collective-permute-start | bytes 1179656 | tf_op jit(solution)/shard_map/ppermute | solution.py:16
  7.4 20.1 %collective-permute-start.4 = (bf16[4,48,1024]{2,1,0:T(8,128)(2,1)S(1)}, bf16[4,48,1024]{2,1,0:T(8,128)(2,1)S(1)}, u32[]{:S(2)}, u32[]{:S(2)}) collective-permute-start(bf16[4,48,1024]{2,1,0:T(8,128)(2,1)S(1)} %get-tuple-element.44), channel_id=1, source_target_pairs={{0,6},{1,7},{2,4},{3,5},{4,2},{5,3},{6,0},{7,1},{8,14},{9,15},{10,... | collective-permute-start | bytes 1179656 | tf_op jit(solution)/shard_map/ppermute | solution.py:16
  10.0 10.9 %collective-permute-start.7 = (bf16[4,48,768]{2,1,0:T(8,128)(2,1)S(1)}, bf16[4,48,768]{2,1,0:T(8,128)(2,1)S(1)}, u32[]{:S(2)}, u32[]{:S(2)}) collective-permute-start(bf16[4,48,768]{2,1,0:T(8,128)(2,1)S(1)} %hidden.1.refs_0_), channel_id=1, source_target_pairs={{0,24},{8,16},{16,8},{24,0},{1,25},{9,17},{17,9},{25,1},{2,26},{10... | collective-permute-start | bytes 884744 | tf_op jit(solution)/shard_map/ppermute | solution.py:16
  12.6 13.3 %collective-permute-start.6 = (bf16[4,48,768]{2,1,0:T(8,128)(2,1)S(1)}, bf16[4,48,768]{2,1,0:T(8,128)(2,1)S(1)}, u32[]{:S(2)}, u32[]{:S(2)}) collective-permute-start(bf16[4,48,768]{2,1,0:T(8,128)(2,1)S(1)} %hidden.1.refs_0_), channel_id=1, source_target_pairs={{0,16},{8,24},{16,0},{24,8},{1,17},{9,25},{17,1},{25,9},{2,18},{10... | collective-permute-start | bytes 884744 | tf_op jit(solution)/shard_map/ppermute | solution.py:16
  13.1 12.9 %collective-permute-start.5 = (bf16[4,48,768]{2,1,0:T(8,128)(2,1)S(1)}, bf16[4,48,768]{2,1,0:T(8,128)(2,1)S(1)}, u32[]{:S(2)}, u32[]{:S(2)}) collective-permute-start(bf16[4,48,768]{2,1,0:T(8,128)(2,1)S(1)} %hidden.1.refs_0_), channel_id=1, source_target_pairs={{0,8},{8,0},{16,24},{24,16},{1,9},{9,1},{17,25},{25,17},{2,10},{10... | collective-permute-start | bytes 884744 | tf_op jit(solution)/shard_map/ppermute | solution.py:16
  27.5 19.0 %collective-permute-start.8 = (bf16[4,48,1024]{2,1,0:T(8,128)(2,1)S(1)}, bf16[4,48,1024]{2,1,0:T(8,128)(2,1)S(1)}, u32[]{:S(2)}, u32[]{:S(2)}) collective-permute-start(bf16[4,48,1024]{2,1,0:T(8,128)(2,1)S(1)} %get-tuple-element.49), channel_id=1, source_target_pairs={{0,4},{1,5},{2,6},{3,7},{4,0},{5,1},{6,2},{7,3},{8,12},{9,13},{10,... | collective-permute-start | bytes 1179656 | tf_op jit(solution)/shard_map/ppermute | solution.py:16
  29.3 10.0 %collective-permute-start.9 = (bf16[144,1024]{1,0:T(8,128)(2,1)S(1)}, bf16[144,1024]{1,0:T(8,128)(2,1)S(1)}, u32[]{:S(2)}, u32[]{:S(2)}) collective-permute-start(bf16[144,1024]{1,0:T(8,128)(2,1)S(1)} %get-tuple-element.55), channel_id=1, source_target_pairs={{0,8},{8,0},{16,24},{24,16},{1,9},{9,1},{17,25},{25,17},{2,10},{10... | collective-permute-start | bytes 884744 | tf_op jit(solution)/shard_map/ppermute | solution.py:16
  30.9 13.6 %collective-permute-start.10 = (bf16[144,1024]{1,0:T(8,128)(2,1)S(1)}, bf16[144,1024]{1,0:T(8,128)(2,1)S(1)}, u32[]{:S(2)}, u32[]{:S(2)}) collective-permute-start(bf16[144,1024]{1,0:T(8,128)(2,1)S(1)} %get-tuple-element.56), channel_id=1, source_target_pairs={{0,16},{8,24},{16,0},{24,8},{1,17},{9,25},{17,1},{25,9},{2,18},{10... | collective-permute-start | bytes 884744 | tf_op jit(solution)/shard_map/ppermute | solution.py:16
  32.4 12.1 %collective-permute-start.11 = (bf16[144,1024]{1,0:T(8,128)(2,1)S(1)}, bf16[144,1024]{1,0:T(8,128)(2,1)S(1)}, u32[]{:S(2)}, u32[]{:S(2)}) collective-permute-start(bf16[144,1024]{1,0:T(8,128)(2,1)S(1)} %get-tuple-element.57), channel_id=1, source_target_pairs={{0,24},{8,16},{16,8},{24,0},{1,25},{9,17},{17,9},{25,1},{2,26},{10... | collective-permute-start | bytes 884744 | tf_op jit(solution)/shard_map/ppermute | solution.py:16
  35.7 10.4 %collective-permute-start.12 = (f32[1,48]{1,0:T(1,128)S(1)}, f32[1,48]{1,0:T(1,128)S(1)}, u32[]{:S(2)}, u32[]{:S(2)}) collective-permute-start(f32[1,48]{1,0:T(1,128)S(1)} %get-tuple-element.60), channel_id=1, source_target_pairs={{0,2},{1,3},{2,0},{3,1},{4,6},{5,7},{6,4},{7,5},{8,10},{9,11},{10,... | collective-permute-start | bytes 584 | tf_op jit(solution)/shard_map/ppermute | solution.py:16
  39.4 10.7 %collective-permute-start.13 = (f32[1,48]{1,0:T(1,128)S(1)}, f32[1,48]{1,0:T(1,128)S(1)}, u32[]{:S(2)}, u32[]{:S(2)}) collective-permute-start(f32[1,48]{1,0:T(1,128)S(1)} %get-tuple-element.67), channel_id=1, source_target_pairs={{0,6},{1,7},{2,4},{3,5},{4,2},{5,3},{6,0},{7,1},{8,14},{9,15},{10,... | collective-permute-start | bytes 584 | tf_op jit(solution)/shard_map/ppermute | solution.py:16
  46.5 8.2 %collective-permute-start.19 = (bf16[48,1024]{1,0:T(8,128)(2,1)S(1)}, bf16[48,1024]{1,0:T(8,128)(2,1)S(1)}, u32[]{:S(2)}, u32[]{:S(2)}) collective-permute-start(bf16[48,1024]{1,0:T(8,128)(2,1)S(1)} %get-tuple-element.83), channel_id=1, source_target_pairs={{0,24},{8,16},{16,8},{24,0},{1,25},{9,17},{17,9},{25,1},{2,26},{10... | collective-permute-start | bytes 294920 | tf_op jit(solution)/shard_map/ppermute | solution.py:16
  48.4 6.3 %collective-permute-start.18 = (bf16[48,1024]{1,0:T(8,128)(2,1)S(1)}, bf16[48,1024]{1,0:T(8,128)(2,1)S(1)}, u32[]{:S(2)}, u32[]{:S(2)}) collective-permute-start(bf16[48,1024]{1,0:T(8,128)(2,1)S(1)} %get-tuple-element.84), channel_id=1, source_target_pairs={{0,16},{8,24},{16,0},{24,8},{1,17},{9,25},{17,1},{25,9},{2,18},{10... | collective-permute-start | bytes 294920 | tf_op jit(solution)/shard_map/ppermute | solution.py:16
  49.5 5.2 %collective-permute-start.17 = (bf16[48,1024]{1,0:T(8,128)(2,1)S(1)}, bf16[48,1024]{1,0:T(8,128)(2,1)S(1)}, u32[]{:S(2)}, u32[]{:S(2)}) collective-permute-start(bf16[48,1024]{1,0:T(8,128)(2,1)S(1)} %get-tuple-element.85), channel_id=1, source_target_pairs={{0,8},{8,0},{16,24},{24,16},{1,9},{9,1},{17,25},{25,17},{2,10},{10... | collective-permute-start | bytes 294920 | tf_op jit(solution)/shard_map/ppermute | solution.py:16
  50.3 1.7 %collective-permute-start.14 = (f32[1,128]{1,0:T(1,128)S(1)}, f32[1,128]{1,0:T(1,128)S(1)}, u32[]{:S(2)}, u32[]{:S(2)}) collective-permute-start(f32[1,128]{1,0:T(1,128)S(1)} %bitcast.34), channel_id=1, source_target_pairs={{0,1},{1,0},{2,3},{3,2},{4,5},{5,4},{6,7},{7,6},{8,9},{9,8},{10,11... | collective-permute-start | bytes 1544 | tf_op jit(solution)/shard_map/ppermute | solution.py:16
  51.9 4.9 %collective-permute-start.15 = (f32[1,24]{1,0:T(1,128)S(1)}, f32[1,24]{1,0:T(1,128)S(1)}, u32[]{:S(2)}, u32[]{:S(2)}) collective-permute-start(f32[1,24]{1,0:T(1,128)S(1)} %get-tuple-element.68), channel_id=1, source_target_pairs={{0,4},{1,5},{2,6},{3,7},{4,0},{5,1},{6,2},{7,3},{8,12},{9,13},{10,... | collective-permute-start | bytes 296 | tf_op jit(solution)/shard_map/ppermute | solution.py:16
  53.0 3.9 %collective-permute-start.16 = (f32[1,24]{1,0:T(1,128)S(1)}, f32[1,24]{1,0:T(1,128)S(1)}, u32[]{:S(2)}, u32[]{:S(2)}) collective-permute-start(f32[1,24]{1,0:T(1,128)S(1)} %get-tuple-element.69), channel_id=1, source_target_pairs={{0,5},{1,4},{2,7},{3,6},{4,1},{5,0},{6,3},{7,2},{8,13},{9,12},{10,... | collective-permute-start | bytes 296 | tf_op jit(solution)/shard_map/ppermute | solution.py:16

commit v5 on v2

--- a/solution.py
+++ b/solution.py
@@ -39,43 +39,51 @@
         hidden[k] = (gate * sigmoid * up).astype(jnp.bfloat16)
 
 
-def place_kernel(cap, order, cot, cot_sib, routes, routes_sib, weights, weights_sib, *outs):
-    chips = len(order)
-    blocks, slots_out, last_out = outs[:chips], outs[chips], outs[chips + 1]
-    me, mine = lax.axis_index("exp"), lax.axis_index("rep")
+def placement_of(cap, order, own, ids, gains):
+    me = lax.axis_index("exp")
     chip, core = me // 2, lax.rem(me, 2)
-    replicas, pair, share = blocks[0].shape
-    tokens = cot.shape[0]
+    source = core if own else 1 - core
+    chips, pair, tokens = len(order), 2 * cap, ids.shape[1]
     before = (
         lax.broadcasted_iota(jnp.int32, (tokens, tokens), 0)
         < lax.broadcasted_iota(jnp.int32, (tokens, tokens), 1)
     ).astype(jnp.bfloat16)
-    placements = []
-    for i, (ids, gains) in enumerate(((routes, weights), (routes_sib, weights_sib))):
-        expert = ids[...]
-        weight = gains[...].astype(jnp.bfloat16).astype(jnp.float32)
-        hot = lax.broadcasted_iota(jnp.int32, (2 * chips, tokens), 0) == expert
-        earlier = jnp.dot(hot.astype(jnp.bfloat16), before, preferred_element_type=jnp.float32)
-        position = jnp.sum(jnp.where(hot, earlier, 0.0), axis=0, keepdims=True).astype(jnp.int32)
-        source = core if i == 0 else 1 - core
-        step = (expert >> 1) ^ chip
-        same = (expert & 1) == core
-        rank = sum(jnp.where(step == k, i, 0) for i, k in enumerate(order))
-        slot = jnp.where(same, rank * pair + source * cap + position, -1)
-        slots_out[i : i + 1, :] = slot
-        if i == 0:
-            last_out[...] = jnp.where(
-                step == order[-1], jnp.where(same, position, cap + position), -1
-            )
-        here = lax.broadcasted_iota(jnp.int32, (chips * pair, tokens), 0) == slot
-        placements.append(jnp.where(here, weight, 0.0).astype(jnp.bfloat16))
-    placement = jnp.concatenate(placements, axis=1)
+    expert = ids[...]
+    weight = gains[...].astype(jnp.bfloat16).astype(jnp.float32)
+    hot = lax.broadcasted_iota(jnp.int32, (2 * chips, tokens), 0) == expert
+    earlier = jnp.dot(hot.astype(jnp.bfloat16), before, preferred_element_type=jnp.float32)
+    position = jnp.sum(jnp.where(hot, earlier, 0.0), axis=0, keepdims=True).astype(jnp.int32)
+    step = (expert >> 1) ^ chip
+    same = (expert & 1) == core
+    rank = sum(jnp.where(step == k, i, 0) for i, k in enumerate(order))
+    slot = jnp.where(same, rank * pair + source * cap + position, -1)
+    last_slot = jnp.where(step == order[-1], jnp.where(same, position, cap + position), -1)
+    here = lax.broadcasted_iota(jnp.int32, (chips * pair, tokens), 0) == slot
+    return slot, last_slot, jnp.where(here, weight, 0.0).astype(jnp.bfloat16)
+
+
+def place_own_kernel(cap, order, cot, ids, gains, placed, slots, last_slots):
+    mine = lax.axis_index("rep")
+    replicas, _, share = placed.shape
+    slots[...], last_slots[...], placement = placement_of(cap, order, True, ids, gains)
     for j in range(replicas):
         columns = pl.ds(pl.multiple_of((mine ^ j) * share, share), share)
-        rows = jnp.concatenate([cot[:, columns], cot_sib[:, columns]], axis=0)
-        sent = jnp.dot(placement, rows, preferred_element_type=jnp.float32).astype(jnp.bfloat16)
-        for k in range(chips):
-            blocks[k][j] = sent[k * pair : (k + 1) * pair]
+        placed[j] = jnp.dot(
+            placement, cot[:, columns], preferred_element_type=jnp.float32
+        ).astype(jnp.bfloat16)
+
+
+def place_sib_kernel(cap, order, placed, cot, ids, gains, *outs):
+    mine = lax.axis_index("rep")
+    blocks, slots = outs[:-1], outs[-1]
+    replicas, pair, share = blocks[0].shape
+    slots[...], _, placement = placement_of(cap, order, False, ids, gains)
+    for j in range(replicas):
+        columns = pl.ds(pl.multiple_of((mine ^ j) * share, share), share)
+        sent = jnp.dot(placement, cot[:, columns], preferred_element_type=jnp.float32)
+        sent = (sent + placed[j].astype(jnp.float32)).astype(jnp.bfloat16)
+        for i, block in enumerate(blocks):
+            block[j] = sent[i * pair : (i + 1) * pair]
 
 
 def products(arrived, down):
@@ -232,15 +240,18 @@
         "own_rows",
         LARGE,
     )[0]
-    *blocks, slots, last_slots = kernel_call(
-        lambda *refs: place_kernel(cap, order, *refs),
-        [jax.ShapeDtypeStruct((replicas, pair, share), jnp.bfloat16)] * chips
-        + [
-            jax.ShapeDtypeStruct((2, tokens), jnp.int32),
-            jax.ShapeDtypeStruct((1, tokens), jnp.int32),
-        ],
-        [own_rows, cot_sib, routes, routes_sib, weights, weights_sib],
-        "place",
+    slot_shape = jax.ShapeDtypeStruct((1, tokens), jnp.int32)
+    placed, slots, last_slots = kernel_call(
+        lambda *refs: place_own_kernel(cap, order, *refs),
+        [jax.ShapeDtypeStruct((replicas, chips * pair, share), jnp.bfloat16), slot_shape, slot_shape],
+        [own_rows, routes, weights],
+        "place_own",
+    )
+    *blocks, slots_sib = kernel_call(
+        lambda *refs: place_sib_kernel(cap, order, *refs),
+        [jax.ShapeDtypeStruct((replicas, pair, share), jnp.bfloat16)] * chips + [slot_shape],
+        [placed, cot_sib, routes_sib, weights_sib],
+        "place_sib",
     )
 
     blocks = dict(zip(order, blocks))
@@ -248,7 +259,7 @@
     for k in reversed(early[1:]):
         arrived[k] = swap(blocks[k], "exp", 2 * k)
     saved = saved_pre.reshape(chips, pair, 2 * width)
-    saved, slots = lax.optimization_barrier((saved, slots))
+    saved, slots_sib = lax.optimization_barrier((saved, slots_sib))
     hidden = kernel_call(
         hidden_kernel,
         [jax.ShapeDtypeStruct((chips, pair, width), jnp.bfloat16)],
@@ -288,7 +299,10 @@
         "weight_early",
     )[0]
 
-    rows, grads, total, returned = lax.optimization_barrier((last_rows, grads, total, returned))
+    rows, grads, total, returned = lax.optimization_barrier(
+        (last_rows, grads, total, returned[::-1])
+    )
+    returned = returned[::-1]
     late_rows = [rows[0]] + [swap(rows[j], "rep", j) for j in range(1, replicas)]
     pulled, *routers = kernel_call(
         lambda *refs: pull_last_kernel(last, *refs),
@@ -301,7 +315,7 @@
     slot_index = lax.broadcasted_iota(jnp.int32, (len(early) * pair, 1), 0)
     sums = [
         jnp.sum(jnp.where(slot_index == ids, returned, 0.0), axis=0, keepdims=True)
-        for ids in (slots[0:1], slots[1:2])
+        for ids in (slots, slots_sib)
     ]
     sum_sib = swap(sums[1], "exp", 1)
     routers, sum_sib = lax.optimization_barrier((routers, sum_sib))

time: 57.7 us -> 58.6 us (1.016)
  waiting for transfers between devices: 22 us -> 22.7 us
  Pallas kernels: 9.76 us -> 10.4 us
    pallas_call x10 -> x11, Pallas kernels: 9.76 us -> 10.4 us  [kernel_call(): pl.pallas_call(kernel, out_shape=outs, compiler_params=pltpu.CompilerPara...]
    ppermute x20, waiting for transfers between devices: 22 us -> 22.7 us  [swap(): return lax.ppermute(value, axis, [(i, i ^ step) for i in range(n)])]
  transfers between devices with their start and end apart: 20 -> 20, of which waited for: 8 -> 7; matrix products, arithmetic and copies ran while one was open for 0% -> 0% of each run, Pallas kernels for 15% -> 15%
where the time goes in v5:
time: 58.6 us; the launch traced here: 58.5 us
  starting transfers between devices  22.9 us (39%)
  waiting for transfers between devices  22.7 us (39%)
  Pallas kernels  10.4 us (18%)
  local copies, waits for them, and re-layouts  1.55 us (3%)
  between operations  0.8 us (1%)
    ppermute x20, starting transfers between devices, swap(): return lax.ppermute(value, axis, [(i, i ^ step) for i in range(n)])  22.9 us
    ppermute x20, waiting for transfers between devices, swap(): return lax.ppermute(value, axis, [(i, i ^ step) for i in range(n)])  22.7 us
    pallas_call x11, Pallas kernels, kernel_call(): pl.pallas_call(kernel, out_shape=outs, compiler_params=pltpu.CompilerPara...  10.4 us
    unnamed x12, local copies, waits for them, and re-layouts  1.52 us
  transfers between devices with their start and end apart: 20, of which 7 were waited for; matrix products, arithmetic and copies ran while one was open for 0% of the time, Pallas kernels for 15%

profile of v5, /device:TPU:0, one launch (start us, length us, event | category | flops | bytes accessed | tf_op | source)
XLA Modules:
  0.0 58.5 jit_solution(8841789049247887314)
XLA Ops:
  0.6 0.5 collective-permute-start
  1.1 0.1 collective-permute-start.1
  1.2 0.0 copy-start.1
  1.2 0.0 copy-start.2
  1.2 0.0 slice-start.1
  1.2 0.5 collective-permute-start.2
  1.7 0.0 copy-start.3
  1.7 1.5 %copy-done.3 = bf16[128,4096]{1,0:T(8,128)(2,1)S(1)} copy-done((bf16[128,4096]{1,0:T(8,128)(2,1)S(1)}, bf16[128,4096]{1,0:T(8,128)(2,1)}, u32[]{:S(2)}) %copy-start.3) | copy-done | bytes 1048600
  3.2 0.1 own_rows.1.refs_0_
  3.3 0.0 copy-done.1
  3.3 0.0 copy-done.2
  3.3 0.0 copy-start
  3.3 0.7 %place_own.1 = (bf16[4,192,1024]{2,1,0:T(8,128)(2,1)S(1)}, s32[1,128]{1,0:T(1,128)S(1)}, s32[1,128]{1,0:T(1,128)S(1)}) custom-call(bf16[128,4096]{1,0:T(8,128)(2,1)S(1)} %own_rows.1.refs_0_, s32[1,128]{1,0:T(1,128)S(1)} %bitcast.29, f32[1,128]{1,0:T(1,128)S(1)} %bitcast.25), custom_call_target="tpu_custom_call" | custom-call | flops 1024 | bytes 1024 | tf_op jit(solution)/shard_map/place_own/pallas_call | solution.py:22
  4.0 0.0 collective-permute-done.1.refs_2_
  4.0 0.0 collective-permute-done.2.refs_3_
  4.1 0.0 collective-permute-done.refs_1_
  4.1 0.7 %place_sib.1 = (bf16[4,48,1024]{2,1,0:T(8,128)(2,1)S(1)}, bf16[4,48,1024]{2,1,0:T(8,128)(2,1)S(1)}, bf16[4,48,1024]{2,1,0:T(8,128)(2,1)S(1)}, bf16[4,48,1024]{2,1,0:T(8,128)(2,1)S(1)}, s32[1,128]{1,0:T(1,128)S(1)}) custom-call(bf16[4,192,1024]{2,1,0:T(8,128)(2,1)S(1)} %get-tuple-element.45.refs_0_, bf16[128,4096]{1,0:T(8,128)(2,1)S(1)} %collective-permute-done.refs_1_, ...), custom_call_target="tpu_custom_call" | custom-call | flops 1024 | bytes 1024 | tf_op jit(solution)/shard_map/place_sib/pallas_call | solution.py:22
  4.8 2.6 %collective-permute-start.3 = (bf16[4,48,1024]{2,1,0:T(8,128)(2,1)S(1)}, bf16[4,48,1024]{2,1,0:T(8,128)(2,1)S(1)}, u32[]{:S(2)}, u32[]{:S(2)}) collective-permute-start(bf16[4,48,1024]{2,1,0:T(8,128)(2,1)S(1)} %get-tuple-element.47), channel_id=1, source_target_pairs={{0,2},{1,3},{2,0},{3,1},{4,6},{5,7},{6,4},{7,5},{8,10},{9,11},{10,... | collective-permute-start | bytes 1179656 | tf_op jit(solution)/shard_map/ppermute | solution.py:16
  7.4 2.5 %collective-permute-start.4 = (bf16[4,48,1024]{2,1,0:T(8,128)(2,1)S(1)}, bf16[4,48,1024]{2,1,0:T(8,128)(2,1)S(1)}, u32[]{:S(2)}, u32[]{:S(2)}) collective-permute-start(bf16[4,48,1024]{2,1,0:T(8,128)(2,1)S(1)} %get-tuple-element.48), channel_id=1, source_target_pairs={{0,6},{1,7},{2,4},{3,5},{4,2},{5,3},{6,0},{7,1},{8,14},{9,15},{10,... | collective-permute-start | bytes 1179656 | tf_op jit(solution)/shard_map/ppermute | solution.py:16
  9.8 0.0 copy-done
  9.8 0.2 hidden.1.refs_0_
  10.0 2.5 %collective-permute-start.7 = (bf16[4,48,768]{2,1,0:T(8,128)(2,1)S(1)}, bf16[4,48,768]{2,1,0:T(8,128)(2,1)S(1)}, u32[]{:S(2)}, u32[]{:S(2)}) collective-permute-start(bf16[4,48,768]{2,1,0:T(8,128)(2,1)S(1)} %hidden.1.refs_0_), channel_id=1, source_target_pairs={{0,24},{8,16},{16,8},{24,0},{1,25},{9,17},{17,9},{25,1},{2,26},{10... | collective-permute-start | bytes 884744 | tf_op jit(solution)/shard_map/ppermute | solution.py:16
  12.6 0.5 collective-permute-start.6
  13.1 0.5 collective-permute-start.5
  13.6 7.3 %collective-permute-done.7.refs_3_ = bf16[4,48,768]{2,1,0:T(8,128)(2,1)S(1)} collective-permute-done((bf16[4,48,768]{2,1,0:T(8,128)(2,1)S(1)}, bf16[4,48,768]{2,1,0:T(8,128)(2,1)S(1)}, u32[]{:S(2)}, u32[]{:S(2)}) %collective-permute-start.7) | collective-permute-done | bytes 294944 | tf_op jit(solution)/shard_map/ppermute | solution.py:16
  20.9 5.3 %collective-permute-done.6.refs_2_ = bf16[4,48,768]{2,1,0:T(8,128)(2,1)S(1)} collective-permute-done((bf16[4,48,768]{2,1,0:T(8,128)(2,1)S(1)}, bf16[4,48,768]{2,1,0:T(8,128)(2,1)S(1)}, u32[]{:S(2)}, u32[]{:S(2)}) %collective-permute-start.6) | collective-permute-done | bytes 294944 | tf_op jit(solution)/shard_map/ppermute | solution.py:16
  26.2 0.1 collective-permute-done.5.refs_1_
  26.3 0.1 units.1
  26.4 0.0 collective-permute-done.3.refs_1_
  26.4 1.5 %collective-permute-done.4.refs_2_ = bf16[4,48,1024]{2,1,0:T(8,128)(2,1)S(1)} collective-permute-done((bf16[4,48,1024]{2,1,0:T(8,128)(2,1)S(1)}, bf16[4,48,1024]{2,1,0:T(8,128)(2,1)S(1)}, u32[]{:S(2)}, u32[]{:S(2)}) %collective-permute-start.4) | collective-permute-done | bytes 393248 | tf_op jit(solution)/shard_map/ppermute | solution.py:16
  27.9 1.8 %collective-permute-start.8 = (bf16[4,48,1024]{2,1,0:T(8,128)(2,1)S(1)}, bf16[4,48,1024]{2,1,0:T(8,128)(2,1)S(1)}, u32[]{:S(2)}, u32[]{:S(2)}) collective-permute-start(bf16[4,48,1024]{2,1,0:T(8,128)(2,1)S(1)} %get-tuple-element.53), channel_id=1, source_target_pairs={{0,4},{1,5},{2,6},{3,7},{4,0},{5,1},{6,2},{7,3},{8,12},{9,13},{10,... | collective-permute-start | bytes 1179656 | tf_op jit(solution)/shard_map/ppermute | solution.py:16
  29.7 0.1 stack.1
  29.7 1.6 %collective-permute-start.9 = (bf16[144,1024]{1,0:T(8,128)(2,1)S(1)}, bf16[144,1024]{1,0:T(8,128)(2,1)S(1)}, u32[]{:S(2)}, u32[]{:S(2)}) collective-permute-start(bf16[144,1024]{1,0:T(8,128)(2,1)S(1)} %get-tuple-element.59), channel_id=1, source_target_pairs={{0,8},{8,0},{16,24},{24,16},{1,9},{9,1},{17,25},{25,17},{2,10},{10... | collective-permute-start | bytes 884744 | tf_op jit(solution)/shard_map/ppermute | solution.py:16
  31.3 1.5 %collective-permute-start.10 = (bf16[144,1024]{1,0:T(8,128)(2,1)S(1)}, bf16[144,1024]{1,0:T(8,128)(2,1)S(1)}, u32[]{:S(2)}, u32[]{:S(2)}) collective-permute-start(bf16[144,1024]{1,0:T(8,128)(2,1)S(1)} %get-tuple-element.60), channel_id=1, source_target_pairs={{0,16},{8,24},{16,0},{24,8},{1,17},{9,25},{17,1},{25,9},{2,18},{10... | collective-permute-start | bytes 884744 | tf_op jit(solution)/shard_map/ppermute | solution.py:16
  32.8 0.5 collective-permute-start.11
  33.3 0.0 slice-done
  33.3 0.0 slice-done.1
  33.3 2.7 %pull_early.1 = (bf16[4,48,1536]{2,1,0:T(8,128)(2,1)}, f32[1,48]{1,0:T(1,128)S(1)}, f32[1,48]{1,0:T(1,128)S(1)}, f32[1,48]{1,0:T(1,128)S(1)}) custom-call(bf16[4,48,1024]{2,1,0:T(8,128)(2,1)S(1)} %get-tuple-element.54.refs_0_, bf16[4,48,1024]{2,1,0:T(8,128)(2,1)S(1)} %collective-permute-done.3.refs_1_, ...), custom_call_target="tpu_custom_call" | custom-call | flops 1024 | bytes 1024 | tf_op jit(solution)/shard_map/pull_early/pallas_call | solution.py:22
  36.1 1.2 %collective-permute-start.12 = (f32[1,48]{1,0:T(1,128)S(1)}, f32[1,48]{1,0:T(1,128)S(1)}, u32[]{:S(2)}, u32[]{:S(2)}) collective-permute-start(f32[1,48]{1,0:T(1,128)S(1)} %get-tuple-element.63), channel_id=1, source_target_pairs={{0,6},{1,7},{2,4},{3,5},{4,2},{5,3},{6,0},{7,1},{8,14},{9,15},{10,... | collective-permute-start | bytes 584 | tf_op jit(solution)/shard_map/ppermute | solution.py:16
  37.2 2.5 %collective-permute-done.9.refs_1_ = bf16[144,1024]{1,0:T(8,128)(2,1)S(1)} collective-permute-done((bf16[144,1024]{1,0:T(8,128)(2,1)S(1)}, bf16[144,1024]{1,0:T(8,128)(2,1)S(1)}, u32[]{:S(2)}, u32[]{:S(2)}) %collective-permute-start.9) | collective-permute-done | bytes 294944 | tf_op jit(solution)/shard_map/ppermute | solution.py:16
  39.8 0.3 collective-permute-start.13
  40.0 5.4 %collective-permute-done.10.refs_2_ = bf16[144,1024]{1,0:T(8,128)(2,1)S(1)} collective-permute-done((bf16[144,1024]{1,0:T(8,128)(2,1)S(1)}, bf16[144,1024]{1,0:T(8,128)(2,1)S(1)}, u32[]{:S(2)}, u32[]{:S(2)}) %collective-permute-start.10) | collective-permute-done | bytes 294944 | tf_op jit(solution)/shard_map/ppermute | solution.py:16
  45.5 0.0 collective-permute-done.11.refs_3_
  45.5 1.5 %weight_early.1.refs_5_ = f32[1024,768]{1,0:T(8,128)S(1)} custom-call(bf16[144,1024]{1,0:T(8,128)(2,1)S(1)} %get-tuple-element.58.refs_0_, bf16[144,1024]{1,0:T(8,128)(2,1)S(1)} %collective-permute-done.9.refs_1_, bf16[144,1024]{1,0:T(8,128)(2,1)S(1)} %collective-permute-done.10.refs_2_, bf16[144,1024]{1,0:T(8,128)(2,1)S(1)} %collective-permute-done.11.refs_3_, ...), custom_call_target="tpu_custom_call" | custom-call | flops 1024 | bytes 1024 | tf_op jit(solution)/shard_map/weight_early/pallas_call | solution.py:22
  46.9 0.0 collective-permute-done.12
  46.9 0.0 collective-permute-done.13
  47.0 0.0 collective-permute-done.8.refs_0_
  47.0 2.4 %collective-permute-start.19 = (bf16[48,1024]{1,0:T(8,128)(2,1)S(1)}, bf16[48,1024]{1,0:T(8,128)(2,1)S(1)}, u32[]{:S(2)}, u32[]{:S(2)}) collective-permute-start(bf16[48,1024]{1,0:T(8,128)(2,1)S(1)} %get-tuple-element.89), channel_id=1, source_target_pairs={{0,24},{8,16},{16,8},{24,0},{1,25},{9,17},{17,9},{25,1},{2,26},{10... | collective-permute-start | bytes 294920 | tf_op jit(solution)/shard_map/ppermute | solution.py:16
  49.4 0.5 collective-permute-start.18
  50.0 0.6 %collective-permute-start.17 = (bf16[48,1024]{1,0:T(8,128)(2,1)S(1)}, bf16[48,1024]{1,0:T(8,128)(2,1)S(1)}, u32[]{:S(2)}, u32[]{:S(2)}) collective-permute-start(bf16[48,1024]{1,0:T(8,128)(2,1)S(1)} %get-tuple-element.91), channel_id=1, source_target_pairs={{0,8},{8,0},{16,24},{24,16},{1,9},{9,1},{17,25},{25,17},{2,10},{10... | collective-permute-start | bytes 294920 | tf_op jit(solution)/shard_map/ppermute | solution.py:16
  50.6 0.1 pad_maximum_fusion
  50.6 0.1 select_reduce_fusion
  50.7 0.1 collective-permute-start.14
  50.8 1.6 %pull_last.1 = (f32[48,768]{1,0:T(8,128)S(1)}, f32[1,24]{1,0:T(1,128)S(1)}, f32[1,24]{1,0:T(1,128)S(1)}) custom-call(bf16[4,48,1024]{2,1,0:T(8,128)(2,1)S(1)} %collective-permute-done.8.refs_0_, bf16[1,4096,768]{2,1,0:T(8,128)(2,1)S(1)} %bitcast.19, bf16[4,48,1536]{2,1,0:T(8,128)(2,1)S(1)} %bitcast.22), custom_call_target="tpu_custom_call" | custom-call | flops 1024 | bytes 1024 | tf_op jit(solution)/shard_map/pull_last/pallas_call | solution.py:22
  52.4 0.0 collective-permute-done.14.sib
  52.4 1.5 %collective-permute-start.15 = (f32[1,24]{1,0:T(1,128)S(1)}, f32[1,24]{1,0:T(1,128)S(1)}, u32[]{:S(2)}, u32[]{:S(2)}) collective-permute-start(f32[1,24]{1,0:T(1,128)S(1)} %get-tuple-element.73), channel_id=1, source_target_pairs={{0,4},{1,5},{2,6},{3,7},{4,0},{5,1},{6,2},{7,3},{8,12},{9,13},{10,... | collective-permute-start | bytes 296 | tf_op jit(solution)/shard_map/ppermute | solution.py:16
  53.9 1.3 %collective-permute-start.16 = (f32[1,24]{1,0:T(1,128)S(1)}, f32[1,24]{1,0:T(1,128)S(1)}, u32[]{:S(2)}, u32[]{:S(2)}) collective-permute-start(f32[1,24]{1,0:T(1,128)S(1)} %get-tuple-element.74), channel_id=1, source_target_pairs={{0,5},{1,4},{2,7},{3,6},{4,1},{5,0},{6,3},{7,2},{8,13},{9,12},{10,... | collective-permute-start | bytes 296 | tf_op jit(solution)/shard_map/ppermute | solution.py:16
  55.2 0.0 collective-permute-done.19.refs_3_
  55.2 0.0 collective-permute-done.18.refs_2_
  55.2 0.0 collective-permute-done.17.refs_1_
  55.2 2.1 %finish.1 = (f32[1,1024,768]{2,1,0:T(8,128)}, bf16[4,48,1536]{2,1,0:T(8,128)(2,1)}) custom-call(bf16[48,1024]{1,0:T(8,128)(2,1)S(1)} %get-tuple-element.92.refs_0_, bf16[48,1024]{1,0:T(8,128)(2,1)S(1)} %collective-permute-done.17.refs_1_, bf16[48,1024]{1,0:T(8,128)(2,1)S(1)} %collective-permute-done.18.refs_2_, ...), custom_call_target="tpu_custom_call", output_to_operand_aliasing={{1}: (8, {})} | custom-call | flops 10000000000 | bytes 1024 | tf_op jit(solution)/shard_map/finish/pallas_call | solution.py:22
  57.3 0.0 collective-permute-done.15.same
  57.3 0.5 collective-permute-done.16.other
  57.8 0.7 %token_.1 = f32[1,128]{1,0:T(1,128)} custom-call(f32[1,24]{1,0:T(1,128)S(1)} %collective-permute-done.15.same, f32[1,24]{1,0:T(1,128)S(1)} %collective-permute-done.16.other, s32[1,128]{1,0:T(1,128)S(1)} %get-tuple-element.84.last_slots, f32[1,128]{1,0:T(1,128)S(1)} %bitcast.27, f32[1,128]{1,0:T(1,128)S(1)} %collective-permute-done.14.sib, f32[1,128]{1,0:T(1,128)S(1)} %bitcast.26), custom_call_target="tpu_custom_call" | custom-call | flops 1024 | bytes 1024 | tf_op jit(solution)/shard_map/token/pallas_call | solution.py:22
  (3 shorter events, 0.0 us)
Async XLA Ops:
  0.6 3.4 %collective-permute-start = (bf16[128,4096]{1,0:T(8,128)(2,1)}, bf16[128,4096]{1,0:T(8,128)(2,1)S(1)}, u32[]{:S(2)}, u32[]{:S(2)}) collective-permute-start(bf16[128,4096]{1,0:T(8,128)(2,1)} %rows.1), channel_id=1, source_target_pairs={{0,1},{1,0},{2,3},{3,2},{4,5},{5,4},{6,7},{7,6},{8,9},{9,8},{10,11... | collective-permute-start | bytes 3145736 | tf_op jit(solution)/shard_map/ppermute | solution.py:16
  1.1 2.9 %collective-permute-start.1 = (s32[1,128]{1,0:T(1,128)}, s32[1,128]{1,0:T(1,128)S(1)}, u32[]{:S(2)}, u32[]{:S(2)}) collective-permute-start(s32[1,128]{1,0:T(1,128)} %bitcast.28), channel_id=1, source_target_pairs={{0,1},{1,0},{2,3},{3,2},{4,5},{5,4},{6,7},{7,6},{8,9},{9,8},{10,11... | collective-permute-start | bytes 1544 | tf_op jit(solution)/shard_map/ppermute | solution.py:16
  1.2 32.1 %slice-start = ((s8[6291456]{0:T(1024)(128)(4,1)}), s8[4194304]{0:T(1024)(128)(4,1)S(1)}, s32[]{:S(2)}) async-start(s8[6291456]{0:T(1024)(128)(4,1)} %bitcast.18), calls=%async_computation | async-start | bytes 8388608
  1.2 2.1 %copy-start.1 = (f32[128,1]{0,1:T(1,128)S(1)}, f32[128,1]{0,1:T(1,128)}, u32[]{:S(2)}) copy-start(f32[128,1]{0,1:T(1,128)} %param.7) | copy-start | bytes 1540
  1.2 2.1 %copy-start.2 = (s32[128,1]{0,1:T(1,128)S(1)}, s32[128,1]{0,1:T(1,128)}, u32[]{:S(2)}) copy-start(s32[128,1]{0,1:T(1,128)} %param.6) | copy-start | bytes 1540
  1.2 32.1 %slice-start.1 = ((s8[6291456]{0:T(1024)(128)(4,1)}), s8[2097152]{0:T(1024)(128)(4,1)S(1)}, s32[]{:S(2)}) async-start(s8[6291456]{0:T(1024)(128)(4,1)} %bitcast.18), calls=%async_computation.1 | async-start | bytes 4194304
  1.2 2.8 %collective-permute-start.2 = (f32[1,128]{1,0:T(1,128)}, f32[1,128]{1,0:T(1,128)S(1)}, u32[]{:S(2)}, u32[]{:S(2)}) collective-permute-start(f32[1,128]{1,0:T(1,128)} %bitcast.24), channel_id=1, source_target_pairs={{0,1},{1,0},{2,3},{3,2},{4,5},{5,4},{6,7},{7,6},{8,9},{9,8},{10,11... | collective-permute-start | bytes 1544 | tf_op jit(solution)/shard_map/ppermute | solution.py:16
  1.7 1.5 %copy-start.3 = (bf16[128,4096]{1,0:T(8,128)(2,1)S(1)}, bf16[128,4096]{1,0:T(8,128)(2,1)}, u32[]{:S(2)}) copy-start(bf16[128,4096]{1,0:T(8,128)(2,1)} %rows.1) | copy-start | bytes 3145732
  3.3 6.5 %copy-start = (bf16[1,1,192,1536]{3,2,1,0:T(8,128)(2,1)S(1)}, bf16[1,1,192,1536]{3,2,1,0:T(8,128)(2,1)}, u32[]{:S(2)}) copy-start(bf16[1,1,192,1536]{3,2,1,0:T(8,128)(2,1)} %param.9) | copy-start | bytes 1769476
  4.8 21.6 %collective-permute-start.3 = (bf16[4,48,1024]{2,1,0:T(8,128)(2,1)S(1)}, bf16[4,48,1024]{2,1,0:T(8,128)(2,1)S(1)}, u32[]{:S(2)}, u32[]{:S(2)}) collective-permute-start(bf16[4,48,1024]{2,1,0:T(8,128)(2,1)S(1)} %get-tuple-element.47), channel_id=1, source_target_pairs={{0,2},{1,3},{2,0},{3,1},{4,6},{5,7},{6,4},{7,5},{8,10},{9,11},{10,... | collective-permute-start | bytes 1179656 | tf_op jit(solution)/shard_map/ppermute | solution.py:16
  7.4 20.6 %collective-permute-start.4 = (bf16[4,48,1024]{2,1,0:T(8,128)(2,1)S(1)}, bf16[4,48,1024]{2,1,0:T(8,128)(2,1)S(1)}, u32[]{:S(2)}, u32[]{:S(2)}) collective-permute-start(bf16[4,48,1024]{2,1,0:T(8,128)(2,1)S(1)} %get-tuple-element.48), channel_id=1, source_target_pairs={{0,6},{1,7},{2,4},{3,5},{4,2},{5,3},{6,0},{7,1},{8,14},{9,15},{10,... | collective-permute-start | bytes 1179656 | tf_op jit(solution)/shard_map/ppermute | solution.py:16
  10.0 10.9 %collective-permute-start.7 = (bf16[4,48,768]{2,1,0:T(8,128)(2,1)S(1)}, bf16[4,48,768]{2,1,0:T(8,128)(2,1)S(1)}, u32[]{:S(2)}, u32[]{:S(2)}) collective-permute-start(bf16[4,48,768]{2,1,0:T(8,128)(2,1)S(1)} %hidden.1.refs_0_), channel_id=1, source_target_pairs={{0,24},{8,16},{16,8},{24,0},{1,25},{9,17},{17,9},{25,1},{2,26},{10... | collective-permute-start | bytes 884744 | tf_op jit(solution)/shard_map/ppermute | solution.py:16
  12.6 13.7 %collective-permute-start.6 = (bf16[4,48,768]{2,1,0:T(8,128)(2,1)S(1)}, bf16[4,48,768]{2,1,0:T(8,128)(2,1)S(1)}, u32[]{:S(2)}, u32[]{:S(2)}) collective-permute-start(bf16[4,48,768]{2,1,0:T(8,128)(2,1)S(1)} %hidden.1.refs_0_), channel_id=1, source_target_pairs={{0,16},{8,24},{16,0},{24,8},{1,17},{9,25},{17,1},{25,9},{2,18},{10... | collective-permute-start | bytes 884744 | tf_op jit(solution)/shard_map/ppermute | solution.py:16
  13.1 13.3 %collective-permute-start.5 = (bf16[4,48,768]{2,1,0:T(8,128)(2,1)S(1)}, bf16[4,48,768]{2,1,0:T(8,128)(2,1)S(1)}, u32[]{:S(2)}, u32[]{:S(2)}) collective-permute-start(bf16[4,48,768]{2,1,0:T(8,128)(2,1)S(1)} %hidden.1.refs_0_), channel_id=1, source_target_pairs={{0,8},{8,0},{16,24},{24,16},{1,9},{9,1},{17,25},{25,17},{2,10},{10... | collective-permute-start | bytes 884744 | tf_op jit(solution)/shard_map/ppermute | solution.py:16
  27.9 19.0 %collective-permute-start.8 = (bf16[4,48,1024]{2,1,0:T(8,128)(2,1)S(1)}, bf16[4,48,1024]{2,1,0:T(8,128)(2,1)S(1)}, u32[]{:S(2)}, u32[]{:S(2)}) collective-permute-start(bf16[4,48,1024]{2,1,0:T(8,128)(2,1)S(1)} %get-tuple-element.53), channel_id=1, source_target_pairs={{0,4},{1,5},{2,6},{3,7},{4,0},{5,1},{6,2},{7,3},{8,12},{9,13},{10,... | collective-permute-start | bytes 1179656 | tf_op jit(solution)/shard_map/ppermute | solution.py:16
  29.7 10.0 %collective-permute-start.9 = (bf16[144,1024]{1,0:T(8,128)(2,1)S(1)}, bf16[144,1024]{1,0:T(8,128)(2,1)S(1)}, u32[]{:S(2)}, u32[]{:S(2)}) collective-permute-start(bf16[144,1024]{1,0:T(8,128)(2,1)S(1)} %get-tuple-element.59), channel_id=1, source_target_pairs={{0,8},{8,0},{16,24},{24,16},{1,9},{9,1},{17,25},{25,17},{2,10},{10... | collective-permute-start | bytes 884744 | tf_op jit(solution)/shard_map/ppermute | solution.py:16
  31.3 14.1 %collective-permute-start.10 = (bf16[144,1024]{1,0:T(8,128)(2,1)S(1)}, bf16[144,1024]{1,0:T(8,128)(2,1)S(1)}, u32[]{:S(2)}, u32[]{:S(2)}) collective-permute-start(bf16[144,1024]{1,0:T(8,128)(2,1)S(1)} %get-tuple-element.60), channel_id=1, source_target_pairs={{0,16},{8,24},{16,0},{24,8},{1,17},{9,25},{17,1},{25,9},{2,18},{10... | collective-permute-start | bytes 884744 | tf_op jit(solution)/shard_map/ppermute | solution.py:16
  32.8 12.6 %collective-permute-start.11 = (bf16[144,1024]{1,0:T(8,128)(2,1)S(1)}, bf16[144,1024]{1,0:T(8,128)(2,1)S(1)}, u32[]{:S(2)}, u32[]{:S(2)}) collective-permute-start(bf16[144,1024]{1,0:T(8,128)(2,1)S(1)} %get-tuple-element.61), channel_id=1, source_target_pairs={{0,24},{8,16},{16,8},{24,0},{1,25},{9,17},{17,9},{25,1},{2,26},{10... | collective-permute-start | bytes 884744 | tf_op jit(solution)/shard_map/ppermute | solution.py:16
  36.1 10.9 %collective-permute-start.12 = (f32[1,48]{1,0:T(1,128)S(1)}, f32[1,48]{1,0:T(1,128)S(1)}, u32[]{:S(2)}, u32[]{:S(2)}) collective-permute-start(f32[1,48]{1,0:T(1,128)S(1)} %get-tuple-element.63), channel_id=1, source_target_pairs={{0,6},{1,7},{2,4},{3,5},{4,2},{5,3},{6,0},{7,1},{8,14},{9,15},{10,... | collective-permute-start | bytes 584 | tf_op jit(solution)/shard_map/ppermute | solution.py:16
  39.8 7.2 %collective-permute-start.13 = (f32[1,48]{1,0:T(1,128)S(1)}, f32[1,48]{1,0:T(1,128)S(1)}, u32[]{:S(2)}, u32[]{:S(2)}) collective-permute-start(f32[1,48]{1,0:T(1,128)S(1)} %get-tuple-element.64), channel_id=1, source_target_pairs={{0,2},{1,3},{2,0},{3,1},{4,6},{5,7},{6,4},{7,5},{8,10},{9,11},{10,... | collective-permute-start | bytes 584 | tf_op jit(solution)/shard_map/ppermute | solution.py:16
  47.0 8.2 %collective-permute-start.19 = (bf16[48,1024]{1,0:T(8,128)(2,1)S(1)}, bf16[48,1024]{1,0:T(8,128)(2,1)S(1)}, u32[]{:S(2)}, u32[]{:S(2)}) collective-permute-start(bf16[48,1024]{1,0:T(8,128)(2,1)S(1)} %get-tuple-element.89), channel_id=1, source_target_pairs={{0,24},{8,16},{16,8},{24,0},{1,25},{9,17},{17,9},{25,1},{2,26},{10... | collective-permute-start | bytes 294920 | tf_op jit(solution)/shard_map/ppermute | solution.py:16
  49.4 5.8 %collective-permute-start.18 = (bf16[48,1024]{1,0:T(8,128)(2,1)S(1)}, bf16[48,1024]{1,0:T(8,128)(2,1)S(1)}, u32[]{:S(2)}, u32[]{:S(2)}) collective-permute-start(bf16[48,1024]{1,0:T(8,128)(2,1)S(1)} %get-tuple-element.90), channel_id=1, source_target_pairs={{0,16},{8,24},{16,0},{24,8},{1,17},{9,25},{17,1},{25,9},{2,18},{10... | collective-permute-start | bytes 294920 | tf_op jit(solution)/shard_map/ppermute | solution.py:16
  50.0 5.2 %collective-permute-start.17 = (bf16[48,1024]{1,0:T(8,128)(2,1)S(1)}, bf16[48,1024]{1,0:T(8,128)(2,1)S(1)}, u32[]{:S(2)}, u32[]{:S(2)}) collective-permute-start(bf16[48,1024]{1,0:T(8,128)(2,1)S(1)} %get-tuple-element.91), channel_id=1, source_target_pairs={{0,8},{8,0},{16,24},{24,16},{1,9},{9,1},{17,25},{25,17},{2,10},{10... | collective-permute-start | bytes 294920 | tf_op jit(solution)/shard_map/ppermute | solution.py:16
  50.7 1.7 %collective-permute-start.14 = (f32[1,128]{1,0:T(1,128)S(1)}, f32[1,128]{1,0:T(1,128)S(1)}, u32[]{:S(2)}, u32[]{:S(2)}) collective-permute-start(f32[1,128]{1,0:T(1,128)S(1)} %bitcast.34), channel_id=1, source_target_pairs={{0,1},{1,0},{2,3},{3,2},{4,5},{5,4},{6,7},{7,6},{8,9},{9,8},{10,11... | collective-permute-start | bytes 1544 | tf_op jit(solution)/shard_map/ppermute | solution.py:16
  52.4 4.9 %collective-permute-start.15 = (f32[1,24]{1,0:T(1,128)S(1)}, f32[1,24]{1,0:T(1,128)S(1)}, u32[]{:S(2)}, u32[]{:S(2)}) collective-permute-start(f32[1,24]{1,0:T(1,128)S(1)} %get-tuple-element.73), channel_id=1, source_target_pairs={{0,4},{1,5},{2,6},{3,7},{4,0},{5,1},{6,2},{7,3},{8,12},{9,13},{10,... | collective-permute-start | bytes 296 | tf_op jit(solution)/shard_map/ppermute | solution.py:16
  53.9 3.9 %collective-permute-start.16 = (f32[1,24]{1,0:T(1,128)S(1)}, f32[1,24]{1,0:T(1,128)S(1)}, u32[]{:S(2)}, u32[]{:S(2)}) collective-permute-start(f32[1,24]{1,0:T(1,128)S(1)} %get-tuple-element.74), channel_id=1, source_target_pairs={{0,5},{1,4},{2,7},{3,6},{4,1},{5,0},{6,3},{7,2},{8,13},{9,12},{10,... | collective-permute-start | bytes 296 | tf_op jit(solution)/shard_map/ppermute | solution.py:16

commit v6 on v2

--- a/solution.py
+++ b/solution.py
@@ -168,7 +168,7 @@
 
 
 def finish_kernel(step, replicas, parts, *refs):
-    rows = refs[:replicas]
+    rows = refs[:replicas][::-1]
     units, early, pulled, saved, _, out, grads, held, held_grads, sems = refs[replicas:]
     size = early.shape[0] // parts
     copies = []
@@ -288,7 +288,10 @@
         "weight_early",
     )[0]
 
-    rows, grads, total, returned = lax.optimization_barrier((last_rows, grads, total, returned))
+    rows, grads, total, returned = lax.optimization_barrier(
+        (last_rows, grads, total, returned[::-1])
+    )
+    returned = returned[::-1]
     late_rows = [rows[0]] + [swap(rows[j], "rep", j) for j in range(1, replicas)]
     pulled, *routers = kernel_call(
         lambda *refs: pull_last_kernel(last, *refs),
@@ -313,7 +316,7 @@
             jax.ShapeDtypeStruct((1, share, width), jnp.float32),
             jax.ShapeDtypeStruct(saved.shape, jnp.bfloat16),
         ],
-        [*late_rows, units_last, total, pulled, saved, grads],
+        [*reversed(late_rows), units_last, total, pulled, saved, grads],
         "finish",
         LARGE,
         in_specs=[WHOLE_VMEM] * (replicas + 4) + [IN_PLACE],

time: 57.7 us -> 57.8 us (level)
  transfers between devices with their start and end apart: 20 -> 20, of which waited for: 8 -> 9; matrix products, arithmetic and copies ran while one was open for 0% -> 0% of each run, Pallas kernels for 15% -> 14%
where the time goes in v6:
time: 57.8 us; the launch traced here: 57.7 us
  starting transfers between devices  23.3 us (40%)
  waiting for transfers between devices  22.1 us (38%)
  Pallas kernels  9.76 us (17%)
  local copies, waits for them, and re-layouts  1.56 us (3%)
  between operations  0.77 us (1%)
    ppermute x20, starting transfers between devices, swap(): return lax.ppermute(value, axis, [(i, i ^ step) for i in range(n)])  23.3 us
    ppermute x20, waiting for transfers between devices, swap(): return lax.ppermute(value, axis, [(i, i ^ step) for i in range(n)])  22.1 us
    pallas_call x10, Pallas kernels, kernel_call(): pl.pallas_call(kernel, out_shape=outs, compiler_params=pltpu.CompilerPara...  9.76 us
    unnamed x12, local copies, waits for them, and re-layouts  1.53 us
  transfers between devices with their start and end apart: 20, of which 9 were waited for; matrix products, arithmetic and copies ran while one was open for 0% of the time, Pallas kernels for 14%

profile of v6, /device:TPU:0, one launch (start us, length us, event | category | flops | bytes accessed | tf_op | source)
XLA Modules:
  0.0 57.7 jit_solution(11186706908591373998)
XLA Ops:
  0.6 0.5 collective-permute-start
  1.1 0.1 collective-permute-start.1
  1.2 0.0 slice-start
  1.2 0.0 copy-start.1
  1.2 0.0 copy-start.2
  1.2 0.0 copy-start
  1.2 0.0 slice-start.1
  1.2 0.5 collective-permute-start.2
  1.7 0.0 copy-start.3
  1.7 1.5 %copy-done.3 = bf16[128,4096]{1,0:T(8,128)(2,1)S(1)} copy-done((bf16[128,4096]{1,0:T(8,128)(2,1)S(1)}, bf16[128,4096]{1,0:T(8,128)(2,1)}, u32[]{:S(2)}) %copy-start.3) | copy-done | bytes 1048600
  3.3 0.1 own_rows.1.refs_0_
  3.3 0.3 collective-permute-done.1.refs_3_
  3.6 0.0 collective-permute-done.2.refs_5_
  3.7 0.0 collective-permute-done.refs_1_
  3.7 0.0 copy-done.1
  3.7 0.0 copy-done.2
  3.7 0.7 %place.1 = (bf16[4,48,1024]{2,1,0:T(8,128)(2,1)S(1)}, bf16[4,48,1024]{2,1,0:T(8,128)(2,1)S(1)}, bf16[4,48,1024]{2,1,0:T(8,128)(2,1)S(1)}, bf16[4,48,1024]{2,1,0:...) custom-call(bf16[128,4096]{1,0:T(8,128)(2,1)S(1)} %own_rows.1.refs_0_, ...), custom_call_target="tpu_custom_call" | custom-call | flops 1024 | bytes 1024 | tf_op jit(solution)/shard_map/place/pallas_call | solution.py:22
  4.4 3.0 %collective-permute-start.3 = (bf16[4,48,1024]{2,1,0:T(8,128)(2,1)S(1)}, bf16[4,48,1024]{2,1,0:T(8,128)(2,1)S(1)}, u32[]{:S(2)}, u32[]{:S(2)}) collective-permute-start(bf16[4,48,1024]{2,1,0:T(8,128)(2,1)S(1)} %get-tuple-element.44), channel_id=1, source_target_pairs={{0,2},{1,3},{2,0},{3,1},{4,6},{5,7},{6,4},{7,5},{8,10},{9,11},{10,... | collective-permute-start | bytes 1179656 | tf_op jit(solution)/shard_map/ppermute | solution.py:16
  7.4 2.5 %collective-permute-start.4 = (bf16[4,48,1024]{2,1,0:T(8,128)(2,1)S(1)}, bf16[4,48,1024]{2,1,0:T(8,128)(2,1)S(1)}, u32[]{:S(2)}, u32[]{:S(2)}) collective-permute-start(bf16[4,48,1024]{2,1,0:T(8,128)(2,1)S(1)} %get-tuple-element.45), channel_id=1, source_target_pairs={{0,6},{1,7},{2,4},{3,5},{4,2},{5,3},{6,0},{7,1},{8,14},{9,15},{10,... | collective-permute-start | bytes 1179656 | tf_op jit(solution)/shard_map/ppermute | solution.py:16
  9.9 0.0 copy-done
  9.9 0.2 hidden.1.refs_0_
  10.0 2.5 %collective-permute-start.7 = (bf16[4,48,768]{2,1,0:T(8,128)(2,1)S(1)}, bf16[4,48,768]{2,1,0:T(8,128)(2,1)S(1)}, u32[]{:S(2)}, u32[]{:S(2)}) collective-permute-start(bf16[4,48,768]{2,1,0:T(8,128)(2,1)S(1)} %hidden.1.refs_0_), channel_id=1, source_target_pairs={{0,24},{8,16},{16,8},{24,0},{1,25},{9,17},{17,9},{25,1},{2,26},{10... | collective-permute-start | bytes 884744 | tf_op jit(solution)/shard_map/ppermute | solution.py:16
  12.6 0.5 collective-permute-start.6
  13.1 0.5 collective-permute-start.5
  13.6 7.4 %collective-permute-done.7.refs_3_ = bf16[4,48,768]{2,1,0:T(8,128)(2,1)S(1)} collective-permute-done((bf16[4,48,768]{2,1,0:T(8,128)(2,1)S(1)}, bf16[4,48,768]{2,1,0:T(8,128)(2,1)S(1)}, u32[]{:S(2)}, u32[]{:S(2)}) %collective-permute-start.7) | collective-permute-done | bytes 294944 | tf_op jit(solution)/shard_map/ppermute | solution.py:16
  21.0 4.8 %collective-permute-done.6.refs_2_ = bf16[4,48,768]{2,1,0:T(8,128)(2,1)S(1)} collective-permute-done((bf16[4,48,768]{2,1,0:T(8,128)(2,1)S(1)}, bf16[4,48,768]{2,1,0:T(8,128)(2,1)S(1)}, u32[]{:S(2)}, u32[]{:S(2)}) %collective-permute-start.6) | collective-permute-done | bytes 294944 | tf_op jit(solution)/shard_map/ppermute | solution.py:16
  25.8 0.1 collective-permute-done.5.refs_1_
  25.9 0.1 units.1
  26.0 0.0 collective-permute-done.3.refs_1_
  26.0 1.5 %collective-permute-done.4.refs_2_ = bf16[4,48,1024]{2,1,0:T(8,128)(2,1)S(1)} collective-permute-done((bf16[4,48,1024]{2,1,0:T(8,128)(2,1)S(1)}, bf16[4,48,1024]{2,1,0:T(8,128)(2,1)S(1)}, u32[]{:S(2)}, u32[]{:S(2)}) %collective-permute-start.4) | collective-permute-done | bytes 393248 | tf_op jit(solution)/shard_map/ppermute | solution.py:16
  27.5 1.7 %collective-permute-start.8 = (bf16[4,48,1024]{2,1,0:T(8,128)(2,1)S(1)}, bf16[4,48,1024]{2,1,0:T(8,128)(2,1)S(1)}, u32[]{:S(2)}, u32[]{:S(2)}) collective-permute-start(bf16[4,48,1024]{2,1,0:T(8,128)(2,1)S(1)} %get-tuple-element.50), channel_id=1, source_target_pairs={{0,4},{1,5},{2,6},{3,7},{4,0},{5,1},{6,2},{7,3},{8,12},{9,13},{10,... | collective-permute-start | bytes 1179656 | tf_op jit(solution)/shard_map/ppermute | solution.py:16
  29.3 0.1 stack.1
  29.3 1.6 %collective-permute-start.9 = (bf16[144,1024]{1,0:T(8,128)(2,1)S(1)}, bf16[144,1024]{1,0:T(8,128)(2,1)S(1)}, u32[]{:S(2)}, u32[]{:S(2)}) collective-permute-start(bf16[144,1024]{1,0:T(8,128)(2,1)S(1)} %get-tuple-element.56), channel_id=1, source_target_pairs={{0,8},{8,0},{16,24},{24,16},{1,9},{9,1},{17,25},{25,17},{2,10},{10... | collective-permute-start | bytes 884744 | tf_op jit(solution)/shard_map/ppermute | solution.py:16
  30.9 1.5 %collective-permute-start.10 = (bf16[144,1024]{1,0:T(8,128)(2,1)S(1)}, bf16[144,1024]{1,0:T(8,128)(2,1)S(1)}, u32[]{:S(2)}, u32[]{:S(2)}) collective-permute-start(bf16[144,1024]{1,0:T(8,128)(2,1)S(1)} %get-tuple-element.57), channel_id=1, source_target_pairs={{0,16},{8,24},{16,0},{24,8},{1,17},{9,25},{17,1},{25,9},{2,18},{10... | collective-permute-start | bytes 884744 | tf_op jit(solution)/shard_map/ppermute | solution.py:16
  32.4 0.5 collective-permute-start.11
  32.9 0.0 slice-done
  32.9 0.0 slice-done.1
  32.9 2.8 %pull_early.1 = (bf16[4,48,1536]{2,1,0:T(8,128)(2,1)}, f32[1,48]{1,0:T(1,128)S(1)}, f32[1,48]{1,0:T(1,128)S(1)}, f32[1,48]{1,0:T(1,128)S(1)}) custom-call(bf16[4,48,1024]{2,1,0:T(8,128)(2,1)S(1)} %get-tuple-element.51.refs_0_, bf16[4,48,1024]{2,1,0:T(8,128)(2,1)S(1)} %collective-permute-done.3.refs_1_, ...), custom_call_target="tpu_custom_call" | custom-call | flops 1024 | bytes 1024 | tf_op jit(solution)/shard_map/pull_early/pallas_call | solution.py:22
  35.7 1.2 %collective-permute-start.12 = (f32[1,48]{1,0:T(1,128)S(1)}, f32[1,48]{1,0:T(1,128)S(1)}, u32[]{:S(2)}, u32[]{:S(2)}) collective-permute-start(f32[1,48]{1,0:T(1,128)S(1)} %get-tuple-element.60), channel_id=1, source_target_pairs={{0,6},{1,7},{2,4},{3,5},{4,2},{5,3},{6,0},{7,1},{8,14},{9,15},{10,... | collective-permute-start | bytes 584 | tf_op jit(solution)/shard_map/ppermute | solution.py:16
  36.9 2.5 %collective-permute-done.9.refs_1_ = bf16[144,1024]{1,0:T(8,128)(2,1)S(1)} collective-permute-done((bf16[144,1024]{1,0:T(8,128)(2,1)S(1)}, bf16[144,1024]{1,0:T(8,128)(2,1)S(1)}, u32[]{:S(2)}, u32[]{:S(2)}) %collective-permute-start.9) | collective-permute-done | bytes 294944 | tf_op jit(solution)/shard_map/ppermute | solution.py:16
  39.4 0.3 collective-permute-start.13
  39.6 4.9 %collective-permute-done.10.refs_2_ = bf16[144,1024]{1,0:T(8,128)(2,1)S(1)} collective-permute-done((bf16[144,1024]{1,0:T(8,128)(2,1)S(1)}, bf16[144,1024]{1,0:T(8,128)(2,1)S(1)}, u32[]{:S(2)}, u32[]{:S(2)}) %collective-permute-start.10) | collective-permute-done | bytes 294944 | tf_op jit(solution)/shard_map/ppermute | solution.py:16
  44.6 0.0 collective-permute-done.11.refs_3_
  44.6 1.5 %weight_early.1.refs_5_ = f32[1024,768]{1,0:T(8,128)S(1)} custom-call(bf16[144,1024]{1,0:T(8,128)(2,1)S(1)} %get-tuple-element.55.refs_0_, bf16[144,1024]{1,0:T(8,128)(2,1)S(1)} %collective-permute-done.9.refs_1_, bf16[144,1024]{1,0:T(8,128)(2,1)S(1)} %collective-permute-done.10.refs_2_, bf16[144,1024]{1,0:T(8,128)(2,1)S(1)} %collective-permute-done.11.refs_3_, ...), custom_call_target="tpu_custom_call" | custom-call | flops 1024 | bytes 1024 | tf_op jit(solution)/shard_map/weight_early/pallas_call | solution.py:22
  46.0 0.0 collective-permute-done.12
  46.1 0.0 collective-permute-done.13
  46.1 0.4 collective-permute-done.8.refs_0_
  46.5 1.6 %collective-permute-start.19 = (bf16[48,1024]{1,0:T(8,128)(2,1)S(1)}, bf16[48,1024]{1,0:T(8,128)(2,1)S(1)}, u32[]{:S(2)}, u32[]{:S(2)}) collective-permute-start(bf16[48,1024]{1,0:T(8,128)(2,1)S(1)} %get-tuple-element.86), channel_id=1, source_target_pairs={{0,8},{8,0},{16,24},{24,16},{1,9},{9,1},{17,25},{25,17},{2,10},{10... | collective-permute-start | bytes 294920 | tf_op jit(solution)/shard_map/ppermute | solution.py:16
  48.1 0.9 %collective-permute-start.18 = (bf16[48,1024]{1,0:T(8,128)(2,1)S(1)}, bf16[48,1024]{1,0:T(8,128)(2,1)S(1)}, u32[]{:S(2)}, u32[]{:S(2)}) collective-permute-start(bf16[48,1024]{1,0:T(8,128)(2,1)S(1)} %get-tuple-element.87), channel_id=1, source_target_pairs={{0,16},{8,24},{16,0},{24,8},{1,17},{9,25},{17,1},{25,9},{2,18},{10... | collective-permute-start | bytes 294920 | tf_op jit(solution)/shard_map/ppermute | solution.py:16
  48.9 1.1 %collective-permute-start.17 = (bf16[48,1024]{1,0:T(8,128)(2,1)S(1)}, bf16[48,1024]{1,0:T(8,128)(2,1)S(1)}, u32[]{:S(2)}, u32[]{:S(2)}) collective-permute-start(bf16[48,1024]{1,0:T(8,128)(2,1)S(1)} %get-tuple-element.88), channel_id=1, source_target_pairs={{0,24},{8,16},{16,8},{24,0},{1,25},{9,17},{17,9},{25,1},{2,26},{10... | collective-permute-start | bytes 294920 | tf_op jit(solution)/shard_map/ppermute | solution.py:16
  50.1 0.1 pad_maximum_fusion
  50.1 0.1 select_reduce_fusion
  50.3 0.1 collective-permute-start.14
  50.3 1.6 %pull_last.1 = (f32[48,768]{1,0:T(8,128)S(1)}, f32[1,24]{1,0:T(1,128)S(1)}, f32[1,24]{1,0:T(1,128)S(1)}) custom-call(bf16[4,48,1024]{2,1,0:T(8,128)(2,1)S(1)} %collective-permute-done.8.refs_0_, bf16[1,4096,768]{2,1,0:T(8,128)(2,1)S(1)} %bitcast.21, bf16[4,48,1536]{2,1,0:T(8,128)(2,1)S(1)} %bitcast.24), custom_call_target="tpu_custom_call" | custom-call | flops 1024 | bytes 1024 | tf_op jit(solution)/shard_map/pull_last/pallas_call | solution.py:22
  51.9 0.0 collective-permute-done.14.sib
  51.9 1.1 %collective-permute-start.15 = (f32[1,24]{1,0:T(1,128)S(1)}, f32[1,24]{1,0:T(1,128)S(1)}, u32[]{:S(2)}, u32[]{:S(2)}) collective-permute-start(f32[1,24]{1,0:T(1,128)S(1)} %get-tuple-element.70), channel_id=1, source_target_pairs={{0,4},{1,5},{2,6},{3,7},{4,0},{5,1},{6,2},{7,3},{8,12},{9,13},{10,... | collective-permute-start | bytes 296 | tf_op jit(solution)/shard_map/ppermute | solution.py:16
  53.0 1.7 %collective-permute-start.16 = (f32[1,24]{1,0:T(1,128)S(1)}, f32[1,24]{1,0:T(1,128)S(1)}, u32[]{:S(2)}, u32[]{:S(2)}) collective-permute-start(f32[1,24]{1,0:T(1,128)S(1)} %get-tuple-element.71), channel_id=1, source_target_pairs={{0,5},{1,4},{2,7},{3,6},{4,1},{5,0},{6,3},{7,2},{8,13},{9,12},{10,... | collective-permute-start | bytes 296 | tf_op jit(solution)/shard_map/ppermute | solution.py:16
  54.7 0.0 collective-permute-done.19.refs_2_
  54.7 0.1 collective-permute-done.18.refs_1_
  54.8 0.0 collective-permute-done.17.refs_0_
  54.8 2.1 %finish.1 = (f32[1,1024,768]{2,1,0:T(8,128)}, bf16[4,48,1536]{2,1,0:T(8,128)(2,1)}) custom-call(bf16[48,1024]{1,0:T(8,128)(2,1)S(1)} %collective-permute-done.17.refs_0_, bf16[48,1024]{1,0:T(8,128)(2,1)S(1)} %collective-permute-done.18.refs_1_, bf16[48,1024]{1,0:T(8,128)(2,1)S(1)} %collective-permute-done.19.refs_2_, ...), custom_call_target="tpu_custom_call", output_to_operand_aliasing={{1}: (8, {})} | custom-call | flops 10000000000 | bytes 1024 | tf_op jit(solution)/shard_map/finish/pallas_call | solution.py:22
  56.9 0.0 collective-permute-done.15.same
  56.9 0.0 collective-permute-done.16.other
  56.9 0.7 %token_.1 = f32[1,128]{1,0:T(1,128)} custom-call(f32[1,24]{1,0:T(1,128)S(1)} %collective-permute-done.15.same, f32[1,24]{1,0:T(1,128)S(1)} %collective-permute-done.16.other, s32[1,128]{1,0:T(1,128)S(1)} %get-tuple-element.81.last_slots, f32[1,128]{1,0:T(1,128)S(1)} %bitcast.29, f32[1,128]{1,0:T(1,128)S(1)} %collective-permute-done.14.sib, f32[1,128]{1,0:T(1,128)S(1)} %bitcast.28), custom_call_target="tpu_custom_call" | custom-call | flops 1024 | bytes 1024 | tf_op jit(solution)/shard_map/token/pallas_call | solution.py:22
  (3 shorter events, 0.0 us)
Async XLA Ops:
  0.6 3.0 %collective-permute-start = (bf16[128,4096]{1,0:T(8,128)(2,1)}, bf16[128,4096]{1,0:T(8,128)(2,1)S(1)}, u32[]{:S(2)}, u32[]{:S(2)}) collective-permute-start(bf16[128,4096]{1,0:T(8,128)(2,1)} %rows.1), channel_id=1, source_target_pairs={{0,1},{1,0},{2,3},{3,2},{4,5},{5,4},{6,7},{7,6},{8,9},{9,8},{10,11... | collective-permute-start | bytes 3145736 | tf_op jit(solution)/shard_map/ppermute | solution.py:16
  1.1 2.5 %collective-permute-start.1 = (s32[1,128]{1,0:T(1,128)}, s32[1,128]{1,0:T(1,128)S(1)}, u32[]{:S(2)}, u32[]{:S(2)}) collective-permute-start(s32[1,128]{1,0:T(1,128)} %bitcast.30), channel_id=1, source_target_pairs={{0,1},{1,0},{2,3},{3,2},{4,5},{5,4},{6,7},{7,6},{8,9},{9,8},{10,11... | collective-permute-start | bytes 1544 | tf_op jit(solution)/shard_map/ppermute | solution.py:16
  1.2 31.7 %slice-start = ((s8[6291456]{0:T(1024)(128)(4,1)}), s8[4194304]{0:T(1024)(128)(4,1)S(1)}, s32[]{:S(2)}) async-start(s8[6291456]{0:T(1024)(128)(4,1)} %bitcast.20), calls=%async_computation | async-start | bytes 8388608
  1.2 2.4 %copy-start.1 = (f32[128,1]{0,1:T(1,128)S(1)}, f32[128,1]{0,1:T(1,128)}, u32[]{:S(2)}) copy-start(f32[128,1]{0,1:T(1,128)} %param.7) | copy-start | bytes 1540
  1.2 2.4 %copy-start.2 = (s32[128,1]{0,1:T(1,128)S(1)}, s32[128,1]{0,1:T(1,128)}, u32[]{:S(2)}) copy-start(s32[128,1]{0,1:T(1,128)} %param.6) | copy-start | bytes 1540
  1.2 8.6 %copy-start = (bf16[1,1,192,1536]{3,2,1,0:T(8,128)(2,1)S(1)}, bf16[1,1,192,1536]{3,2,1,0:T(8,128)(2,1)}, u32[]{:S(2)}) copy-start(bf16[1,1,192,1536]{3,2,1,0:T(8,128)(2,1)} %param.9) | copy-start | bytes 1769476
  1.2 31.7 %slice-start.1 = ((s8[6291456]{0:T(1024)(128)(4,1)}), s8[2097152]{0:T(1024)(128)(4,1)S(1)}, s32[]{:S(2)}) async-start(s8[6291456]{0:T(1024)(128)(4,1)} %bitcast.20), calls=%async_computation.1 | async-start | bytes 4194304
  1.2 2.4 %collective-permute-start.2 = (f32[1,128]{1,0:T(1,128)}, f32[1,128]{1,0:T(1,128)S(1)}, u32[]{:S(2)}, u32[]{:S(2)}) collective-permute-start(f32[1,128]{1,0:T(1,128)} %bitcast.26), channel_id=1, source_target_pairs={{0,1},{1,0},{2,3},{3,2},{4,5},{5,4},{6,7},{7,6},{8,9},{9,8},{10,11... | collective-permute-start | bytes 1544 | tf_op jit(solution)/shard_map/ppermute | solution.py:16
  1.7 1.5 %copy-start.3 = (bf16[128,4096]{1,0:T(8,128)(2,1)S(1)}, bf16[128,4096]{1,0:T(8,128)(2,1)}, u32[]{:S(2)}) copy-start(bf16[128,4096]{1,0:T(8,128)(2,1)} %rows.1) | copy-start | bytes 3145732
  4.4 21.6 %collective-permute-start.3 = (bf16[4,48,1024]{2,1,0:T(8,128)(2,1)S(1)}, bf16[4,48,1024]{2,1,0:T(8,128)(2,1)S(1)}, u32[]{:S(2)}, u32[]{:S(2)}) collective-permute-start(bf16[4,48,1024]{2,1,0:T(8,128)(2,1)S(1)} %get-tuple-element.44), channel_id=1, source_target_pairs={{0,2},{1,3},{2,0},{3,1},{4,6},{5,7},{6,4},{7,5},{8,10},{9,11},{10,... | collective-permute-start | bytes 1179656 | tf_op jit(solution)/shard_map/ppermute | solution.py:16
  7.4 20.1 %collective-permute-start.4 = (bf16[4,48,1024]{2,1,0:T(8,128)(2,1)S(1)}, bf16[4,48,1024]{2,1,0:T(8,128)(2,1)S(1)}, u32[]{:S(2)}, u32[]{:S(2)}) collective-permute-start(bf16[4,48,1024]{2,1,0:T(8,128)(2,1)S(1)} %get-tuple-element.45), channel_id=1, source_target_pairs={{0,6},{1,7},{2,4},{3,5},{4,2},{5,3},{6,0},{7,1},{8,14},{9,15},{10,... | collective-permute-start | bytes 1179656 | tf_op jit(solution)/shard_map/ppermute | solution.py:16
  10.0 10.9 %collective-permute-start.7 = (bf16[4,48,768]{2,1,0:T(8,128)(2,1)S(1)}, bf16[4,48,768]{2,1,0:T(8,128)(2,1)S(1)}, u32[]{:S(2)}, u32[]{:S(2)}) collective-permute-start(bf16[4,48,768]{2,1,0:T(8,128)(2,1)S(1)} %hidden.1.refs_0_), channel_id=1, source_target_pairs={{0,24},{8,16},{16,8},{24,0},{1,25},{9,17},{17,9},{25,1},{2,26},{10... | collective-permute-start | bytes 884744 | tf_op jit(solution)/shard_map/ppermute | solution.py:16
  12.6 13.3 %collective-permute-start.6 = (bf16[4,48,768]{2,1,0:T(8,128)(2,1)S(1)}, bf16[4,48,768]{2,1,0:T(8,128)(2,1)S(1)}, u32[]{:S(2)}, u32[]{:S(2)}) collective-permute-start(bf16[4,48,768]{2,1,0:T(8,128)(2,1)S(1)} %hidden.1.refs_0_), channel_id=1, source_target_pairs={{0,16},{8,24},{16,0},{24,8},{1,17},{9,25},{17,1},{25,9},{2,18},{10... | collective-permute-start | bytes 884744 | tf_op jit(solution)/shard_map/ppermute | solution.py:16
  13.1 12.9 %collective-permute-start.5 = (bf16[4,48,768]{2,1,0:T(8,128)(2,1)S(1)}, bf16[4,48,768]{2,1,0:T(8,128)(2,1)S(1)}, u32[]{:S(2)}, u32[]{:S(2)}) collective-permute-start(bf16[4,48,768]{2,1,0:T(8,128)(2,1)S(1)} %hidden.1.refs_0_), channel_id=1, source_target_pairs={{0,8},{8,0},{16,24},{24,16},{1,9},{9,1},{17,25},{25,17},{2,10},{10... | collective-permute-start | bytes 884744 | tf_op jit(solution)/shard_map/ppermute | solution.py:16
  27.5 19.0 %collective-permute-start.8 = (bf16[4,48,1024]{2,1,0:T(8,128)(2,1)S(1)}, bf16[4,48,1024]{2,1,0:T(8,128)(2,1)S(1)}, u32[]{:S(2)}, u32[]{:S(2)}) collective-permute-start(bf16[4,48,1024]{2,1,0:T(8,128)(2,1)S(1)} %get-tuple-element.50), channel_id=1, source_target_pairs={{0,4},{1,5},{2,6},{3,7},{4,0},{5,1},{6,2},{7,3},{8,12},{9,13},{10,... | collective-permute-start | bytes 1179656 | tf_op jit(solution)/shard_map/ppermute | solution.py:16
  29.3 10.0 %collective-permute-start.9 = (bf16[144,1024]{1,0:T(8,128)(2,1)S(1)}, bf16[144,1024]{1,0:T(8,128)(2,1)S(1)}, u32[]{:S(2)}, u32[]{:S(2)}) collective-permute-start(bf16[144,1024]{1,0:T(8,128)(2,1)S(1)} %get-tuple-element.56), channel_id=1, source_target_pairs={{0,8},{8,0},{16,24},{24,16},{1,9},{9,1},{17,25},{25,17},{2,10},{10... | collective-permute-start | bytes 884744 | tf_op jit(solution)/shard_map/ppermute | solution.py:16
  30.9 13.6 %collective-permute-start.10 = (bf16[144,1024]{1,0:T(8,128)(2,1)S(1)}, bf16[144,1024]{1,0:T(8,128)(2,1)S(1)}, u32[]{:S(2)}, u32[]{:S(2)}) collective-permute-start(bf16[144,1024]{1,0:T(8,128)(2,1)S(1)} %get-tuple-element.57), channel_id=1, source_target_pairs={{0,16},{8,24},{16,0},{24,8},{1,17},{9,25},{17,1},{25,9},{2,18},{10... | collective-permute-start | bytes 884744 | tf_op jit(solution)/shard_map/ppermute | solution.py:16
  32.4 12.1 %collective-permute-start.11 = (bf16[144,1024]{1,0:T(8,128)(2,1)S(1)}, bf16[144,1024]{1,0:T(8,128)(2,1)S(1)}, u32[]{:S(2)}, u32[]{:S(2)}) collective-permute-start(bf16[144,1024]{1,0:T(8,128)(2,1)S(1)} %get-tuple-element.58), channel_id=1, source_target_pairs={{0,24},{8,16},{16,8},{24,0},{1,25},{9,17},{17,9},{25,1},{2,26},{10... | collective-permute-start | bytes 884744 | tf_op jit(solution)/shard_map/ppermute | solution.py:16
  35.7 10.4 %collective-permute-start.12 = (f32[1,48]{1,0:T(1,128)S(1)}, f32[1,48]{1,0:T(1,128)S(1)}, u32[]{:S(2)}, u32[]{:S(2)}) collective-permute-start(f32[1,48]{1,0:T(1,128)S(1)} %get-tuple-element.60), channel_id=1, source_target_pairs={{0,6},{1,7},{2,4},{3,5},{4,2},{5,3},{6,0},{7,1},{8,14},{9,15},{10,... | collective-permute-start | bytes 584 | tf_op jit(solution)/shard_map/ppermute | solution.py:16
  39.4 6.7 %collective-permute-start.13 = (f32[1,48]{1,0:T(1,128)S(1)}, f32[1,48]{1,0:T(1,128)S(1)}, u32[]{:S(2)}, u32[]{:S(2)}) collective-permute-start(f32[1,48]{1,0:T(1,128)S(1)} %get-tuple-element.61), channel_id=1, source_target_pairs={{0,2},{1,3},{2,0},{3,1},{4,6},{5,7},{6,4},{7,5},{8,10},{9,11},{10,... | collective-permute-start | bytes 584 | tf_op jit(solution)/shard_map/ppermute | solution.py:16
  46.5 8.2 %collective-permute-start.19 = (bf16[48,1024]{1,0:T(8,128)(2,1)S(1)}, bf16[48,1024]{1,0:T(8,128)(2,1)S(1)}, u32[]{:S(2)}, u32[]{:S(2)}) collective-permute-start(bf16[48,1024]{1,0:T(8,128)(2,1)S(1)} %get-tuple-element.86), channel_id=1, source_target_pairs={{0,8},{8,0},{16,24},{24,16},{1,9},{9,1},{17,25},{25,17},{2,10},{10... | collective-permute-start | bytes 294920 | tf_op jit(solution)/shard_map/ppermute | solution.py:16
  48.1 6.7 %collective-permute-start.18 = (bf16[48,1024]{1,0:T(8,128)(2,1)S(1)}, bf16[48,1024]{1,0:T(8,128)(2,1)S(1)}, u32[]{:S(2)}, u32[]{:S(2)}) collective-permute-start(bf16[48,1024]{1,0:T(8,128)(2,1)S(1)} %get-tuple-element.87), channel_id=1, source_target_pairs={{0,16},{8,24},{16,0},{24,8},{1,17},{9,25},{17,1},{25,9},{2,18},{10... | collective-permute-start | bytes 294920 | tf_op jit(solution)/shard_map/ppermute | solution.py:16
  48.9 5.9 %collective-permute-start.17 = (bf16[48,1024]{1,0:T(8,128)(2,1)S(1)}, bf16[48,1024]{1,0:T(8,128)(2,1)S(1)}, u32[]{:S(2)}, u32[]{:S(2)}) collective-permute-start(bf16[48,1024]{1,0:T(8,128)(2,1)S(1)} %get-tuple-element.88), channel_id=1, source_target_pairs={{0,24},{8,16},{16,8},{24,0},{1,25},{9,17},{17,9},{25,1},{2,26},{10... | collective-permute-start | bytes 294920 | tf_op jit(solution)/shard_map/ppermute | solution.py:16
  50.3 1.7 %collective-permute-start.14 = (f32[1,128]{1,0:T(1,128)S(1)}, f32[1,128]{1,0:T(1,128)S(1)}, u32[]{:S(2)}, u32[]{:S(2)}) collective-permute-start(f32[1,128]{1,0:T(1,128)S(1)} %bitcast.34), channel_id=1, source_target_pairs={{0,1},{1,0},{2,3},{3,2},{4,5},{5,4},{6,7},{7,6},{8,9},{9,8},{10,11... | collective-permute-start | bytes 1544 | tf_op jit(solution)/shard_map/ppermute | solution.py:16
  51.9 5.0 %collective-permute-start.15 = (f32[1,24]{1,0:T(1,128)S(1)}, f32[1,24]{1,0:T(1,128)S(1)}, u32[]{:S(2)}, u32[]{:S(2)}) collective-permute-start(f32[1,24]{1,0:T(1,128)S(1)} %get-tuple-element.70), channel_id=1, source_target_pairs={{0,4},{1,5},{2,6},{3,7},{4,0},{5,1},{6,2},{7,3},{8,12},{9,13},{10,... | collective-permute-start | bytes 296 | tf_op jit(solution)/shard_map/ppermute | solution.py:16
  53.0 3.9 %collective-permute-start.16 = (f32[1,24]{1,0:T(1,128)S(1)}, f32[1,24]{1,0:T(1,128)S(1)}, u32[]{:S(2)}, u32[]{:S(2)}) collective-permute-start(f32[1,24]{1,0:T(1,128)S(1)} %get-tuple-element.71), channel_id=1, source_target_pairs={{0,5},{1,4},{2,7},{3,6},{4,1},{5,0},{6,3},{7,2},{8,13},{9,12},{10,... | collective-permute-start | bytes 296 | tf_op jit(solution)/shard_map/ppermute | solution.py:16

commit v7 on v4

--- a/solution.py
+++ b/solution.py
@@ -151,7 +151,7 @@
 
 
 def units_kernel(order, *refs):
-    hidden, early, late = refs[:-2], refs[-2], refs[-1]
+    hidden, early, late = refs[-3::-1], refs[-2], refs[-1]
     chip = lax.axis_index("exp") // 2
     early[...] = jnp.concatenate([ref[chip ^ k] for ref in hidden for k in order[:-1]], axis=0)
     late[...] = jnp.concatenate([ref[chip ^ order[-1]] for ref in hidden], axis=0)
@@ -168,7 +168,7 @@
 
 
 def finish_kernel(step, replicas, parts, *refs):
-    rows = refs[:replicas]
+    rows = refs[:replicas][::-1]
     units, early, pulled, saved, _, out, grads, held, held_grads, sems = refs[replicas:]
     size = early.shape[0] // parts
     copies = []
@@ -262,7 +262,7 @@
             jax.ShapeDtypeStruct((replicas * len(early) * pair, width), jnp.bfloat16),
             jax.ShapeDtypeStruct((replicas * pair, width), jnp.bfloat16),
         ],
-        hidden_of,
+        hidden_of[::-1],
         "units",
     )
 
@@ -293,6 +293,13 @@
     )
     returned = [*near_returned, *returned[2:]]
     late_rows = [rows[0]] + [swap(rows[j], "rep", j) for j in range(1, replicas)]
+    returned = jnp.concatenate(returned, axis=1).reshape(len(early) * pair, 1)
+    slot_index = lax.broadcasted_iota(jnp.int32, (len(early) * pair, 1), 0)
+    sums = [
+        jnp.sum(jnp.where(slot_index == ids, returned, 0.0), axis=0, keepdims=True)
+        for ids in (slots[0:1], slots[1:2])
+    ]
+    rows, sums = lax.optimization_barrier((rows, sums))
     pulled, *routers = kernel_call(
         lambda *refs: pull_last_kernel(last, *refs),
         [jax.ShapeDtypeStruct((pair, width), jnp.float32)]
@@ -300,15 +307,10 @@
         [rows, down_weight, saved],
         "pull_last",
     )
-    returned = jnp.concatenate(returned, axis=1).reshape(len(early) * pair, 1)
-    slot_index = lax.broadcasted_iota(jnp.int32, (len(early) * pair, 1), 0)
-    sums = [
-        jnp.sum(jnp.where(slot_index == ids, returned, 0.0), axis=0, keepdims=True)
-        for ids in (slots[0:1], slots[1:2])
-    ]
-    sum_sib = swap(sums[1], "exp", 1)
-    routers, sum_sib = lax.optimization_barrier((routers, sum_sib))
     returned_last = [swap(routers[i], "exp", 2 * last + i) for i in range(2)]
+    late_rows, sum_sib = lax.optimization_barrier((late_rows[::-1], sums[1]))
+    late_rows = late_rows[::-1]
+    sum_sib = swap(sum_sib, "exp", 1)
     parts = 4
     weight_grad, grads = kernel_call(
         lambda *refs: finish_kernel(last, replicas, parts, *refs),
@@ -316,7 +318,7 @@
             jax.ShapeDtypeStruct((1, share, width), jnp.float32),
             jax.ShapeDtypeStruct(saved.shape, jnp.bfloat16),
         ],
-        [*late_rows, units_last, total, pulled, saved, grads],
+        [*reversed(late_rows), units_last, total, pulled, saved, grads],
         "finish",
         LARGE,
         in_specs=[WHOLE_VMEM] * (replicas + 4) + [IN_PLACE],

time: 57.7 us -> 57.6 us (level)
  starting transfers between devices: 23.3 us -> 21.8 us
  waiting for transfers between devices: 22 us -> 23.4 us
    ppermute x20, starting transfers between devices: 23.3 us -> 21.8 us  [swap(): return lax.ppermute(value, axis, [(i, i ^ step) for i in range(n)])]
    ppermute x20, waiting for transfers between devices: 22 us -> 23.4 us  [swap(): return lax.ppermute(value, axis, [(i, i ^ step) for i in range(n)])]
  transfers between devices with their start and end apart: 20 -> 20, of which waited for: 8 -> 9; matrix products, arithmetic and copies ran while one was open for 0% -> 0% of each run, Pallas kernels for 15% -> 15%
where the time goes in v7:
time: 57.6 us; the launch traced here: 57.5 us
  waiting for transfers between devices  23.4 us (41%)
  starting transfers between devices  21.8 us (38%)
  Pallas kernels  9.76 us (17%)
  local copies, waits for them, and re-layouts  1.56 us (3%)
  between operations  0.76 us (1%)
    ppermute x20, waiting for transfers between devices, swap(): return lax.ppermute(value, axis, [(i, i ^ step) for i in range(n)])  23.4 us
    ppermute x20, starting transfers between devices, swap(): return lax.ppermute(value, axis, [(i, i ^ step) for i in range(n)])  21.8 us
    pallas_call x10, Pallas kernels, kernel_call(): pl.pallas_call(kernel, out_shape=outs, compiler_params=pltpu.CompilerPara...  9.76 us
    unnamed x12, local copies, waits for them, and re-layouts  1.53 us
  transfers between devices with their start and end apart: 20, of which 9 were waited for; matrix products, arithmetic and copies ran while one was open for 0% of the time, Pallas kernels for 15%

profile of v7, /device:TPU:0, one launch (start us, length us, event | category | flops | bytes accessed | tf_op | source)
XLA Modules:
  0.0 57.5 jit_solution(8125214609156653483)
XLA Ops:
  0.6 0.5 collective-permute-start
  1.1 0.1 collective-permute-start.1
  1.2 0.0 slice-start
  1.2 0.0 copy-start.1
  1.2 0.0 copy-start.2
  1.2 0.0 copy-start
  1.2 0.0 slice-start.1
  1.2 0.5 collective-permute-start.2
  1.7 0.0 copy-start.3
  1.7 1.5 %copy-done.3 = bf16[128,4096]{1,0:T(8,128)(2,1)S(1)} copy-done((bf16[128,4096]{1,0:T(8,128)(2,1)S(1)}, bf16[128,4096]{1,0:T(8,128)(2,1)}, u32[]{:S(2)}) %copy-start.3) | copy-done | bytes 1048600
  3.3 0.1 own_rows.1.refs_0_
  3.3 0.3 collective-permute-done.1.refs_3_
  3.6 0.0 collective-permute-done.2.refs_5_
  3.7 0.0 collective-permute-done.refs_1_
  3.7 0.0 copy-done.1
  3.7 0.0 copy-done.2
  3.7 0.7 %place.1 = (bf16[4,48,1024]{2,1,0:T(8,128)(2,1)S(1)}, bf16[4,48,1024]{2,1,0:T(8,128)(2,1)S(1)}, bf16[4,48,1024]{2,1,0:T(8,128)(2,1)S(1)}, bf16[4,48,1024]{2,1,0:...) custom-call(bf16[128,4096]{1,0:T(8,128)(2,1)S(1)} %own_rows.1.refs_0_, ...), custom_call_target="tpu_custom_call" | custom-call | flops 1024 | bytes 1024 | tf_op jit(solution)/shard_map/place/pallas_call | solution.py:22
  4.4 3.0 %collective-permute-start.3 = (bf16[4,48,1024]{2,1,0:T(8,128)(2,1)S(1)}, bf16[4,48,1024]{2,1,0:T(8,128)(2,1)S(1)}, u32[]{:S(2)}, u32[]{:S(2)}) collective-permute-start(bf16[4,48,1024]{2,1,0:T(8,128)(2,1)S(1)} %get-tuple-element.48), channel_id=1, source_target_pairs={{0,2},{1,3},{2,0},{3,1},{4,6},{5,7},{6,4},{7,5},{8,10},{9,11},{10,... | collective-permute-start | bytes 1179656 | tf_op jit(solution)/shard_map/ppermute | solution.py:16
  7.4 2.5 %collective-permute-start.4 = (bf16[4,48,1024]{2,1,0:T(8,128)(2,1)S(1)}, bf16[4,48,1024]{2,1,0:T(8,128)(2,1)S(1)}, u32[]{:S(2)}, u32[]{:S(2)}) collective-permute-start(bf16[4,48,1024]{2,1,0:T(8,128)(2,1)S(1)} %get-tuple-element.49), channel_id=1, source_target_pairs={{0,6},{1,7},{2,4},{3,5},{4,2},{5,3},{6,0},{7,1},{8,14},{9,15},{10,... | collective-permute-start | bytes 1179656 | tf_op jit(solution)/shard_map/ppermute | solution.py:16
  9.9 0.0 copy-done
  9.9 0.2 hidden.1.refs_3_
  10.0 1.6 %collective-permute-start.7 = (bf16[4,48,768]{2,1,0:T(8,128)(2,1)S(1)}, bf16[4,48,768]{2,1,0:T(8,128)(2,1)S(1)}, u32[]{:S(2)}, u32[]{:S(2)}) collective-permute-start(bf16[4,48,768]{2,1,0:T(8,128)(2,1)S(1)} %hidden.1.refs_3_), channel_id=1, source_target_pairs={{0,8},{8,0},{16,24},{24,16},{1,9},{9,1},{17,25},{25,17},{2,10},{10... | collective-permute-start | bytes 884744 | tf_op jit(solution)/shard_map/ppermute | solution.py:16
  11.6 1.5 %collective-permute-start.6 = (bf16[4,48,768]{2,1,0:T(8,128)(2,1)S(1)}, bf16[4,48,768]{2,1,0:T(8,128)(2,1)S(1)}, u32[]{:S(2)}, u32[]{:S(2)}) collective-permute-start(bf16[4,48,768]{2,1,0:T(8,128)(2,1)S(1)} %hidden.1.refs_3_), channel_id=1, source_target_pairs={{0,16},{8,24},{16,0},{24,8},{1,17},{9,25},{17,1},{25,9},{2,18},{10... | collective-permute-start | bytes 884744 | tf_op jit(solution)/shard_map/ppermute | solution.py:16
  13.1 0.5 collective-permute-start.5
  13.6 6.4 %collective-permute-done.7.refs_2_ = bf16[4,48,768]{2,1,0:T(8,128)(2,1)S(1)} collective-permute-done((bf16[4,48,768]{2,1,0:T(8,128)(2,1)S(1)}, bf16[4,48,768]{2,1,0:T(8,128)(2,1)S(1)}, u32[]{:S(2)}, u32[]{:S(2)}) %collective-permute-start.7) | collective-permute-done | bytes 294944 | tf_op jit(solution)/shard_map/ppermute | solution.py:16
  20.0 6.1 %collective-permute-done.6.refs_1_ = bf16[4,48,768]{2,1,0:T(8,128)(2,1)S(1)} collective-permute-done((bf16[4,48,768]{2,1,0:T(8,128)(2,1)S(1)}, bf16[4,48,768]{2,1,0:T(8,128)(2,1)S(1)}, u32[]{:S(2)}, u32[]{:S(2)}) %collective-permute-start.6) | collective-permute-done | bytes 294944 | tf_op jit(solution)/shard_map/ppermute | solution.py:16
  26.1 0.0 collective-permute-done.5.refs_0_
  26.1 0.1 units.1
  26.2 0.0 collective-permute-done.3.refs_1_
  26.2 1.3 %collective-permute-done.4.refs_2_ = bf16[4,48,1024]{2,1,0:T(8,128)(2,1)S(1)} collective-permute-done((bf16[4,48,1024]{2,1,0:T(8,128)(2,1)S(1)}, bf16[4,48,1024]{2,1,0:T(8,128)(2,1)S(1)}, u32[]{:S(2)}, u32[]{:S(2)}) %collective-permute-start.4) | collective-permute-done | bytes 393248 | tf_op jit(solution)/shard_map/ppermute | solution.py:16
  27.5 1.7 %collective-permute-start.8 = (bf16[4,48,1024]{2,1,0:T(8,128)(2,1)S(1)}, bf16[4,48,1024]{2,1,0:T(8,128)(2,1)S(1)}, u32[]{:S(2)}, u32[]{:S(2)}) collective-permute-start(bf16[4,48,1024]{2,1,0:T(8,128)(2,1)S(1)} %get-tuple-element.54), channel_id=1, source_target_pairs={{0,4},{1,5},{2,6},{3,7},{4,0},{5,1},{6,2},{7,3},{8,12},{9,13},{10,... | collective-permute-start | bytes 1179656 | tf_op jit(solution)/shard_map/ppermute | solution.py:16
  29.3 0.1 stack.1
  29.3 1.6 %collective-permute-start.9 = (bf16[144,1024]{1,0:T(8,128)(2,1)S(1)}, bf16[144,1024]{1,0:T(8,128)(2,1)S(1)}, u32[]{:S(2)}, u32[]{:S(2)}) collective-permute-start(bf16[144,1024]{1,0:T(8,128)(2,1)S(1)} %get-tuple-element.60), channel_id=1, source_target_pairs={{0,8},{8,0},{16,24},{24,16},{1,9},{9,1},{17,25},{25,17},{2,10},{10... | collective-permute-start | bytes 884744 | tf_op jit(solution)/shard_map/ppermute | solution.py:16
  30.9 1.5 %collective-permute-start.10 = (bf16[144,1024]{1,0:T(8,128)(2,1)S(1)}, bf16[144,1024]{1,0:T(8,128)(2,1)S(1)}, u32[]{:S(2)}, u32[]{:S(2)}) collective-permute-start(bf16[144,1024]{1,0:T(8,128)(2,1)S(1)} %get-tuple-element.61), channel_id=1, source_target_pairs={{0,16},{8,24},{16,0},{24,8},{1,17},{9,25},{17,1},{25,9},{2,18},{10... | collective-permute-start | bytes 884744 | tf_op jit(solution)/shard_map/ppermute | solution.py:16
  32.4 0.5 collective-permute-start.11
  32.9 0.0 slice-done
  32.9 0.0 slice-done.1
  32.9 2.8 %pull_early.1 = (bf16[4,48,1536]{2,1,0:T(8,128)(2,1)}, f32[1,48]{1,0:T(1,128)S(1)}, f32[1,48]{1,0:T(1,128)S(1)}, f32[1,48]{1,0:T(1,128)S(1)}) custom-call(bf16[4,48,1024]{2,1,0:T(8,128)(2,1)S(1)} %get-tuple-element.55.refs_0_, bf16[4,48,1024]{2,1,0:T(8,128)(2,1)S(1)} %collective-permute-done.3.refs_1_, ...), custom_call_target="tpu_custom_call" | custom-call | flops 1024 | bytes 1024 | tf_op jit(solution)/shard_map/pull_early/pallas_call | solution.py:22
  35.7 0.3 collective-permute-start.12
  36.0 3.4 %collective-permute-done.9.refs_1_ = bf16[144,1024]{1,0:T(8,128)(2,1)S(1)} collective-permute-done((bf16[144,1024]{1,0:T(8,128)(2,1)S(1)}, bf16[144,1024]{1,0:T(8,128)(2,1)S(1)}, u32[]{:S(2)}, u32[]{:S(2)}) %collective-permute-start.9) | collective-permute-done | bytes 294944 | tf_op jit(solution)/shard_map/ppermute | solution.py:16
  39.4 1.0 %collective-permute-start.13 = (f32[1,48]{1,0:T(1,128)S(1)}, f32[1,48]{1,0:T(1,128)S(1)}, u32[]{:S(2)}, u32[]{:S(2)}) collective-permute-start(f32[1,48]{1,0:T(1,128)S(1)} %get-tuple-element.70), channel_id=1, source_target_pairs={{0,6},{1,7},{2,4},{3,5},{4,2},{5,3},{6,0},{7,1},{8,14},{9,15},{10,... | collective-permute-start | bytes 584 | tf_op jit(solution)/shard_map/ppermute | solution.py:16
  40.3 4.2 %collective-permute-done.10.refs_2_ = bf16[144,1024]{1,0:T(8,128)(2,1)S(1)} collective-permute-done((bf16[144,1024]{1,0:T(8,128)(2,1)S(1)}, bf16[144,1024]{1,0:T(8,128)(2,1)S(1)}, u32[]{:S(2)}, u32[]{:S(2)}) %collective-permute-start.10) | collective-permute-done | bytes 294944 | tf_op jit(solution)/shard_map/ppermute | solution.py:16
  44.6 0.0 collective-permute-done.11.refs_3_
  44.6 1.5 %weight_early.1.refs_5_ = f32[1024,768]{1,0:T(8,128)S(1)} custom-call(bf16[144,1024]{1,0:T(8,128)(2,1)S(1)} %get-tuple-element.59.refs_0_, bf16[144,1024]{1,0:T(8,128)(2,1)S(1)} %collective-permute-done.9.refs_1_, bf16[144,1024]{1,0:T(8,128)(2,1)S(1)} %collective-permute-done.10.refs_2_, bf16[144,1024]{1,0:T(8,128)(2,1)S(1)} %collective-permute-done.11.refs_3_, ...), custom_call_target="tpu_custom_call" | custom-call | flops 1024 | bytes 1024 | tf_op jit(solution)/shard_map/weight_early/pallas_call | solution.py:22
  46.0 0.0 collective-permute-done.12
  46.1 0.0 collective-permute-done.8.refs_0_
  46.1 1.3 %collective-permute-start.18 = (bf16[48,1024]{1,0:T(8,128)(2,1)S(1)}, bf16[48,1024]{1,0:T(8,128)(2,1)S(1)}, u32[]{:S(2)}, u32[]{:S(2)}) collective-permute-start(bf16[48,1024]{1,0:T(8,128)(2,1)S(1)} %get-tuple-element.94), channel_id=1, source_target_pairs={{0,8},{8,0},{16,24},{24,16},{1,9},{9,1},{17,25},{25,17},{2,10},{10... | collective-permute-start | bytes 294920 | tf_op jit(solution)/shard_map/ppermute | solution.py:16
  47.4 1.5 %collective-permute-start.17 = (bf16[48,1024]{1,0:T(8,128)(2,1)S(1)}, bf16[48,1024]{1,0:T(8,128)(2,1)S(1)}, u32[]{:S(2)}, u32[]{:S(2)}) collective-permute-start(bf16[48,1024]{1,0:T(8,128)(2,1)S(1)} %get-tuple-element.95), channel_id=1, source_target_pairs={{0,16},{8,24},{16,0},{24,8},{1,17},{9,25},{17,1},{25,9},{2,18},{10... | collective-permute-start | bytes 294920 | tf_op jit(solution)/shard_map/ppermute | solution.py:16
  48.9 0.7 %collective-permute-start.16 = (bf16[48,1024]{1,0:T(8,128)(2,1)S(1)}, bf16[48,1024]{1,0:T(8,128)(2,1)S(1)}, u32[]{:S(2)}, u32[]{:S(2)}) collective-permute-start(bf16[48,1024]{1,0:T(8,128)(2,1)S(1)} %get-tuple-element.96), channel_id=1, source_target_pairs={{0,24},{8,16},{16,8},{24,0},{1,25},{9,17},{17,9},{25,1},{2,26},{10... | collective-permute-start | bytes 294920 | tf_op jit(solution)/shard_map/ppermute | solution.py:16
  49.7 0.0 collective-permute-done.13
  49.7 0.1 pad_maximum_fusion
  49.7 0.1 select_reduce_fusion
  49.8 1.6 %pull_last.1 = (f32[48,768]{1,0:T(8,128)S(1)}, f32[1,24]{1,0:T(1,128)S(1)}, f32[1,24]{1,0:T(1,128)S(1)}) custom-call(bf16[4,48,1024]{2,1,0:T(8,128)(2,1)S(1)} %collective-permute-done.8.refs_0_, bf16[1,4096,768]{2,1,0:T(8,128)(2,1)S(1)} %bitcast.21, bf16[4,48,1536]{2,1,0:T(8,128)(2,1)S(1)} %bitcast.24), custom_call_target="tpu_custom_call" | custom-call | flops 1024 | bytes 1024 | tf_op jit(solution)/shard_map/pull_last/pallas_call | solution.py:22
  51.4 1.5 %collective-permute-start.14 = (f32[1,24]{1,0:T(1,128)S(1)}, f32[1,24]{1,0:T(1,128)S(1)}, u32[]{:S(2)}, u32[]{:S(2)}) collective-permute-start(f32[1,24]{1,0:T(1,128)S(1)} %get-tuple-element.72), channel_id=1, source_target_pairs={{0,4},{1,5},{2,6},{3,7},{4,0},{5,1},{6,2},{7,3},{8,12},{9,13},{10,... | collective-permute-start | bytes 296 | tf_op jit(solution)/shard_map/ppermute | solution.py:16
  52.9 0.0 collective-permute-start.15
  52.9 0.0 collective-permute-done.18.refs_2_
  52.9 0.2 collective-permute-done.17.refs_1_
  53.1 1.4 %collective-permute-done.16.refs_0_ = bf16[48,1024]{1,0:T(8,128)(2,1)S(1)} collective-permute-done((bf16[48,1024]{1,0:T(8,128)(2,1)S(1)}, bf16[48,1024]{1,0:T(8,128)(2,1)S(1)}, u32[]{:S(2)}, u32[]{:S(2)}) %collective-permute-start.16) | collective-permute-done | bytes 98336 | tf_op jit(solution)/shard_map/ppermute | solution.py:16
  54.5 0.1 collective-permute-start.19
  54.6 2.1 %finish.1 = (f32[1,1024,768]{2,1,0:T(8,128)}, bf16[4,48,1536]{2,1,0:T(8,128)(2,1)}) custom-call(bf16[48,1024]{1,0:T(8,128)(2,1)S(1)} %collective-permute-done.16.refs_0_, bf16[48,1024]{1,0:T(8,128)(2,1)S(1)} %collective-permute-done.17.refs_1_, bf16[48,1024]{1,0:T(8,128)(2,1)S(1)} %collective-permute-done.18.refs_2_, ...), custom_call_target="tpu_custom_call", output_to_operand_aliasing={{1}: (8, {})} | custom-call | flops 10000000000 | bytes 1024 | tf_op jit(solution)/shard_map/finish/pallas_call | solution.py:22
  56.7 0.0 collective-permute-done.14.same
  56.7 0.1 collective-permute-done.15.other
  56.8 0.0 collective-permute-done.19.sib
  56.8 0.7 %token_.1 = f32[1,128]{1,0:T(1,128)} custom-call(f32[1,24]{1,0:T(1,128)S(1)} %collective-permute-done.14.same, f32[1,24]{1,0:T(1,128)S(1)} %collective-permute-done.15.other, s32[1,128]{1,0:T(1,128)S(1)} %get-tuple-element.88.last_slots, f32[1,128]{1,0:T(1,128)S(1)} %bitcast.29, f32[1,128]{1,0:T(1,128)S(1)} %collective-permute-done.19.sib, f32[1,128]{1,0:T(1,128)S(1)} %bitcast.28), custom_call_target="tpu_custom_call" | custom-call | flops 1024 | bytes 1024 | tf_op jit(solution)/shard_map/token/pallas_call | solution.py:22
  (3 shorter events, 0.0 us)
Async XLA Ops:
  0.6 3.0 %collective-permute-start = (bf16[128,4096]{1,0:T(8,128)(2,1)}, bf16[128,4096]{1,0:T(8,128)(2,1)S(1)}, u32[]{:S(2)}, u32[]{:S(2)}) collective-permute-start(bf16[128,4096]{1,0:T(8,128)(2,1)} %rows.1), channel_id=1, source_target_pairs={{0,1},{1,0},{2,3},{3,2},{4,5},{5,4},{6,7},{7,6},{8,9},{9,8},{10,11... | collective-permute-start | bytes 3145736 | tf_op jit(solution)/shard_map/ppermute | solution.py:16
  1.1 2.5 %collective-permute-start.1 = (s32[1,128]{1,0:T(1,128)}, s32[1,128]{1,0:T(1,128)S(1)}, u32[]{:S(2)}, u32[]{:S(2)}) collective-permute-start(s32[1,128]{1,0:T(1,128)} %bitcast.30), channel_id=1, source_target_pairs={{0,1},{1,0},{2,3},{3,2},{4,5},{5,4},{6,7},{7,6},{8,9},{9,8},{10,11... | collective-permute-start | bytes 1544 | tf_op jit(solution)/shard_map/ppermute | solution.py:16
  1.2 31.7 %slice-start = ((s8[6291456]{0:T(1024)(128)(4,1)}), s8[4194304]{0:T(1024)(128)(4,1)S(1)}, s32[]{:S(2)}) async-start(s8[6291456]{0:T(1024)(128)(4,1)} %bitcast.20), calls=%async_computation | async-start | bytes 8388608
  1.2 2.4 %copy-start.1 = (f32[128,1]{0,1:T(1,128)S(1)}, f32[128,1]{0,1:T(1,128)}, u32[]{:S(2)}) copy-start(f32[128,1]{0,1:T(1,128)} %param.7) | copy-start | bytes 1540
  1.2 2.4 %copy-start.2 = (s32[128,1]{0,1:T(1,128)S(1)}, s32[128,1]{0,1:T(1,128)}, u32[]{:S(2)}) copy-start(s32[128,1]{0,1:T(1,128)} %param.6) | copy-start | bytes 1540
  1.2 8.6 %copy-start = (bf16[1,1,192,1536]{3,2,1,0:T(8,128)(2,1)S(1)}, bf16[1,1,192,1536]{3,2,1,0:T(8,128)(2,1)}, u32[]{:S(2)}) copy-start(bf16[1,1,192,1536]{3,2,1,0:T(8,128)(2,1)} %param.9) | copy-start | bytes 1769476
  1.2 31.7 %slice-start.1 = ((s8[6291456]{0:T(1024)(128)(4,1)}), s8[2097152]{0:T(1024)(128)(4,1)S(1)}, s32[]{:S(2)}) async-start(s8[6291456]{0:T(1024)(128)(4,1)} %bitcast.20), calls=%async_computation.1 | async-start | bytes 4194304
  1.2 2.4 %collective-permute-start.2 = (f32[1,128]{1,0:T(1,128)}, f32[1,128]{1,0:T(1,128)S(1)}, u32[]{:S(2)}, u32[]{:S(2)}) collective-permute-start(f32[1,128]{1,0:T(1,128)} %bitcast.26), channel_id=1, source_target_pairs={{0,1},{1,0},{2,3},{3,2},{4,5},{5,4},{6,7},{7,6},{8,9},{9,8},{10,11... | collective-permute-start | bytes 1544 | tf_op jit(solution)/shard_map/ppermute | solution.py:16
  1.7 1.5 %copy-start.3 = (bf16[128,4096]{1,0:T(8,128)(2,1)S(1)}, bf16[128,4096]{1,0:T(8,128)(2,1)}, u32[]{:S(2)}) copy-start(bf16[128,4096]{1,0:T(8,128)(2,1)} %rows.1) | copy-start | bytes 3145732
  4.4 21.9 %collective-permute-start.3 = (bf16[4,48,1024]{2,1,0:T(8,128)(2,1)S(1)}, bf16[4,48,1024]{2,1,0:T(8,128)(2,1)S(1)}, u32[]{:S(2)}, u32[]{:S(2)}) collective-permute-start(bf16[4,48,1024]{2,1,0:T(8,128)(2,1)S(1)} %get-tuple-element.48), channel_id=1, source_target_pairs={{0,2},{1,3},{2,0},{3,1},{4,6},{5,7},{6,4},{7,5},{8,10},{9,11},{10,... | collective-permute-start | bytes 1179656 | tf_op jit(solution)/shard_map/ppermute | solution.py:16
  7.4 20.1 %collective-permute-start.4 = (bf16[4,48,1024]{2,1,0:T(8,128)(2,1)S(1)}, bf16[4,48,1024]{2,1,0:T(8,128)(2,1)S(1)}, u32[]{:S(2)}, u32[]{:S(2)}) collective-permute-start(bf16[4,48,1024]{2,1,0:T(8,128)(2,1)S(1)} %get-tuple-element.49), channel_id=1, source_target_pairs={{0,6},{1,7},{2,4},{3,5},{4,2},{5,3},{6,0},{7,1},{8,14},{9,15},{10,... | collective-permute-start | bytes 1179656 | tf_op jit(solution)/shard_map/ppermute | solution.py:16
  10.0 10.0 %collective-permute-start.7 = (bf16[4,48,768]{2,1,0:T(8,128)(2,1)S(1)}, bf16[4,48,768]{2,1,0:T(8,128)(2,1)S(1)}, u32[]{:S(2)}, u32[]{:S(2)}) collective-permute-start(bf16[4,48,768]{2,1,0:T(8,128)(2,1)S(1)} %hidden.1.refs_3_), channel_id=1, source_target_pairs={{0,8},{8,0},{16,24},{24,16},{1,9},{9,1},{17,25},{25,17},{2,10},{10... | collective-permute-start | bytes 884744 | tf_op jit(solution)/shard_map/ppermute | solution.py:16
  11.6 14.5 %collective-permute-start.6 = (bf16[4,48,768]{2,1,0:T(8,128)(2,1)S(1)}, bf16[4,48,768]{2,1,0:T(8,128)(2,1)S(1)}, u32[]{:S(2)}, u32[]{:S(2)}) collective-permute-start(bf16[4,48,768]{2,1,0:T(8,128)(2,1)S(1)} %hidden.1.refs_3_), channel_id=1, source_target_pairs={{0,16},{8,24},{16,0},{24,8},{1,17},{9,25},{17,1},{25,9},{2,18},{10... | collective-permute-start | bytes 884744 | tf_op jit(solution)/shard_map/ppermute | solution.py:16
  13.1 13.0 %collective-permute-start.5 = (bf16[4,48,768]{2,1,0:T(8,128)(2,1)S(1)}, bf16[4,48,768]{2,1,0:T(8,128)(2,1)S(1)}, u32[]{:S(2)}, u32[]{:S(2)}) collective-permute-start(bf16[4,48,768]{2,1,0:T(8,128)(2,1)S(1)} %hidden.1.refs_3_), channel_id=1, source_target_pairs={{0,24},{8,16},{16,8},{24,0},{1,25},{9,17},{17,9},{25,1},{2,26},{10... | collective-permute-start | bytes 884744 | tf_op jit(solution)/shard_map/ppermute | solution.py:16
  27.5 18.5 %collective-permute-start.8 = (bf16[4,48,1024]{2,1,0:T(8,128)(2,1)S(1)}, bf16[4,48,1024]{2,1,0:T(8,128)(2,1)S(1)}, u32[]{:S(2)}, u32[]{:S(2)}) collective-permute-start(bf16[4,48,1024]{2,1,0:T(8,128)(2,1)S(1)} %get-tuple-element.54), channel_id=1, source_target_pairs={{0,4},{1,5},{2,6},{3,7},{4,0},{5,1},{6,2},{7,3},{8,12},{9,13},{10,... | collective-permute-start | bytes 1179656 | tf_op jit(solution)/shard_map/ppermute | solution.py:16
  29.3 10.0 %collective-permute-start.9 = (bf16[144,1024]{1,0:T(8,128)(2,1)S(1)}, bf16[144,1024]{1,0:T(8,128)(2,1)S(1)}, u32[]{:S(2)}, u32[]{:S(2)}) collective-permute-start(bf16[144,1024]{1,0:T(8,128)(2,1)S(1)} %get-tuple-element.60), channel_id=1, source_target_pairs={{0,8},{8,0},{16,24},{24,16},{1,9},{9,1},{17,25},{25,17},{2,10},{10... | collective-permute-start | bytes 884744 | tf_op jit(solution)/shard_map/ppermute | solution.py:16
  30.9 13.6 %collective-permute-start.10 = (bf16[144,1024]{1,0:T(8,128)(2,1)S(1)}, bf16[144,1024]{1,0:T(8,128)(2,1)S(1)}, u32[]{:S(2)}, u32[]{:S(2)}) collective-permute-start(bf16[144,1024]{1,0:T(8,128)(2,1)S(1)} %get-tuple-element.61), channel_id=1, source_target_pairs={{0,16},{8,24},{16,0},{24,8},{1,17},{9,25},{17,1},{25,9},{2,18},{10... | collective-permute-start | bytes 884744 | tf_op jit(solution)/shard_map/ppermute | solution.py:16
  32.4 12.1 %collective-permute-start.11 = (bf16[144,1024]{1,0:T(8,128)(2,1)S(1)}, bf16[144,1024]{1,0:T(8,128)(2,1)S(1)}, u32[]{:S(2)}, u32[]{:S(2)}) collective-permute-start(bf16[144,1024]{1,0:T(8,128)(2,1)S(1)} %get-tuple-element.62), channel_id=1, source_target_pairs={{0,24},{8,16},{16,8},{24,0},{1,25},{9,17},{17,9},{25,1},{2,26},{10... | collective-permute-start | bytes 884744 | tf_op jit(solution)/shard_map/ppermute | solution.py:16
  35.7 10.4 %collective-permute-start.12 = (f32[1,48]{1,0:T(1,128)S(1)}, f32[1,48]{1,0:T(1,128)S(1)}, u32[]{:S(2)}, u32[]{:S(2)}) collective-permute-start(f32[1,48]{1,0:T(1,128)S(1)} %get-tuple-element.65), channel_id=1, source_target_pairs={{0,2},{1,3},{2,0},{3,1},{4,6},{5,7},{6,4},{7,5},{8,10},{9,11},{10,... | collective-permute-start | bytes 584 | tf_op jit(solution)/shard_map/ppermute | solution.py:16
  39.4 10.3 %collective-permute-start.13 = (f32[1,48]{1,0:T(1,128)S(1)}, f32[1,48]{1,0:T(1,128)S(1)}, u32[]{:S(2)}, u32[]{:S(2)}) collective-permute-start(f32[1,48]{1,0:T(1,128)S(1)} %get-tuple-element.70), channel_id=1, source_target_pairs={{0,6},{1,7},{2,4},{3,5},{4,2},{5,3},{6,0},{7,1},{8,14},{9,15},{10,... | collective-permute-start | bytes 584 | tf_op jit(solution)/shard_map/ppermute | solution.py:16
  46.1 6.8 %collective-permute-start.18 = (bf16[48,1024]{1,0:T(8,128)(2,1)S(1)}, bf16[48,1024]{1,0:T(8,128)(2,1)S(1)}, u32[]{:S(2)}, u32[]{:S(2)}) collective-permute-start(bf16[48,1024]{1,0:T(8,128)(2,1)S(1)} %get-tuple-element.94), channel_id=1, source_target_pairs={{0,8},{8,0},{16,24},{24,16},{1,9},{9,1},{17,25},{25,17},{2,10},{10... | collective-permute-start | bytes 294920 | tf_op jit(solution)/shard_map/ppermute | solution.py:16
  47.4 5.7 %collective-permute-start.17 = (bf16[48,1024]{1,0:T(8,128)(2,1)S(1)}, bf16[48,1024]{1,0:T(8,128)(2,1)S(1)}, u32[]{:S(2)}, u32[]{:S(2)}) collective-permute-start(bf16[48,1024]{1,0:T(8,128)(2,1)S(1)} %get-tuple-element.95), channel_id=1, source_target_pairs={{0,16},{8,24},{16,0},{24,8},{1,17},{9,25},{17,1},{25,9},{2,18},{10... | collective-permute-start | bytes 294920 | tf_op jit(solution)/shard_map/ppermute | solution.py:16
  48.9 5.5 %collective-permute-start.16 = (bf16[48,1024]{1,0:T(8,128)(2,1)S(1)}, bf16[48,1024]{1,0:T(8,128)(2,1)S(1)}, u32[]{:S(2)}, u32[]{:S(2)}) collective-permute-start(bf16[48,1024]{1,0:T(8,128)(2,1)S(1)} %get-tuple-element.96), channel_id=1, source_target_pairs={{0,24},{8,16},{16,8},{24,0},{1,25},{9,17},{17,9},{25,1},{2,26},{10... | collective-permute-start | bytes 294920 | tf_op jit(solution)/shard_map/ppermute | solution.py:16
  51.4 5.3 %collective-permute-start.14 = (f32[1,24]{1,0:T(1,128)S(1)}, f32[1,24]{1,0:T(1,128)S(1)}, u32[]{:S(2)}, u32[]{:S(2)}) collective-permute-start(f32[1,24]{1,0:T(1,128)S(1)} %get-tuple-element.72), channel_id=1, source_target_pairs={{0,4},{1,5},{2,6},{3,7},{4,0},{5,1},{6,2},{7,3},{8,12},{9,13},{10,... | collective-permute-start | bytes 296 | tf_op jit(solution)/shard_map/ppermute | solution.py:16
  52.9 3.9 %collective-permute-start.15 = (f32[1,24]{1,0:T(1,128)S(1)}, f32[1,24]{1,0:T(1,128)S(1)}, u32[]{:S(2)}, u32[]{:S(2)}) collective-permute-start(f32[1,24]{1,0:T(1,128)S(1)} %get-tuple-element.73), channel_id=1, source_target_pairs={{0,5},{1,4},{2,7},{3,6},{4,1},{5,0},{6,3},{7,2},{8,13},{9,12},{10,... | collective-permute-start | bytes 296 | tf_op jit(solution)/shard_map/ppermute | solution.py:16
  54.5 2.3 %collective-permute-start.19 = (f32[1,128]{1,0:T(1,128)S(1)}, f32[1,128]{1,0:T(1,128)S(1)}, u32[]{:S(2)}, u32[]{:S(2)}) collective-permute-start(f32[1,128]{1,0:T(1,128)S(1)} %bitcast.34), channel_id=1, source_target_pairs={{0,1},{1,0},{2,3},{3,2},{4,5},{5,4},{6,7},{7,6},{8,9},{9,8},{10,11... | collective-permute-start | bytes 1544 | tf_op jit(solution)/shard_map/ppermute | solution.py:16

commit v8 on v7

--- a/solution.py
+++ b/solution.py
@@ -157,14 +157,15 @@
     late[...] = jnp.concatenate([ref[chip ^ order[-1]] for ref in hidden], axis=0)
 
 
-def weight_early_kernel(*refs):
-    rows, units, out = refs[:-2], refs[-2], refs[-1]
-    out[...] = lax.dot_general(
+def weight_early_kernel(first, rows, units, before, out):
+    size = rows[0].shape[0]
+    total = lax.dot_general(
         jnp.concatenate([ref[...] for ref in rows], axis=0),
-        units[...],
+        units[first * size : (first + len(rows)) * size, :],
         (((0,), (0,)), ((), ())),
         preferred_element_type=jnp.float32,
     )
+    out[...] = total + before[0][...] if before else total
 
 
 def finish_kernel(step, replicas, parts, *refs):
@@ -281,12 +282,18 @@
         "pull_early",
     )
     returned = routers[:1] + [swap(router, "exp", 2 * k) for router, k in zip(routers[1:], early[1:])]
-    total = kernel_call(
-        weight_early_kernel,
-        [jax.ShapeDtypeStruct((share, width), jnp.float32)],
-        [*early_rows, units],
-        "weight_early",
-    )[0]
+    total = []
+    half = replicas // 2
+    for first, count in ((0, half), (half, replicas - half)):
+        total = kernel_call(
+            lambda *refs: weight_early_kernel(
+                first, refs[:count], refs[count], refs[count + 1 : -1], refs[-1]
+            ),
+            [jax.ShapeDtypeStruct((share, width), jnp.float32)],
+            [*early_rows[first : first + count], units, *total],
+            "weight_rest" if first else "weight_first",
+        )
+    total = total[0]
 
     rows, grads, total, near_returned = lax.optimization_barrier(
         (last_rows, grads, total, returned[:2])

time: 57.6 us -> 57.5 us (level)
  waiting for transfers between devices: 23.4 us -> 22.8 us
    ppermute x20, waiting for transfers between devices: 23.4 us -> 22.8 us  [swap(): return lax.ppermute(value, axis, [(i, i ^ step) for i in range(n)])]
    pallas_call x10 -> x11, Pallas kernels: 9.76 us -> 10.3 us  [kernel_call(): pl.pallas_call(kernel, out_shape=outs, compiler_params=pltpu.CompilerPara...]
  transfers between devices with their start and end apart: 20 -> 20, of which waited for: 9 -> 9; matrix products, arithmetic and copies ran while one was open for 0% -> 0% of each run, Pallas kernels for 15% -> 16%
where the time goes in v8:
time: 57.5 us; the launch traced here: 57.3 us
  waiting for transfers between devices  22.8 us (40%)
  starting transfers between devices  21.7 us (38%)
  Pallas kernels  10.3 us (18%)
  local copies, waits for them, and re-layouts  1.56 us (3%)
  between operations  0.77 us (1%)
    ppermute x20, waiting for transfers between devices, swap(): return lax.ppermute(value, axis, [(i, i ^ step) for i in range(n)])  22.8 us
    ppermute x20, starting transfers between devices, swap(): return lax.ppermute(value, axis, [(i, i ^ step) for i in range(n)])  21.7 us
    pallas_call x11, Pallas kernels, kernel_call(): pl.pallas_call(kernel, out_shape=outs, compiler_params=pltpu.CompilerPara...  10.3 us
    unnamed x12, local copies, waits for them, and re-layouts  1.53 us
  transfers between devices with their start and end apart: 20, of which 9 were waited for; matrix products, arithmetic and copies ran while one was open for 0% of the time, Pallas kernels for 16%

profile of v8, /device:TPU:0, one launch (start us, length us, event | category | flops | bytes accessed | tf_op | source)
XLA Modules:
  0.0 57.3 jit_solution(10111539051882391386)
XLA Ops:
  0.6 0.5 collective-permute-start
  1.1 0.1 collective-permute-start.1
  1.2 0.0 slice-start
  1.2 0.0 copy-start.1
  1.2 0.0 copy-start.2
  1.2 0.0 copy-start
  1.2 0.0 slice-start.1
  1.2 0.5 collective-permute-start.2
  1.7 1.5 %copy-done.3 = bf16[128,4096]{1,0:T(8,128)(2,1)S(1)} copy-done((bf16[128,4096]{1,0:T(8,128)(2,1)S(1)}, bf16[128,4096]{1,0:T(8,128)(2,1)}, u32[]{:S(2)}) %copy-start.3) | copy-done | bytes 1048600
  3.3 0.1 own_rows.1.refs_0_
  3.3 0.3 collective-permute-done.1.refs_3_
  3.6 0.0 collective-permute-done.2.refs_5_
  3.7 0.0 collective-permute-done.refs_1_
  3.7 0.0 copy-done.1
  3.7 0.0 copy-done.2
  3.7 0.7 %place.1 = (bf16[4,48,1024]{2,1,0:T(8,128)(2,1)S(1)}, bf16[4,48,1024]{2,1,0:T(8,128)(2,1)S(1)}, bf16[4,48,1024]{2,1,0:T(8,128)(2,1)S(1)}, bf16[4,48,1024]{2,1,0:...) custom-call(bf16[128,4096]{1,0:T(8,128)(2,1)S(1)} %own_rows.1.refs_0_, ...), custom_call_target="tpu_custom_call" | custom-call | flops 1024 | bytes 1024 | tf_op jit(solution)/shard_map/place/pallas_call | solution.py:22
  4.4 3.0 %collective-permute-start.3 = (bf16[4,48,1024]{2,1,0:T(8,128)(2,1)S(1)}, bf16[4,48,1024]{2,1,0:T(8,128)(2,1)S(1)}, u32[]{:S(2)}, u32[]{:S(2)}) collective-permute-start(bf16[4,48,1024]{2,1,0:T(8,128)(2,1)S(1)} %get-tuple-element.48), channel_id=1, source_target_pairs={{0,2},{1,3},{2,0},{3,1},{4,6},{5,7},{6,4},{7,5},{8,10},{9,11},{10,... | collective-permute-start | bytes 1179656 | tf_op jit(solution)/shard_map/ppermute | solution.py:16
  7.4 2.5 %collective-permute-start.4 = (bf16[4,48,1024]{2,1,0:T(8,128)(2,1)S(1)}, bf16[4,48,1024]{2,1,0:T(8,128)(2,1)S(1)}, u32[]{:S(2)}, u32[]{:S(2)}) collective-permute-start(bf16[4,48,1024]{2,1,0:T(8,128)(2,1)S(1)} %get-tuple-element.49), channel_id=1, source_target_pairs={{0,6},{1,7},{2,4},{3,5},{4,2},{5,3},{6,0},{7,1},{8,14},{9,15},{10,... | collective-permute-start | bytes 1179656 | tf_op jit(solution)/shard_map/ppermute | solution.py:16
  9.9 0.0 copy-done
  9.9 0.2 hidden.1.refs_3_
  10.1 1.5 %collective-permute-start.7 = (bf16[4,48,768]{2,1,0:T(8,128)(2,1)S(1)}, bf16[4,48,768]{2,1,0:T(8,128)(2,1)S(1)}, u32[]{:S(2)}, u32[]{:S(2)}) collective-permute-start(bf16[4,48,768]{2,1,0:T(8,128)(2,1)S(1)} %hidden.1.refs_3_), channel_id=1, source_target_pairs={{0,8},{8,0},{16,24},{24,16},{1,9},{9,1},{17,25},{25,17},{2,10},{10... | collective-permute-start | bytes 884744 | tf_op jit(solution)/shard_map/ppermute | solution.py:16
  11.6 1.5 %collective-permute-start.6 = (bf16[4,48,768]{2,1,0:T(8,128)(2,1)S(1)}, bf16[4,48,768]{2,1,0:T(8,128)(2,1)S(1)}, u32[]{:S(2)}, u32[]{:S(2)}) collective-permute-start(bf16[4,48,768]{2,1,0:T(8,128)(2,1)S(1)} %hidden.1.refs_3_), channel_id=1, source_target_pairs={{0,16},{8,24},{16,0},{24,8},{1,17},{9,25},{17,1},{25,9},{2,18},{10... | collective-permute-start | bytes 884744 | tf_op jit(solution)/shard_map/ppermute | solution.py:16
  13.1 0.5 collective-permute-start.5
  13.6 6.4 %collective-permute-done.7.refs_2_ = bf16[4,48,768]{2,1,0:T(8,128)(2,1)S(1)} collective-permute-done((bf16[4,48,768]{2,1,0:T(8,128)(2,1)S(1)}, bf16[4,48,768]{2,1,0:T(8,128)(2,1)S(1)}, u32[]{:S(2)}, u32[]{:S(2)}) %collective-permute-start.7) | collective-permute-done | bytes 294944 | tf_op jit(solution)/shard_map/ppermute | solution.py:16
  20.1 6.1 %collective-permute-done.6.refs_1_ = bf16[4,48,768]{2,1,0:T(8,128)(2,1)S(1)} collective-permute-done((bf16[4,48,768]{2,1,0:T(8,128)(2,1)S(1)}, bf16[4,48,768]{2,1,0:T(8,128)(2,1)S(1)}, u32[]{:S(2)}, u32[]{:S(2)}) %collective-permute-start.6) | collective-permute-done | bytes 294944 | tf_op jit(solution)/shard_map/ppermute | solution.py:16
  26.2 0.0 collective-permute-done.5.refs_0_
  26.2 0.1 units.1
  26.2 0.0 collective-permute-done.3.refs_1_
  26.2 1.3 %collective-permute-done.4.refs_2_ = bf16[4,48,1024]{2,1,0:T(8,128)(2,1)S(1)} collective-permute-done((bf16[4,48,1024]{2,1,0:T(8,128)(2,1)S(1)}, bf16[4,48,1024]{2,1,0:T(8,128)(2,1)S(1)}, u32[]{:S(2)}, u32[]{:S(2)}) %collective-permute-start.4) | collective-permute-done | bytes 393248 | tf_op jit(solution)/shard_map/ppermute | solution.py:16
  27.5 1.8 %collective-permute-start.8 = (bf16[4,48,1024]{2,1,0:T(8,128)(2,1)S(1)}, bf16[4,48,1024]{2,1,0:T(8,128)(2,1)S(1)}, u32[]{:S(2)}, u32[]{:S(2)}) collective-permute-start(bf16[4,48,1024]{2,1,0:T(8,128)(2,1)S(1)} %get-tuple-element.54), channel_id=1, source_target_pairs={{0,4},{1,5},{2,6},{3,7},{4,0},{5,1},{6,2},{7,3},{8,12},{9,13},{10,... | collective-permute-start | bytes 1179656 | tf_op jit(solution)/shard_map/ppermute | solution.py:16
  29.3 0.1 stack.1
  29.4 1.6 %collective-permute-start.11 = (bf16[144,1024]{1,0:T(8,128)(2,1)S(1)}, bf16[144,1024]{1,0:T(8,128)(2,1)S(1)}, u32[]{:S(2)}, u32[]{:S(2)}) collective-permute-start(bf16[144,1024]{1,0:T(8,128)(2,1)S(1)} %get-tuple-element.63), channel_id=1, source_target_pairs={{0,8},{8,0},{16,24},{24,16},{1,9},{9,1},{17,25},{25,17},{2,10},{10... | collective-permute-start | bytes 884744 | tf_op jit(solution)/shard_map/ppermute | solution.py:16
  30.9 1.5 %collective-permute-start.9 = (bf16[144,1024]{1,0:T(8,128)(2,1)S(1)}, bf16[144,1024]{1,0:T(8,128)(2,1)S(1)}, u32[]{:S(2)}, u32[]{:S(2)}) collective-permute-start(bf16[144,1024]{1,0:T(8,128)(2,1)S(1)} %get-tuple-element.59), channel_id=1, source_target_pairs={{0,16},{8,24},{16,0},{24,8},{1,17},{9,25},{17,1},{25,9},{2,18},{10... | collective-permute-start | bytes 884744 | tf_op jit(solution)/shard_map/ppermute | solution.py:16
  32.4 0.5 collective-permute-start.10
  32.9 0.0 slice-done
  32.9 0.0 slice-done.1
  32.9 2.7 %pull_early.1 = (bf16[4,48,1536]{2,1,0:T(8,128)(2,1)}, f32[1,48]{1,0:T(1,128)S(1)}, f32[1,48]{1,0:T(1,128)S(1)}, f32[1,48]{1,0:T(1,128)S(1)}) custom-call(bf16[4,48,1024]{2,1,0:T(8,128)(2,1)S(1)} %get-tuple-element.55.refs_0_, bf16[4,48,1024]{2,1,0:T(8,128)(2,1)S(1)} %collective-permute-done.3.refs_1_, ...), custom_call_target="tpu_custom_call" | custom-call | flops 1024 | bytes 1024 | tf_op jit(solution)/shard_map/pull_early/pallas_call | solution.py:22
  35.7 0.3 collective-permute-start.12
  36.0 3.4 %collective-permute-done.11.refs_1_ = bf16[144,1024]{1,0:T(8,128)(2,1)S(1)} collective-permute-done((bf16[144,1024]{1,0:T(8,128)(2,1)S(1)}, bf16[144,1024]{1,0:T(8,128)(2,1)S(1)}, u32[]{:S(2)}, u32[]{:S(2)}) %collective-permute-start.11) | collective-permute-done | bytes 294944 | tf_op jit(solution)/shard_map/ppermute | solution.py:16
  39.4 1.0 %collective-permute-start.13 = (f32[1,48]{1,0:T(1,128)S(1)}, f32[1,48]{1,0:T(1,128)S(1)}, u32[]{:S(2)}, u32[]{:S(2)}) collective-permute-start(f32[1,48]{1,0:T(1,128)S(1)} %get-tuple-element.70), channel_id=1, source_target_pairs={{0,6},{1,7},{2,4},{3,5},{4,2},{5,3},{6,0},{7,1},{8,14},{9,15},{10,... | collective-permute-start | bytes 584 | tf_op jit(solution)/shard_map/ppermute | solution.py:16
  40.3 1.0 %weight_first.1.refs_3_ = f32[1024,768]{1,0:T(8,128)S(1)} custom-call(bf16[144,1024]{1,0:T(8,128)(2,1)S(1)} %get-tuple-element.62.refs_0_, bf16[144,1024]{1,0:T(8,128)(2,1)S(1)} %collective-permute-done.11.refs_1_, bf16[576,768]{1,0:T(8,128)(2,1)S(1)} %get-tuple-element.61.refs_2_), custom_call_target="tpu_custom_call" | custom-call | flops 1024 | bytes 1024 | tf_op jit(solution)/shard_map/weight_first/pallas_call | solution.py:22
  41.4 3.2 %collective-permute-done.9.refs_0_ = bf16[144,1024]{1,0:T(8,128)(2,1)S(1)} collective-permute-done((bf16[144,1024]{1,0:T(8,128)(2,1)S(1)}, bf16[144,1024]{1,0:T(8,128)(2,1)S(1)}, u32[]{:S(2)}, u32[]{:S(2)}) %collective-permute-start.9) | collective-permute-done | bytes 294944 | tf_op jit(solution)/shard_map/ppermute | solution.py:16
  44.6 0.0 collective-permute-done.10.refs_1_
  44.6 1.0 %weight_rest.1.refs_5_ = f32[1024,768]{1,0:T(8,128)S(1)} custom-call(bf16[144,1024]{1,0:T(8,128)(2,1)S(1)} %collective-permute-done.9.refs_0_, bf16[144,1024]{1,0:T(8,128)(2,1)S(1)} %collective-permute-done.10.refs_1_, bf16[576,768]{1,0:T(8,128)(2,1)S(1)} %get-tuple-element.61.refs_2_, f32[1024,768]{1,0:T(8,128)S(1)} %weight_first.1.refs_3_), custom_call_target="tpu_custom_call" | custom-call | flops 1024 | bytes 1024 | tf_op jit(solution)/shard_map/weight_rest/pallas_call | solution.py:22
  45.6 0.0 collective-permute-done.12
  45.6 0.2 collective-permute-done.8.refs_0_
  45.9 1.6 %collective-permute-start.18 = (bf16[48,1024]{1,0:T(8,128)(2,1)S(1)}, bf16[48,1024]{1,0:T(8,128)(2,1)S(1)}, u32[]{:S(2)}, u32[]{:S(2)}) collective-permute-start(bf16[48,1024]{1,0:T(8,128)(2,1)S(1)} %get-tuple-element.94), channel_id=1, source_target_pairs={{0,8},{8,0},{16,24},{24,16},{1,9},{9,1},{17,25},{25,17},{2,10},{10... | collective-permute-start | bytes 294920 | tf_op jit(solution)/shard_map/ppermute | solution.py:16
  47.4 1.5 %collective-permute-start.17 = (bf16[48,1024]{1,0:T(8,128)(2,1)S(1)}, bf16[48,1024]{1,0:T(8,128)(2,1)S(1)}, u32[]{:S(2)}, u32[]{:S(2)}) collective-permute-start(bf16[48,1024]{1,0:T(8,128)(2,1)S(1)} %get-tuple-element.95), channel_id=1, source_target_pairs={{0,16},{8,24},{16,0},{24,8},{1,17},{9,25},{17,1},{25,9},{2,18},{10... | collective-permute-start | bytes 294920 | tf_op jit(solution)/shard_map/ppermute | solution.py:16
  49.0 0.5 collective-permute-start.16
  49.4 0.0 collective-permute-done.13
  49.4 0.1 pad_maximum_fusion
  49.5 0.1 select_reduce_fusion
  49.6 1.6 %pull_last.1 = (f32[48,768]{1,0:T(8,128)S(1)}, f32[1,24]{1,0:T(1,128)S(1)}, f32[1,24]{1,0:T(1,128)S(1)}) custom-call(bf16[4,48,1024]{2,1,0:T(8,128)(2,1)S(1)} %collective-permute-done.8.refs_0_, bf16[1,4096,768]{2,1,0:T(8,128)(2,1)S(1)} %bitcast.21, bf16[4,48,1536]{2,1,0:T(8,128)(2,1)S(1)} %bitcast.24), custom_call_target="tpu_custom_call" | custom-call | flops 1024 | bytes 1024 | tf_op jit(solution)/shard_map/pull_last/pallas_call | solution.py:22
  51.2 1.3 %collective-permute-start.14 = (f32[1,24]{1,0:T(1,128)S(1)}, f32[1,24]{1,0:T(1,128)S(1)}, u32[]{:S(2)}, u32[]{:S(2)}) collective-permute-start(f32[1,24]{1,0:T(1,128)S(1)} %get-tuple-element.72), channel_id=1, source_target_pairs={{0,4},{1,5},{2,6},{3,7},{4,0},{5,1},{6,2},{7,3},{8,12},{9,13},{10,... | collective-permute-start | bytes 296 | tf_op jit(solution)/shard_map/ppermute | solution.py:16
  52.5 0.2 collective-permute-start.15
  52.6 0.0 collective-permute-done.18.refs_2_
  52.6 0.5 collective-permute-done.17.refs_1_
  53.1 1.4 %collective-permute-done.16.refs_0_ = bf16[48,1024]{1,0:T(8,128)(2,1)S(1)} collective-permute-done((bf16[48,1024]{1,0:T(8,128)(2,1)S(1)}, bf16[48,1024]{1,0:T(8,128)(2,1)S(1)}, u32[]{:S(2)}, u32[]{:S(2)}) %collective-permute-start.16) | collective-permute-done | bytes 98336 | tf_op jit(solution)/shard_map/ppermute | solution.py:16
  54.5 0.0 collective-permute-start.19
  54.5 2.1 %finish.1 = (f32[1,1024,768]{2,1,0:T(8,128)}, bf16[4,48,1536]{2,1,0:T(8,128)(2,1)}) custom-call(bf16[48,1024]{1,0:T(8,128)(2,1)S(1)} %collective-permute-done.16.refs_0_, bf16[48,1024]{1,0:T(8,128)(2,1)S(1)} %collective-permute-done.17.refs_1_, bf16[48,1024]{1,0:T(8,128)(2,1)S(1)} %collective-permute-done.18.refs_2_, ...), custom_call_target="tpu_custom_call", output_to_operand_aliasing={{1}: (8, {})} | custom-call | flops 10000000000 | bytes 1024 | tf_op jit(solution)/shard_map/finish/pallas_call | solution.py:22
  56.6 0.0 collective-permute-done.14.same
  56.6 0.0 collective-permute-done.15.other
  56.6 0.0 collective-permute-done.19.sib
  56.6 0.7 %token_.1 = f32[1,128]{1,0:T(1,128)} custom-call(f32[1,24]{1,0:T(1,128)S(1)} %collective-permute-done.14.same, f32[1,24]{1,0:T(1,128)S(1)} %collective-permute-done.15.other, s32[1,128]{1,0:T(1,128)S(1)} %get-tuple-element.88.last_slots, f32[1,128]{1,0:T(1,128)S(1)} %bitcast.29, f32[1,128]{1,0:T(1,128)S(1)} %collective-permute-done.19.sib, f32[1,128]{1,0:T(1,128)S(1)} %bitcast.28), custom_call_target="tpu_custom_call" | custom-call | flops 1024 | bytes 1024 | tf_op jit(solution)/shard_map/token/pallas_call | solution.py:22
  (4 shorter events, 0.0 us)
Async XLA Ops:
  0.6 3.0 %collective-permute-start = (bf16[128,4096]{1,0:T(8,128)(2,1)}, bf16[128,4096]{1,0:T(8,128)(2,1)S(1)}, u32[]{:S(2)}, u32[]{:S(2)}) collective-permute-start(bf16[128,4096]{1,0:T(8,128)(2,1)} %rows.1), channel_id=1, source_target_pairs={{0,1},{1,0},{2,3},{3,2},{4,5},{5,4},{6,7},{7,6},{8,9},{9,8},{10,11... | collective-permute-start | bytes 3145736 | tf_op jit(solution)/shard_map/ppermute | solution.py:16
  1.1 2.5 %collective-permute-start.1 = (s32[1,128]{1,0:T(1,128)}, s32[1,128]{1,0:T(1,128)S(1)}, u32[]{:S(2)}, u32[]{:S(2)}) collective-permute-start(s32[1,128]{1,0:T(1,128)} %bitcast.30), channel_id=1, source_target_pairs={{0,1},{1,0},{2,3},{3,2},{4,5},{5,4},{6,7},{7,6},{8,9},{9,8},{10,11... | collective-permute-start | bytes 1544 | tf_op jit(solution)/shard_map/ppermute | solution.py:16
  1.2 31.7 %slice-start = ((s8[6291456]{0:T(1024)(128)(4,1)}), s8[4194304]{0:T(1024)(128)(4,1)S(1)}, s32[]{:S(2)}) async-start(s8[6291456]{0:T(1024)(128)(4,1)} %bitcast.20), calls=%async_computation | async-start | bytes 8388608
  1.2 2.4 %copy-start.1 = (f32[128,1]{0,1:T(1,128)S(1)}, f32[128,1]{0,1:T(1,128)}, u32[]{:S(2)}) copy-start(f32[128,1]{0,1:T(1,128)} %param.7) | copy-start | bytes 1540
  1.2 2.4 %copy-start.2 = (s32[128,1]{0,1:T(1,128)S(1)}, s32[128,1]{0,1:T(1,128)}, u32[]{:S(2)}) copy-start(s32[128,1]{0,1:T(1,128)} %param.6) | copy-start | bytes 1540
  1.2 8.6 %copy-start = (bf16[1,1,192,1536]{3,2,1,0:T(8,128)(2,1)S(1)}, bf16[1,1,192,1536]{3,2,1,0:T(8,128)(2,1)}, u32[]{:S(2)}) copy-start(bf16[1,1,192,1536]{3,2,1,0:T(8,128)(2,1)} %param.9) | copy-start | bytes 1769476
  1.2 31.7 %slice-start.1 = ((s8[6291456]{0:T(1024)(128)(4,1)}), s8[2097152]{0:T(1024)(128)(4,1)S(1)}, s32[]{:S(2)}) async-start(s8[6291456]{0:T(1024)(128)(4,1)} %bitcast.20), calls=%async_computation.1 | async-start | bytes 4194304
  1.2 2.4 %collective-permute-start.2 = (f32[1,128]{1,0:T(1,128)}, f32[1,128]{1,0:T(1,128)S(1)}, u32[]{:S(2)}, u32[]{:S(2)}) collective-permute-start(f32[1,128]{1,0:T(1,128)} %bitcast.26), channel_id=1, source_target_pairs={{0,1},{1,0},{2,3},{3,2},{4,5},{5,4},{6,7},{7,6},{8,9},{9,8},{10,11... | collective-permute-start | bytes 1544 | tf_op jit(solution)/shard_map/ppermute | solution.py:16
  1.7 1.5 %copy-start.3 = (bf16[128,4096]{1,0:T(8,128)(2,1)S(1)}, bf16[128,4096]{1,0:T(8,128)(2,1)}, u32[]{:S(2)}) copy-start(bf16[128,4096]{1,0:T(8,128)(2,1)} %rows.1) | copy-start | bytes 3145732
  4.4 21.9 %collective-permute-start.3 = (bf16[4,48,1024]{2,1,0:T(8,128)(2,1)S(1)}, bf16[4,48,1024]{2,1,0:T(8,128)(2,1)S(1)}, u32[]{:S(2)}, u32[]{:S(2)}) collective-permute-start(bf16[4,48,1024]{2,1,0:T(8,128)(2,1)S(1)} %get-tuple-element.48), channel_id=1, source_target_pairs={{0,2},{1,3},{2,0},{3,1},{4,6},{5,7},{6,4},{7,5},{8,10},{9,11},{10,... | collective-permute-start | bytes 1179656 | tf_op jit(solution)/shard_map/ppermute | solution.py:16
  7.4 20.1 %collective-permute-start.4 = (bf16[4,48,1024]{2,1,0:T(8,128)(2,1)S(1)}, bf16[4,48,1024]{2,1,0:T(8,128)(2,1)S(1)}, u32[]{:S(2)}, u32[]{:S(2)}) collective-permute-start(bf16[4,48,1024]{2,1,0:T(8,128)(2,1)S(1)} %get-tuple-element.49), channel_id=1, source_target_pairs={{0,6},{1,7},{2,4},{3,5},{4,2},{5,3},{6,0},{7,1},{8,14},{9,15},{10,... | collective-permute-start | bytes 1179656 | tf_op jit(solution)/shard_map/ppermute | solution.py:16
  10.1 10.0 %collective-permute-start.7 = (bf16[4,48,768]{2,1,0:T(8,128)(2,1)S(1)}, bf16[4,48,768]{2,1,0:T(8,128)(2,1)S(1)}, u32[]{:S(2)}, u32[]{:S(2)}) collective-permute-start(bf16[4,48,768]{2,1,0:T(8,128)(2,1)S(1)} %hidden.1.refs_3_), channel_id=1, source_target_pairs={{0,8},{8,0},{16,24},{24,16},{1,9},{9,1},{17,25},{25,17},{2,10},{10... | collective-permute-start | bytes 884744 | tf_op jit(solution)/shard_map/ppermute | solution.py:16
  11.6 14.5 %collective-permute-start.6 = (bf16[4,48,768]{2,1,0:T(8,128)(2,1)S(1)}, bf16[4,48,768]{2,1,0:T(8,128)(2,1)S(1)}, u32[]{:S(2)}, u32[]{:S(2)}) collective-permute-start(bf16[4,48,768]{2,1,0:T(8,128)(2,1)S(1)} %hidden.1.refs_3_), channel_id=1, source_target_pairs={{0,16},{8,24},{16,0},{24,8},{1,17},{9,25},{17,1},{25,9},{2,18},{10... | collective-permute-start | bytes 884744 | tf_op jit(solution)/shard_map/ppermute | solution.py:16
  13.1 13.0 %collective-permute-start.5 = (bf16[4,48,768]{2,1,0:T(8,128)(2,1)S(1)}, bf16[4,48,768]{2,1,0:T(8,128)(2,1)S(1)}, u32[]{:S(2)}, u32[]{:S(2)}) collective-permute-start(bf16[4,48,768]{2,1,0:T(8,128)(2,1)S(1)} %hidden.1.refs_3_), channel_id=1, source_target_pairs={{0,24},{8,16},{16,8},{24,0},{1,25},{9,17},{17,9},{25,1},{2,26},{10... | collective-permute-start | bytes 884744 | tf_op jit(solution)/shard_map/ppermute | solution.py:16
  27.5 18.3 %collective-permute-start.8 = (bf16[4,48,1024]{2,1,0:T(8,128)(2,1)S(1)}, bf16[4,48,1024]{2,1,0:T(8,128)(2,1)S(1)}, u32[]{:S(2)}, u32[]{:S(2)}) collective-permute-start(bf16[4,48,1024]{2,1,0:T(8,128)(2,1)S(1)} %get-tuple-element.54), channel_id=1, source_target_pairs={{0,4},{1,5},{2,6},{3,7},{4,0},{5,1},{6,2},{7,3},{8,12},{9,13},{10,... | collective-permute-start | bytes 1179656 | tf_op jit(solution)/shard_map/ppermute | solution.py:16
  29.4 10.0 %collective-permute-start.11 = (bf16[144,1024]{1,0:T(8,128)(2,1)S(1)}, bf16[144,1024]{1,0:T(8,128)(2,1)S(1)}, u32[]{:S(2)}, u32[]{:S(2)}) collective-permute-start(bf16[144,1024]{1,0:T(8,128)(2,1)S(1)} %get-tuple-element.63), channel_id=1, source_target_pairs={{0,8},{8,0},{16,24},{24,16},{1,9},{9,1},{17,25},{25,17},{2,10},{10... | collective-permute-start | bytes 884744 | tf_op jit(solution)/shard_map/ppermute | solution.py:16
  30.9 13.7 %collective-permute-start.9 = (bf16[144,1024]{1,0:T(8,128)(2,1)S(1)}, bf16[144,1024]{1,0:T(8,128)(2,1)S(1)}, u32[]{:S(2)}, u32[]{:S(2)}) collective-permute-start(bf16[144,1024]{1,0:T(8,128)(2,1)S(1)} %get-tuple-element.59), channel_id=1, source_target_pairs={{0,16},{8,24},{16,0},{24,8},{1,17},{9,25},{17,1},{25,9},{2,18},{10... | collective-permute-start | bytes 884744 | tf_op jit(solution)/shard_map/ppermute | solution.py:16
  32.4 12.1 %collective-permute-start.10 = (bf16[144,1024]{1,0:T(8,128)(2,1)S(1)}, bf16[144,1024]{1,0:T(8,128)(2,1)S(1)}, u32[]{:S(2)}, u32[]{:S(2)}) collective-permute-start(bf16[144,1024]{1,0:T(8,128)(2,1)S(1)} %get-tuple-element.60), channel_id=1, source_target_pairs={{0,24},{8,16},{16,8},{24,0},{1,25},{9,17},{17,9},{25,1},{2,26},{10... | collective-permute-start | bytes 884744 | tf_op jit(solution)/shard_map/ppermute | solution.py:16
  35.7 9.9 %collective-permute-start.12 = (f32[1,48]{1,0:T(1,128)S(1)}, f32[1,48]{1,0:T(1,128)S(1)}, u32[]{:S(2)}, u32[]{:S(2)}) collective-permute-start(f32[1,48]{1,0:T(1,128)S(1)} %get-tuple-element.65), channel_id=1, source_target_pairs={{0,2},{1,3},{2,0},{3,1},{4,6},{5,7},{6,4},{7,5},{8,10},{9,11},{10,... | collective-permute-start | bytes 584 | tf_op jit(solution)/shard_map/ppermute | solution.py:16
  39.4 10.0 %collective-permute-start.13 = (f32[1,48]{1,0:T(1,128)S(1)}, f32[1,48]{1,0:T(1,128)S(1)}, u32[]{:S(2)}, u32[]{:S(2)}) collective-permute-start(f32[1,48]{1,0:T(1,128)S(1)} %get-tuple-element.70), channel_id=1, source_target_pairs={{0,6},{1,7},{2,4},{3,5},{4,2},{5,3},{6,0},{7,1},{8,14},{9,15},{10,... | collective-permute-start | bytes 584 | tf_op jit(solution)/shard_map/ppermute | solution.py:16
  45.9 6.8 %collective-permute-start.18 = (bf16[48,1024]{1,0:T(8,128)(2,1)S(1)}, bf16[48,1024]{1,0:T(8,128)(2,1)S(1)}, u32[]{:S(2)}, u32[]{:S(2)}) collective-permute-start(bf16[48,1024]{1,0:T(8,128)(2,1)S(1)} %get-tuple-element.94), channel_id=1, source_target_pairs={{0,8},{8,0},{16,24},{24,16},{1,9},{9,1},{17,25},{25,17},{2,10},{10... | collective-permute-start | bytes 294920 | tf_op jit(solution)/shard_map/ppermute | solution.py:16
  47.4 5.7 %collective-permute-start.17 = (bf16[48,1024]{1,0:T(8,128)(2,1)S(1)}, bf16[48,1024]{1,0:T(8,128)(2,1)S(1)}, u32[]{:S(2)}, u32[]{:S(2)}) collective-permute-start(bf16[48,1024]{1,0:T(8,128)(2,1)S(1)} %get-tuple-element.95), channel_id=1, source_target_pairs={{0,16},{8,24},{16,0},{24,8},{1,17},{9,25},{17,1},{25,9},{2,18},{10... | collective-permute-start | bytes 294920 | tf_op jit(solution)/shard_map/ppermute | solution.py:16
  49.0 5.5 %collective-permute-start.16 = (bf16[48,1024]{1,0:T(8,128)(2,1)S(1)}, bf16[48,1024]{1,0:T(8,128)(2,1)S(1)}, u32[]{:S(2)}, u32[]{:S(2)}) collective-permute-start(bf16[48,1024]{1,0:T(8,128)(2,1)S(1)} %get-tuple-element.96), channel_id=1, source_target_pairs={{0,24},{8,16},{16,8},{24,0},{1,25},{9,17},{17,9},{25,1},{2,26},{10... | collective-permute-start | bytes 294920 | tf_op jit(solution)/shard_map/ppermute | solution.py:16
  51.2 5.4 %collective-permute-start.14 = (f32[1,24]{1,0:T(1,128)S(1)}, f32[1,24]{1,0:T(1,128)S(1)}, u32[]{:S(2)}, u32[]{:S(2)}) collective-permute-start(f32[1,24]{1,0:T(1,128)S(1)} %get-tuple-element.72), channel_id=1, source_target_pairs={{0,4},{1,5},{2,6},{3,7},{4,0},{5,1},{6,2},{7,3},{8,12},{9,13},{10,... | collective-permute-start | bytes 296 | tf_op jit(solution)/shard_map/ppermute | solution.py:16
  52.5 4.1 %collective-permute-start.15 = (f32[1,24]{1,0:T(1,128)S(1)}, f32[1,24]{1,0:T(1,128)S(1)}, u32[]{:S(2)}, u32[]{:S(2)}) collective-permute-start(f32[1,24]{1,0:T(1,128)S(1)} %get-tuple-element.73), channel_id=1, source_target_pairs={{0,5},{1,4},{2,7},{3,6},{4,1},{5,0},{6,3},{7,2},{8,13},{9,12},{10,... | collective-permute-start | bytes 296 | tf_op jit(solution)/shard_map/ppermute | solution.py:16
  54.5 2.1 %collective-permute-start.19 = (f32[1,128]{1,0:T(1,128)S(1)}, f32[1,128]{1,0:T(1,128)S(1)}, u32[]{:S(2)}, u32[]{:S(2)}) collective-permute-start(f32[1,128]{1,0:T(1,128)S(1)} %bitcast.34), channel_id=1, source_target_pairs={{0,1},{1,0},{2,3},{3,2},{4,5},{5,4},{6,7},{7,6},{8,9},{9,8},{10,11... | collective-permute-start | bytes 1544 | tf_op jit(solution)/shard_map/ppermute | solution.py:16

commit v9 on v8

--- a/solution.py
+++ b/solution.py
@@ -169,7 +169,7 @@
 
 
 def finish_kernel(step, replicas, parts, *refs):
-    rows = refs[:replicas][::-1]
+    rows = refs[:replicas]
     units, early, pulled, saved, _, out, grads, held, held_grads, sems = refs[replicas:]
     size = early.shape[0] // parts
     copies = []
@@ -315,8 +315,7 @@
         "pull_last",
     )
     returned_last = [swap(routers[i], "exp", 2 * last + i) for i in range(2)]
-    late_rows, sum_sib = lax.optimization_barrier((late_rows[::-1], sums[1]))
-    late_rows = late_rows[::-1]
+    late_rows, sum_sib = lax.optimization_barrier((late_rows, sums[1]))
     sum_sib = swap(sum_sib, "exp", 1)
     parts = 4
     weight_grad, grads = kernel_call(
@@ -325,7 +324,7 @@
             jax.ShapeDtypeStruct((1, share, width), jnp.float32),
             jax.ShapeDtypeStruct(saved.shape, jnp.bfloat16),
         ],
-        [*reversed(late_rows), units_last, total, pulled, saved, grads],
+        [*late_rows, units_last, total, pulled, saved, grads],
         "finish",
         LARGE,
         in_specs=[WHOLE_VMEM] * (replicas + 4) + [IN_PLACE],

time: 57.5 us -> 57.3 us (level)
  waiting for transfers between devices: 22.8 us -> 22 us
  starting transfers between devices: 21.7 us -> 22.3 us
    ppermute x20, waiting for transfers between devices: 22.8 us -> 22 us  [swap(): return lax.ppermute(value, axis, [(i, i ^ step) for i in range(n)])]
    ppermute x20, starting transfers between devices: 21.7 us -> 22.3 us  [swap(): return lax.ppermute(value, axis, [(i, i ^ step) for i in range(n)])]
where the time goes in v9:
time: 57.3 us; the launch traced here: 57.2 us
  starting transfers between devices  22.3 us (39%)
  waiting for transfers between devices  22 us (38%)
  Pallas kernels  10.3 us (18%)
  local copies, waits for them, and re-layouts  1.56 us (3%)
  between operations  0.77 us (1%)
    ppermute x20, starting transfers between devices, swap(): return lax.ppermute(value, axis, [(i, i ^ step) for i in range(n)])  22.3 us
    ppermute x20, waiting for transfers between devices, swap(): return lax.ppermute(value, axis, [(i, i ^ step) for i in range(n)])  22 us
    pallas_call x11, Pallas kernels, kernel_call(): pl.pallas_call(kernel, out_shape=outs, compiler_params=pltpu.CompilerPara...  10.3 us
    unnamed x12, local copies, waits for them, and re-layouts  1.53 us
  transfers between devices with their start and end apart: 20, of which 9 were waited for; matrix products, arithmetic and copies ran while one was open for 0% of the time, Pallas kernels for 16%

profile of v9, /device:TPU:0, one launch (start us, length us, event | category | flops | bytes accessed | tf_op | source)
XLA Modules:
  0.0 57.2 jit_solution(473214676182323469)
XLA Ops:
  0.6 0.5 collective-permute-start
  1.1 0.1 collective-permute-start.1
  1.2 0.0 slice-start
  1.2 0.0 copy-start.1
  1.2 0.0 copy-start.2
  1.2 0.0 copy-start
  1.2 0.0 slice-start.1
  1.2 0.5 collective-permute-start.2
  1.7 1.5 %copy-done.3 = bf16[128,4096]{1,0:T(8,128)(2,1)S(1)} copy-done((bf16[128,4096]{1,0:T(8,128)(2,1)S(1)}, bf16[128,4096]{1,0:T(8,128)(2,1)}, u32[]{:S(2)}) %copy-start.3) | copy-done | bytes 1048600
  3.3 0.1 own_rows.1.refs_0_
  3.3 0.3 collective-permute-done.1.refs_3_
  3.6 0.0 collective-permute-done.2.refs_5_
  3.7 0.0 collective-permute-done.refs_1_
  3.7 0.0 copy-done.1
  3.7 0.0 copy-done.2
  3.7 0.7 %place.1 = (bf16[4,48,1024]{2,1,0:T(8,128)(2,1)S(1)}, bf16[4,48,1024]{2,1,0:T(8,128)(2,1)S(1)}, bf16[4,48,1024]{2,1,0:T(8,128)(2,1)S(1)}, bf16[4,48,1024]{2,1,0:...) custom-call(bf16[128,4096]{1,0:T(8,128)(2,1)S(1)} %own_rows.1.refs_0_, ...), custom_call_target="tpu_custom_call" | custom-call | flops 1024 | bytes 1024 | tf_op jit(solution)/shard_map/place/pallas_call | solution.py:22
  4.4 3.0 %collective-permute-start.3 = (bf16[4,48,1024]{2,1,0:T(8,128)(2,1)S(1)}, bf16[4,48,1024]{2,1,0:T(8,128)(2,1)S(1)}, u32[]{:S(2)}, u32[]{:S(2)}) collective-permute-start(bf16[4,48,1024]{2,1,0:T(8,128)(2,1)S(1)} %get-tuple-element.48), channel_id=1, source_target_pairs={{0,2},{1,3},{2,0},{3,1},{4,6},{5,7},{6,4},{7,5},{8,10},{9,11},{10,... | collective-permute-start | bytes 1179656 | tf_op jit(solution)/shard_map/ppermute | solution.py:16
  7.4 2.5 %collective-permute-start.4 = (bf16[4,48,1024]{2,1,0:T(8,128)(2,1)S(1)}, bf16[4,48,1024]{2,1,0:T(8,128)(2,1)S(1)}, u32[]{:S(2)}, u32[]{:S(2)}) collective-permute-start(bf16[4,48,1024]{2,1,0:T(8,128)(2,1)S(1)} %get-tuple-element.49), channel_id=1, source_target_pairs={{0,6},{1,7},{2,4},{3,5},{4,2},{5,3},{6,0},{7,1},{8,14},{9,15},{10,... | collective-permute-start | bytes 1179656 | tf_op jit(solution)/shard_map/ppermute | solution.py:16
  9.9 0.0 copy-done
  9.9 0.2 hidden.1.refs_3_
  10.1 1.5 %collective-permute-start.7 = (bf16[4,48,768]{2,1,0:T(8,128)(2,1)S(1)}, bf16[4,48,768]{2,1,0:T(8,128)(2,1)S(1)}, u32[]{:S(2)}, u32[]{:S(2)}) collective-permute-start(bf16[4,48,768]{2,1,0:T(8,128)(2,1)S(1)} %hidden.1.refs_3_), channel_id=1, source_target_pairs={{0,8},{8,0},{16,24},{24,16},{1,9},{9,1},{17,25},{25,17},{2,10},{10... | collective-permute-start | bytes 884744 | tf_op jit(solution)/shard_map/ppermute | solution.py:16
  11.6 1.5 %collective-permute-start.6 = (bf16[4,48,768]{2,1,0:T(8,128)(2,1)S(1)}, bf16[4,48,768]{2,1,0:T(8,128)(2,1)S(1)}, u32[]{:S(2)}, u32[]{:S(2)}) collective-permute-start(bf16[4,48,768]{2,1,0:T(8,128)(2,1)S(1)} %hidden.1.refs_3_), channel_id=1, source_target_pairs={{0,16},{8,24},{16,0},{24,8},{1,17},{9,25},{17,1},{25,9},{2,18},{10... | collective-permute-start | bytes 884744 | tf_op jit(solution)/shard_map/ppermute | solution.py:16
  13.1 0.5 collective-permute-start.5
  13.6 6.4 %collective-permute-done.7.refs_2_ = bf16[4,48,768]{2,1,0:T(8,128)(2,1)S(1)} collective-permute-done((bf16[4,48,768]{2,1,0:T(8,128)(2,1)S(1)}, bf16[4,48,768]{2,1,0:T(8,128)(2,1)S(1)}, u32[]{:S(2)}, u32[]{:S(2)}) %collective-permute-start.7) | collective-permute-done | bytes 294944 | tf_op jit(solution)/shard_map/ppermute | solution.py:16
  20.1 6.1 %collective-permute-done.6.refs_1_ = bf16[4,48,768]{2,1,0:T(8,128)(2,1)S(1)} collective-permute-done((bf16[4,48,768]{2,1,0:T(8,128)(2,1)S(1)}, bf16[4,48,768]{2,1,0:T(8,128)(2,1)S(1)}, u32[]{:S(2)}, u32[]{:S(2)}) %collective-permute-start.6) | collective-permute-done | bytes 294944 | tf_op jit(solution)/shard_map/ppermute | solution.py:16
  26.2 0.0 collective-permute-done.5.refs_0_
  26.2 0.1 units.1
  26.2 0.0 collective-permute-done.3.refs_1_
  26.2 1.3 %collective-permute-done.4.refs_2_ = bf16[4,48,1024]{2,1,0:T(8,128)(2,1)S(1)} collective-permute-done((bf16[4,48,1024]{2,1,0:T(8,128)(2,1)S(1)}, bf16[4,48,1024]{2,1,0:T(8,128)(2,1)S(1)}, u32[]{:S(2)}, u32[]{:S(2)}) %collective-permute-start.4) | collective-permute-done | bytes 393248 | tf_op jit(solution)/shard_map/ppermute | solution.py:16
  27.5 1.8 %collective-permute-start.8 = (bf16[4,48,1024]{2,1,0:T(8,128)(2,1)S(1)}, bf16[4,48,1024]{2,1,0:T(8,128)(2,1)S(1)}, u32[]{:S(2)}, u32[]{:S(2)}) collective-permute-start(bf16[4,48,1024]{2,1,0:T(8,128)(2,1)S(1)} %get-tuple-element.54), channel_id=1, source_target_pairs={{0,4},{1,5},{2,6},{3,7},{4,0},{5,1},{6,2},{7,3},{8,12},{9,13},{10,... | collective-permute-start | bytes 1179656 | tf_op jit(solution)/shard_map/ppermute | solution.py:16
  29.3 0.1 stack.1
  29.4 1.6 %collective-permute-start.11 = (bf16[144,1024]{1,0:T(8,128)(2,1)S(1)}, bf16[144,1024]{1,0:T(8,128)(2,1)S(1)}, u32[]{:S(2)}, u32[]{:S(2)}) collective-permute-start(bf16[144,1024]{1,0:T(8,128)(2,1)S(1)} %get-tuple-element.63), channel_id=1, source_target_pairs={{0,8},{8,0},{16,24},{24,16},{1,9},{9,1},{17,25},{25,17},{2,10},{10... | collective-permute-start | bytes 884744 | tf_op jit(solution)/shard_map/ppermute | solution.py:16
  30.9 1.5 %collective-permute-start.9 = (bf16[144,1024]{1,0:T(8,128)(2,1)S(1)}, bf16[144,1024]{1,0:T(8,128)(2,1)S(1)}, u32[]{:S(2)}, u32[]{:S(2)}) collective-permute-start(bf16[144,1024]{1,0:T(8,128)(2,1)S(1)} %get-tuple-element.59), channel_id=1, source_target_pairs={{0,16},{8,24},{16,0},{24,8},{1,17},{9,25},{17,1},{25,9},{2,18},{10... | collective-permute-start | bytes 884744 | tf_op jit(solution)/shard_map/ppermute | solution.py:16
  32.4 0.5 collective-permute-start.10
  32.9 0.0 slice-done
  32.9 0.0 slice-done.1
  32.9 2.7 %pull_early.1 = (bf16[4,48,1536]{2,1,0:T(8,128)(2,1)}, f32[1,48]{1,0:T(1,128)S(1)}, f32[1,48]{1,0:T(1,128)S(1)}, f32[1,48]{1,0:T(1,128)S(1)}) custom-call(bf16[4,48,1024]{2,1,0:T(8,128)(2,1)S(1)} %get-tuple-element.55.refs_0_, bf16[4,48,1024]{2,1,0:T(8,128)(2,1)S(1)} %collective-permute-done.3.refs_1_, ...), custom_call_target="tpu_custom_call" | custom-call | flops 1024 | bytes 1024 | tf_op jit(solution)/shard_map/pull_early/pallas_call | solution.py:22
  35.7 0.3 collective-permute-start.12
  36.0 3.4 %collective-permute-done.11.refs_1_ = bf16[144,1024]{1,0:T(8,128)(2,1)S(1)} collective-permute-done((bf16[144,1024]{1,0:T(8,128)(2,1)S(1)}, bf16[144,1024]{1,0:T(8,128)(2,1)S(1)}, u32[]{:S(2)}, u32[]{:S(2)}) %collective-permute-start.11) | collective-permute-done | bytes 294944 | tf_op jit(solution)/shard_map/ppermute | solution.py:16
  39.4 1.0 %collective-permute-start.13 = (f32[1,48]{1,0:T(1,128)S(1)}, f32[1,48]{1,0:T(1,128)S(1)}, u32[]{:S(2)}, u32[]{:S(2)}) collective-permute-start(f32[1,48]{1,0:T(1,128)S(1)} %get-tuple-element.70), channel_id=1, source_target_pairs={{0,6},{1,7},{2,4},{3,5},{4,2},{5,3},{6,0},{7,1},{8,14},{9,15},{10,... | collective-permute-start | bytes 584 | tf_op jit(solution)/shard_map/ppermute | solution.py:16
  40.3 1.0 %weight_first.1.refs_3_ = f32[1024,768]{1,0:T(8,128)S(1)} custom-call(bf16[144,1024]{1,0:T(8,128)(2,1)S(1)} %get-tuple-element.62.refs_0_, bf16[144,1024]{1,0:T(8,128)(2,1)S(1)} %collective-permute-done.11.refs_1_, bf16[576,768]{1,0:T(8,128)(2,1)S(1)} %get-tuple-element.61.refs_2_), custom_call_target="tpu_custom_call" | custom-call | flops 1024 | bytes 1024 | tf_op jit(solution)/shard_map/weight_first/pallas_call | solution.py:22
  41.4 3.2 %collective-permute-done.9.refs_0_ = bf16[144,1024]{1,0:T(8,128)(2,1)S(1)} collective-permute-done((bf16[144,1024]{1,0:T(8,128)(2,1)S(1)}, bf16[144,1024]{1,0:T(8,128)(2,1)S(1)}, u32[]{:S(2)}, u32[]{:S(2)}) %collective-permute-start.9) | collective-permute-done | bytes 294944 | tf_op jit(solution)/shard_map/ppermute | solution.py:16
  44.6 0.0 collective-permute-done.10.refs_1_
  44.6 1.0 %weight_rest.1.refs_5_ = f32[1024,768]{1,0:T(8,128)S(1)} custom-call(bf16[144,1024]{1,0:T(8,128)(2,1)S(1)} %collective-permute-done.9.refs_0_, bf16[144,1024]{1,0:T(8,128)(2,1)S(1)} %collective-permute-done.10.refs_1_, bf16[576,768]{1,0:T(8,128)(2,1)S(1)} %get-tuple-element.61.refs_2_, f32[1024,768]{1,0:T(8,128)S(1)} %weight_first.1.refs_3_), custom_call_target="tpu_custom_call" | custom-call | flops 1024 | bytes 1024 | tf_op jit(solution)/shard_map/weight_rest/pallas_call | solution.py:22
  45.6 0.0 collective-permute-done.12
  45.6 0.2 collective-permute-done.8.refs_0_
  45.9 2.5 %collective-permute-start.18 = (bf16[48,1024]{1,0:T(8,128)(2,1)S(1)}, bf16[48,1024]{1,0:T(8,128)(2,1)S(1)}, u32[]{:S(2)}, u32[]{:S(2)}) collective-permute-start(bf16[48,1024]{1,0:T(8,128)(2,1)S(1)} %get-tuple-element.93), channel_id=1, source_target_pairs={{0,24},{8,16},{16,8},{24,0},{1,25},{9,17},{17,9},{25,1},{2,26},{10... | collective-permute-start | bytes 294920 | tf_op jit(solution)/shard_map/ppermute | solution.py:16
  48.4 0.5 collective-permute-start.17
  48.9 0.5 collective-permute-start.16
  49.4 0.0 collective-permute-done.13
  49.4 0.1 pad_maximum_fusion
  49.5 0.1 select_reduce_fusion
  49.6 1.6 %pull_last.1 = (f32[48,768]{1,0:T(8,128)S(1)}, f32[1,24]{1,0:T(1,128)S(1)}, f32[1,24]{1,0:T(1,128)S(1)}) custom-call(bf16[4,48,1024]{2,1,0:T(8,128)(2,1)S(1)} %collective-permute-done.8.refs_0_, bf16[1,4096,768]{2,1,0:T(8,128)(2,1)S(1)} %bitcast.21, bf16[4,48,1536]{2,1,0:T(8,128)(2,1)S(1)} %bitcast.24), custom_call_target="tpu_custom_call" | custom-call | flops 1024 | bytes 1024 | tf_op jit(solution)/shard_map/pull_last/pallas_call | solution.py:22
  51.2 1.3 %collective-permute-start.14 = (f32[1,24]{1,0:T(1,128)S(1)}, f32[1,24]{1,0:T(1,128)S(1)}, u32[]{:S(2)}, u32[]{:S(2)}) collective-permute-start(f32[1,24]{1,0:T(1,128)S(1)} %get-tuple-element.72), channel_id=1, source_target_pairs={{0,4},{1,5},{2,6},{3,7},{4,0},{5,1},{6,2},{7,3},{8,12},{9,13},{10,... | collective-permute-start | bytes 296 | tf_op jit(solution)/shard_map/ppermute | solution.py:16
  52.5 0.2 collective-permute-start.15
  52.6 0.0 collective-permute-done.18.refs_3_
  52.6 1.0 %collective-permute-done.17.refs_2_ = bf16[48,1024]{1,0:T(8,128)(2,1)S(1)} collective-permute-done((bf16[48,1024]{1,0:T(8,128)(2,1)S(1)}, bf16[48,1024]{1,0:T(8,128)(2,1)S(1)}, u32[]{:S(2)}, u32[]{:S(2)}) %collective-permute-start.17) | collective-permute-done | bytes 98336 | tf_op jit(solution)/shard_map/ppermute | solution.py:16
  53.6 0.1 collective-permute-done.16.refs_1_
  53.7 0.6 %collective-permute-start.19 = (f32[1,128]{1,0:T(1,128)S(1)}, f32[1,128]{1,0:T(1,128)S(1)}, u32[]{:S(2)}, u32[]{:S(2)}) collective-permute-start(f32[1,128]{1,0:T(1,128)S(1)} %bitcast.34), channel_id=1, source_target_pairs={{0,1},{1,0},{2,3},{3,2},{4,5},{5,4},{6,7},{7,6},{8,9},{9,8},{10,11... | collective-permute-start | bytes 1544 | tf_op jit(solution)/shard_map/ppermute | solution.py:16
  54.3 2.1 %finish.1 = (f32[1,1024,768]{2,1,0:T(8,128)}, bf16[4,48,1536]{2,1,0:T(8,128)(2,1)}) custom-call(bf16[48,1024]{1,0:T(8,128)(2,1)S(1)} %get-tuple-element.75.refs_0_, bf16[48,1024]{1,0:T(8,128)(2,1)S(1)} %collective-permute-done.16.refs_1_, bf16[48,1024]{1,0:T(8,128)(2,1)S(1)} %collective-permute-done.17.refs_2_, ...), custom_call_target="tpu_custom_call", output_to_operand_aliasing={{1}: (8, {})} | custom-call | flops 10000000000 | bytes 1024 | tf_op jit(solution)/shard_map/finish/pallas_call | solution.py:22
  56.4 0.0 collective-permute-done.14.same
  56.5 0.0 collective-permute-done.15.other
  56.5 0.0 collective-permute-done.19.sib
  56.5 0.7 %token_.1 = f32[1,128]{1,0:T(1,128)} custom-call(f32[1,24]{1,0:T(1,128)S(1)} %collective-permute-done.14.same, f32[1,24]{1,0:T(1,128)S(1)} %collective-permute-done.15.other, s32[1,128]{1,0:T(1,128)S(1)} %get-tuple-element.88.last_slots, f32[1,128]{1,0:T(1,128)S(1)} %bitcast.29, f32[1,128]{1,0:T(1,128)S(1)} %collective-permute-done.19.sib, f32[1,128]{1,0:T(1,128)S(1)} %bitcast.28), custom_call_target="tpu_custom_call" | custom-call | flops 1024 | bytes 1024 | tf_op jit(solution)/shard_map/token/pallas_call | solution.py:22
  (4 shorter events, 0.0 us)
Async XLA Ops:
  0.6 3.0 %collective-permute-start = (bf16[128,4096]{1,0:T(8,128)(2,1)}, bf16[128,4096]{1,0:T(8,128)(2,1)S(1)}, u32[]{:S(2)}, u32[]{:S(2)}) collective-permute-start(bf16[128,4096]{1,0:T(8,128)(2,1)} %rows.1), channel_id=1, source_target_pairs={{0,1},{1,0},{2,3},{3,2},{4,5},{5,4},{6,7},{7,6},{8,9},{9,8},{10,11... | collective-permute-start | bytes 3145736 | tf_op jit(solution)/shard_map/ppermute | solution.py:16
  1.1 2.5 %collective-permute-start.1 = (s32[1,128]{1,0:T(1,128)}, s32[1,128]{1,0:T(1,128)S(1)}, u32[]{:S(2)}, u32[]{:S(2)}) collective-permute-start(s32[1,128]{1,0:T(1,128)} %bitcast.30), channel_id=1, source_target_pairs={{0,1},{1,0},{2,3},{3,2},{4,5},{5,4},{6,7},{7,6},{8,9},{9,8},{10,11... | collective-permute-start | bytes 1544 | tf_op jit(solution)/shard_map/ppermute | solution.py:16
  1.2 31.7 %slice-start = ((s8[6291456]{0:T(1024)(128)(4,1)}), s8[4194304]{0:T(1024)(128)(4,1)S(1)}, s32[]{:S(2)}) async-start(s8[6291456]{0:T(1024)(128)(4,1)} %bitcast.20), calls=%async_computation | async-start | bytes 8388608
  1.2 2.4 %copy-start.1 = (f32[128,1]{0,1:T(1,128)S(1)}, f32[128,1]{0,1:T(1,128)}, u32[]{:S(2)}) copy-start(f32[128,1]{0,1:T(1,128)} %param.7) | copy-start | bytes 1540
  1.2 2.4 %copy-start.2 = (s32[128,1]{0,1:T(1,128)S(1)}, s32[128,1]{0,1:T(1,128)}, u32[]{:S(2)}) copy-start(s32[128,1]{0,1:T(1,128)} %param.6) | copy-start | bytes 1540
  1.2 8.6 %copy-start = (bf16[1,1,192,1536]{3,2,1,0:T(8,128)(2,1)S(1)}, bf16[1,1,192,1536]{3,2,1,0:T(8,128)(2,1)}, u32[]{:S(2)}) copy-start(bf16[1,1,192,1536]{3,2,1,0:T(8,128)(2,1)} %param.9) | copy-start | bytes 1769476
  1.2 31.7 %slice-start.1 = ((s8[6291456]{0:T(1024)(128)(4,1)}), s8[2097152]{0:T(1024)(128)(4,1)S(1)}, s32[]{:S(2)}) async-start(s8[6291456]{0:T(1024)(128)(4,1)} %bitcast.20), calls=%async_computation.1 | async-start | bytes 4194304
  1.2 2.4 %collective-permute-start.2 = (f32[1,128]{1,0:T(1,128)}, f32[1,128]{1,0:T(1,128)S(1)}, u32[]{:S(2)}, u32[]{:S(2)}) collective-permute-start(f32[1,128]{1,0:T(1,128)} %bitcast.26), channel_id=1, source_target_pairs={{0,1},{1,0},{2,3},{3,2},{4,5},{5,4},{6,7},{7,6},{8,9},{9,8},{10,11... | collective-permute-start | bytes 1544 | tf_op jit(solution)/shard_map/ppermute | solution.py:16
  1.7 1.5 %copy-start.3 = (bf16[128,4096]{1,0:T(8,128)(2,1)S(1)}, bf16[128,4096]{1,0:T(8,128)(2,1)}, u32[]{:S(2)}) copy-start(bf16[128,4096]{1,0:T(8,128)(2,1)} %rows.1) | copy-start | bytes 3145732
  4.4 21.9 %collective-permute-start.3 = (bf16[4,48,1024]{2,1,0:T(8,128)(2,1)S(1)}, bf16[4,48,1024]{2,1,0:T(8,128)(2,1)S(1)}, u32[]{:S(2)}, u32[]{:S(2)}) collective-permute-start(bf16[4,48,1024]{2,1,0:T(8,128)(2,1)S(1)} %get-tuple-element.48), channel_id=1, source_target_pairs={{0,2},{1,3},{2,0},{3,1},{4,6},{5,7},{6,4},{7,5},{8,10},{9,11},{10,... | collective-permute-start | bytes 1179656 | tf_op jit(solution)/shard_map/ppermute | solution.py:16
  7.4 20.1 %collective-permute-start.4 = (bf16[4,48,1024]{2,1,0:T(8,128)(2,1)S(1)}, bf16[4,48,1024]{2,1,0:T(8,128)(2,1)S(1)}, u32[]{:S(2)}, u32[]{:S(2)}) collective-permute-start(bf16[4,48,1024]{2,1,0:T(8,128)(2,1)S(1)} %get-tuple-element.49), channel_id=1, source_target_pairs={{0,6},{1,7},{2,4},{3,5},{4,2},{5,3},{6,0},{7,1},{8,14},{9,15},{10,... | collective-permute-start | bytes 1179656 | tf_op jit(solution)/shard_map/ppermute | solution.py:16
  10.1 10.0 %collective-permute-start.7 = (bf16[4,48,768]{2,1,0:T(8,128)(2,1)S(1)}, bf16[4,48,768]{2,1,0:T(8,128)(2,1)S(1)}, u32[]{:S(2)}, u32[]{:S(2)}) collective-permute-start(bf16[4,48,768]{2,1,0:T(8,128)(2,1)S(1)} %hidden.1.refs_3_), channel_id=1, source_target_pairs={{0,8},{8,0},{16,24},{24,16},{1,9},{9,1},{17,25},{25,17},{2,10},{10... | collective-permute-start | bytes 884744 | tf_op jit(solution)/shard_map/ppermute | solution.py:16
  11.6 14.5 %collective-permute-start.6 = (bf16[4,48,768]{2,1,0:T(8,128)(2,1)S(1)}, bf16[4,48,768]{2,1,0:T(8,128)(2,1)S(1)}, u32[]{:S(2)}, u32[]{:S(2)}) collective-permute-start(bf16[4,48,768]{2,1,0:T(8,128)(2,1)S(1)} %hidden.1.refs_3_), channel_id=1, source_target_pairs={{0,16},{8,24},{16,0},{24,8},{1,17},{9,25},{17,1},{25,9},{2,18},{10... | collective-permute-start | bytes 884744 | tf_op jit(solution)/shard_map/ppermute | solution.py:16
  13.1 13.0 %collective-permute-start.5 = (bf16[4,48,768]{2,1,0:T(8,128)(2,1)S(1)}, bf16[4,48,768]{2,1,0:T(8,128)(2,1)S(1)}, u32[]{:S(2)}, u32[]{:S(2)}) collective-permute-start(bf16[4,48,768]{2,1,0:T(8,128)(2,1)S(1)} %hidden.1.refs_3_), channel_id=1, source_target_pairs={{0,24},{8,16},{16,8},{24,0},{1,25},{9,17},{17,9},{25,1},{2,26},{10... | collective-permute-start | bytes 884744 | tf_op jit(solution)/shard_map/ppermute | solution.py:16
  27.5 18.3 %collective-permute-start.8 = (bf16[4,48,1024]{2,1,0:T(8,128)(2,1)S(1)}, bf16[4,48,1024]{2,1,0:T(8,128)(2,1)S(1)}, u32[]{:S(2)}, u32[]{:S(2)}) collective-permute-start(bf16[4,48,1024]{2,1,0:T(8,128)(2,1)S(1)} %get-tuple-element.54), channel_id=1, source_target_pairs={{0,4},{1,5},{2,6},{3,7},{4,0},{5,1},{6,2},{7,3},{8,12},{9,13},{10,... | collective-permute-start | bytes 1179656 | tf_op jit(solution)/shard_map/ppermute | solution.py:16
  29.4 10.0 %collective-permute-start.11 = (bf16[144,1024]{1,0:T(8,128)(2,1)S(1)}, bf16[144,1024]{1,0:T(8,128)(2,1)S(1)}, u32[]{:S(2)}, u32[]{:S(2)}) collective-permute-start(bf16[144,1024]{1,0:T(8,128)(2,1)S(1)} %get-tuple-element.63), channel_id=1, source_target_pairs={{0,8},{8,0},{16,24},{24,16},{1,9},{9,1},{17,25},{25,17},{2,10},{10... | collective-permute-start | bytes 884744 | tf_op jit(solution)/shard_map/ppermute | solution.py:16
  30.9 13.7 %collective-permute-start.9 = (bf16[144,1024]{1,0:T(8,128)(2,1)S(1)}, bf16[144,1024]{1,0:T(8,128)(2,1)S(1)}, u32[]{:S(2)}, u32[]{:S(2)}) collective-permute-start(bf16[144,1024]{1,0:T(8,128)(2,1)S(1)} %get-tuple-element.59), channel_id=1, source_target_pairs={{0,16},{8,24},{16,0},{24,8},{1,17},{9,25},{17,1},{25,9},{2,18},{10... | collective-permute-start | bytes 884744 | tf_op jit(solution)/shard_map/ppermute | solution.py:16
  32.4 12.1 %collective-permute-start.10 = (bf16[144,1024]{1,0:T(8,128)(2,1)S(1)}, bf16[144,1024]{1,0:T(8,128)(2,1)S(1)}, u32[]{:S(2)}, u32[]{:S(2)}) collective-permute-start(bf16[144,1024]{1,0:T(8,128)(2,1)S(1)} %get-tuple-element.60), channel_id=1, source_target_pairs={{0,24},{8,16},{16,8},{24,0},{1,25},{9,17},{17,9},{25,1},{2,26},{10... | collective-permute-start | bytes 884744 | tf_op jit(solution)/shard_map/ppermute | solution.py:16
  35.7 9.9 %collective-permute-start.12 = (f32[1,48]{1,0:T(1,128)S(1)}, f32[1,48]{1,0:T(1,128)S(1)}, u32[]{:S(2)}, u32[]{:S(2)}) collective-permute-start(f32[1,48]{1,0:T(1,128)S(1)} %get-tuple-element.65), channel_id=1, source_target_pairs={{0,2},{1,3},{2,0},{3,1},{4,6},{5,7},{6,4},{7,5},{8,10},{9,11},{10,... | collective-permute-start | bytes 584 | tf_op jit(solution)/shard_map/ppermute | solution.py:16
  39.4 10.0 %collective-permute-start.13 = (f32[1,48]{1,0:T(1,128)S(1)}, f32[1,48]{1,0:T(1,128)S(1)}, u32[]{:S(2)}, u32[]{:S(2)}) collective-permute-start(f32[1,48]{1,0:T(1,128)S(1)} %get-tuple-element.70), channel_id=1, source_target_pairs={{0,6},{1,7},{2,4},{3,5},{4,2},{5,3},{6,0},{7,1},{8,14},{9,15},{10,... | collective-permute-start | bytes 584 | tf_op jit(solution)/shard_map/ppermute | solution.py:16
  45.9 6.8 %collective-permute-start.18 = (bf16[48,1024]{1,0:T(8,128)(2,1)S(1)}, bf16[48,1024]{1,0:T(8,128)(2,1)S(1)}, u32[]{:S(2)}, u32[]{:S(2)}) collective-permute-start(bf16[48,1024]{1,0:T(8,128)(2,1)S(1)} %get-tuple-element.93), channel_id=1, source_target_pairs={{0,24},{8,16},{16,8},{24,0},{1,25},{9,17},{17,9},{25,1},{2,26},{10... | collective-permute-start | bytes 294920 | tf_op jit(solution)/shard_map/ppermute | solution.py:16
  48.4 5.3 %collective-permute-start.17 = (bf16[48,1024]{1,0:T(8,128)(2,1)S(1)}, bf16[48,1024]{1,0:T(8,128)(2,1)S(1)}, u32[]{:S(2)}, u32[]{:S(2)}) collective-permute-start(bf16[48,1024]{1,0:T(8,128)(2,1)S(1)} %get-tuple-element.94), channel_id=1, source_target_pairs={{0,16},{8,24},{16,0},{24,8},{1,17},{9,25},{17,1},{25,9},{2,18},{10... | collective-permute-start | bytes 294920 | tf_op jit(solution)/shard_map/ppermute | solution.py:16
  48.9 4.8 %collective-permute-start.16 = (bf16[48,1024]{1,0:T(8,128)(2,1)S(1)}, bf16[48,1024]{1,0:T(8,128)(2,1)S(1)}, u32[]{:S(2)}, u32[]{:S(2)}) collective-permute-start(bf16[48,1024]{1,0:T(8,128)(2,1)S(1)} %get-tuple-element.95), channel_id=1, source_target_pairs={{0,8},{8,0},{16,24},{24,16},{1,9},{9,1},{17,25},{25,17},{2,10},{10... | collective-permute-start | bytes 294920 | tf_op jit(solution)/shard_map/ppermute | solution.py:16
  51.2 5.3 %collective-permute-start.14 = (f32[1,24]{1,0:T(1,128)S(1)}, f32[1,24]{1,0:T(1,128)S(1)}, u32[]{:S(2)}, u32[]{:S(2)}) collective-permute-start(f32[1,24]{1,0:T(1,128)S(1)} %get-tuple-element.72), channel_id=1, source_target_pairs={{0,4},{1,5},{2,6},{3,7},{4,0},{5,1},{6,2},{7,3},{8,12},{9,13},{10,... | collective-permute-start | bytes 296 | tf_op jit(solution)/shard_map/ppermute | solution.py:16
  52.5 4.0 %collective-permute-start.15 = (f32[1,24]{1,0:T(1,128)S(1)}, f32[1,24]{1,0:T(1,128)S(1)}, u32[]{:S(2)}, u32[]{:S(2)}) collective-permute-start(f32[1,24]{1,0:T(1,128)S(1)} %get-tuple-element.73), channel_id=1, source_target_pairs={{0,5},{1,4},{2,7},{3,6},{4,1},{5,0},{6,3},{7,2},{8,13},{9,12},{10,... | collective-permute-start | bytes 296 | tf_op jit(solution)/shard_map/ppermute | solution.py:16
  53.7 2.8 %collective-permute-start.19 = (f32[1,128]{1,0:T(1,128)S(1)}, f32[1,128]{1,0:T(1,128)S(1)}, u32[]{:S(2)}, u32[]{:S(2)}) collective-permute-start(f32[1,128]{1,0:T(1,128)S(1)} %bitcast.34), channel_id=1, source_target_pairs={{0,1},{1,0},{2,3},{3,2},{4,5},{5,4},{6,7},{7,6},{8,9},{9,8},{10,11... | collective-permute-start | bytes 1544 | tf_op jit(solution)/shard_map/ppermute | solution.py:16
